TPU v7x, 128 devices: a whole 4x4x4 slice. The times are simulated.
128 devices in a mesh: replica: 4 (over z), fsdp: 32 (over y, x, core).
Axes of the slice: x: 4, y: 4, z: 4, core: 2. Of those that a mesh axis runs over, the one named last changes fastest.
Arguments:
- anchor: float32 [1024, 8192], P('fsdp'), may hold values from -6 to 6
- momentum: float32 [1024, 8192], P('fsdp'), may hold values from -3 to 3
- local_weights: bfloat16 [4, 1024, 8192], P('replica', 'fsdp'), may hold values from -64 to 64
- tokens: bfloat16 [4, 32768, 8192], P('replica', 'fsdp'), may hold values from -0.06591797 to 0.06591797
Outputs:
- new_anchor: float32 [1024, 8192], P('fsdp')
- new_momentum: float32 [1024, 8192], P('fsdp')
- merged_weights: bfloat16 [4, 1024, 8192], P('replica', 'fsdp')
- gate_out: bfloat16 [4, 32768, 1024], P('replica', 'fsdp')
All inputs are finite; a program needn't handle non-finite values.
Results may differ from a plain program's by a relative error of at most 0.015.
Values may be sent and summed in bfloat16 or wider, within the bound.
No kernel may reach another device: no remote copies, remote signals or barrier semaphores. Data moves between devices by JAX's collectives and lax.ppermute only.
A program may use at most 128 MiB of HBM per device.

v0:
```python
import jax
import jax.numpy as jnp
from jax import lax
from jax.sharding import PartitionSpec as P


def on_device(anchor, momentum, local_weights, tokens):
    unit_rows, width = anchor.shape
    num_blocks = width // 128
    local_float = local_weights.astype(jnp.float32)
    delta = anchor[None] - local_float
    blocks = delta.reshape(1, unit_rows, num_blocks, 128)
    block_scale = (2.0 * jnp.sqrt(jnp.mean(blocks * blocks, axis=3) + 1e-06)).astype(jnp.bfloat16)
    wide_scale = block_scale.astype(jnp.float32)[..., None]
    codes = jnp.clip(blocks / wide_scale, -1.0, 1.0).astype(jnp.bfloat16)
    replicas = lax.axis_size("replica")
    all_codes, all_scales = (
        lax.all_gather(codes, "replica", axis=0, tiled=True),
        lax.all_gather(block_scale, "replica", axis=0, tiled=True),
    )
    decoded = all_codes.astype(jnp.float32) * all_scales.astype(jnp.float32)[..., None]
    outer_grad = (jnp.sum(decoded, axis=0) / replicas).reshape(unit_rows, width)
    new_momentum = 0.9 * momentum + outer_grad
    new_anchor = anchor - 0.7 * (outer_grad + 0.9 * new_momentum)
    merged = (0.5 * local_float + 0.5 * new_anchor[None]).astype(jnp.bfloat16)
    batch = tokens[0]
    gate_out = lax.dot_general(
        batch,
        lax.all_gather(merged[0], "fsdp", axis=0, tiled=True),
        (((1,), (1,)), ((), ())),
        preferred_element_type=jnp.float32,
    )
    return (new_anchor, new_momentum, merged, gate_out.astype(jnp.bfloat16)[None])


def solution(mesh):
    return jax.shard_map(
        on_device,
        mesh=mesh,
        in_specs=(
            P("fsdp", None),
            P("fsdp", None),
            P("replica", "fsdp", None),
            P("replica", "fsdp", None),
        ),
        out_specs=(
            P("fsdp", None),
            P("fsdp", None),
            P("replica", "fsdp", None),
            P("replica", "fsdp", None),
        ),
        check_vma=False,
    )
```

profile of v0, /device:TPU:1, one launch (start us, length us, event | category | flops | bytes accessed | tf_op | source)
XLA Modules:
  0.0 157.0 jit_solution(12535782091347550151)
XLA Ops:
  7.2 0.0 all-gather.5.cloned.1.call-start
  7.2 1.5 fusion.7
  8.7 0.2 copy.10
  8.9 0.0 copy-start
  8.9 0.0 copy-start.1
  8.9 0.0 copy-start.2
  8.9 0.3 fusion.12
  9.3 1.1 fusion.14
  10.4 0.0 all-gather.5.cloned.1.call-update
  10.5 0.0 all-gather.7.cloned.1.call-start
  10.5 11.3 %all-gather = bf16[128,64]{1,0:T(8,128)(2,1)S(1)} all-gather(bf16[32,64]{1,0:T(8,128)(2,1)S(1)} %get-tuple-element.16), channel_id=2, replica_groups=mesh['replica'=4,'fsdp'=32] {'replica'}, dimensions={0}, use_global_device_ids=true | all-gather | bytes 20480 | tf_op jit(solution)/shard_map/all_gather | solution.py:19
  21.8 23.0 %all-gather.5.cloned.1.call-done = bf16[4,32,64,128]{3,2,1,0:T(8,128)(2,1)} async-done(((bf16[1,32,64,128]{3,2,1,0:T(8,128)(2,1)}), bf16[4,32,64,128]{3,2,1,0:T(8,128)(2,1)}) %all-gather.5.cloned.1.call-update) | async-done | bytes 2097168 | tf_op jit(solution)/shard_map/all_gather | solution.py:18
  44.9 2.6 %multiply_reduce_fusion = f32[32,64,128]{2,1,0:T(8,128)S(1)} fusion(bf16[4,32,64,128]{3,2,1,0:T(8,128)(2,1)} %all-gather.5.cloned.1.call-done, f32[4,32,64]{2,1,0:T(8,128)S(1)} %bitcast_convert_fusion), kind=kLoop, calls=%fused_computation.3 | loop fusion | flops 2883584 | bytes 3178496 | tf_op jit(solution)/shard_map/reduce_sum | solution.py:22
  47.4 0.1 broadcast_multiply_fusion
  47.5 0.0 copy-done
  47.6 0.0 copy-done.1
  47.6 0.0 copy-done.2
  47.6 2.4 %fusion.9 = (bf16[1,32,8192]{2,1,0:T(8,128)(2,1)}, f32[32,8192]{1,0:T(8,128)}, f32[32,8192]{1,0:T(8,128)}) fusion(bf16[1,32,8192]{2,1,0:T(8,128)(2,1)S(1)} %copy-done.1, f32[32,8192]{1,0:T(8,128)S(1)} %copy-done, f32[4,8,64,128]{3,2,1,0:T(8,128)S(1)} %bitcast.48, f32[32,8192]{1,0:T(8,128)S(1)} %copy-done.2), kind=kLoop, calls=%fused_computation.9 | loop fusion | flops 2621440 | bytes 6291456 | tf_op jit(solution)/shard_map/convert_element_type | solution.py:25
  50.0 0.0 all-gather.7.cloned.1.call-update
  50.0 72.8 %all-gather.7.cloned.1.call-done = bf16[1,1024,8192]{2,1,0:T(8,128)(2,1)} async-done(((bf16[1,32,8192]{2,1,0:T(8,128)(2,1)}), bf16[1,1024,8192]{2,1,0:T(8,128)(2,1)}) %all-gather.7.cloned.1.call-update) | async-done | bytes 16777232 | tf_op jit(solution)/shard_map/all_gather | solution.py:29
  122.8 23.4 %convert_bitcast_fusion = bf16[1,1024,1024]{1,2,0:T(8,128)(2,1)} fusion(bf16[1,1024,8192]{2,1,0:T(8,128)(2,1)} %param.7, bf16[1,1024,8192]{2,1,0:T(8,128)(2,1)} %all-gather.7.cloned.1.call-done), kind=kOutput, calls=%fused_computation.4 | convolution fusion | flops 17180917760 | bytes 35651584 | tf_op jit(solution)/shard_map/dot_general | solution.py:27
  146.2 3.9 %copy.9 = bf16[1,1024,1024]{2,1,0:T(8,128)(2,1)} copy(bf16[1,1024,1024]{1,2,0:T(8,128)(2,1)} %convert_bitcast_fusion) | data formatting | bytes 4194304
  (2 shorter events, 0.0 us)
Async XLA Ops:
  7.2 37.7 %all-gather.5.cloned.1.call-start = ((), (), s32[]{:S(2)}) async-start(), calls=%async_computation | async-start | bytes 2621440 | tf_op jit(solution)/shard_map/all_gather | solution.py:18
  8.9 38.7 %copy-start = (f32[32,8192]{1,0:T(8,128)S(1)}, f32[32,8192]{1,0:T(8,128)}, u32[]{:S(2)}) copy-start(f32[32,8192]{1,0:T(8,128)} %param.4) | copy-start | bytes 3145732
  8.9 38.7 %copy-start.1 = (bf16[1,32,8192]{2,1,0:T(8,128)(2,1)S(1)}, bf16[1,32,8192]{2,1,0:T(8,128)(2,1)}, u32[]{:S(2)}) copy-start(bf16[1,32,8192]{2,1,0:T(8,128)(2,1)} %param.6) | copy-start | bytes 1572868
  8.9 38.7 %copy-start.2 = (f32[32,8192]{1,0:T(8,128)S(1)}, f32[32,8192]{1,0:T(8,128)}, u32[]{:S(2)}) copy-start(f32[32,8192]{1,0:T(8,128)} %param.5) | copy-start | bytes 3145732
  10.5 112.4 %all-gather.7.cloned.1.call-start = ((), (), s32[]{:S(2)}) async-start(), calls=%async_computation.1 | async-start | bytes 17301504 | tf_op jit(solution)/shard_map/all_gather | solution.py:29
Sparse Core Ops, SparseCore 0:
  10.6 34.2 all-gather.4
  50.2 72.6 all-gather.6
where the time goes:
time: 157 us
  waiting for transfers between devices  95.9 us (61%)
  matrix products  23.4 us (15%)
  between operations  14.1 us (9%)
  blocking collectives  11.3 us (7%)
  other arithmetic  8.07 us (5%)
  local copies, waits for them, and re-layouts  4.14 us (3%)
    all_gather x1, waiting for transfers between devices, on_device(): lax.all_gather(merged[0], 'fsdp', axis=0, tiled=True)  72.8 us
    dot_general x1, matrix products, on_device(): lax.dot_general(batch, lax.all_gather(merged[0], 'fsdp', axis=0, tiled=Tr...  23.4 us
    all_gather x1, waiting for transfers between devices, on_device(): lax.all_gather(codes, 'replica', axis=0, tiled=True)  23 us
    all_gather x1, blocking collectives, on_device(): lax.all_gather(block_scale, 'replica', axis=0, tiled=True)  11.3 us
    unnamed x8, local copies, waits for them, and re-layouts  4.14 us
  transfers between devices with their start and end apart: 2, of which 2 were waited for; matrix products, arithmetic and copies ran while one was open for 0% of the time, Pallas kernels for 0%

commit v1 on v0

v1 whole, which is shorter than its diff:
```python
import functools

import jax
import jax.numpy as jnp
from jax import lax
from jax.experimental import pallas as pl
from jax.experimental.pallas import tpu as pltpu
from jax.sharding import PartitionSpec as P

SIDE = 4
BLOCK = 128
CHUNKS = 2
MERGE_COLS = 1024
MIB = 1024 * 1024


def fsdp_index(y, x, core):
    return ((y % SIDE) * SIDE + x % SIDE) * 2 + core


def ring_pairs(step, second):
    pairs = []
    for y in range(SIDE):
        for x in range(SIDE):
            for core in range(2):
                along_x = (core == 0) != second
                target = (y, x + step) if along_x else (y + step, x)
                pairs.append((fsdp_index(y, x, core), fsdp_index(*target, core)))
    return pairs


def to_mate(value):
    return lax.ppermute(value, "core", [(0, 1), (1, 0)])


def to_ring(value, step, second):
    return lax.ppermute(value, ("chip", "core"), ring_pairs(step, second))


def to_replica(value, step):
    return lax.ppermute(value, "replica", [(i, (i + step) % SIDE) for i in range(SIDE)])


def merge_body(replica_ref, anchor, momentum, locals_ref, outer_grad, merged):
    rows, width = anchor.shape
    blocks = width // BLOCK

    def stacked(value):
        return jnp.concatenate([value[:, i * BLOCK : (i + 1) * BLOCK] for i in range(blocks)], axis=0)

    local = locals_ref[...].astype(jnp.float32)
    local = jnp.concatenate([stacked(local[r * rows : (r + 1) * rows]) for r in range(SIDE)], axis=0)
    base = stacked(anchor[...])
    delta = jnp.concatenate([base] * SIDE, axis=0) - local
    square = delta * delta
    high = square.astype(jnp.bfloat16)
    low = (square - high.astype(jnp.float32)).astype(jnp.bfloat16)
    spread = jnp.full((BLOCK, BLOCK), 4.0 / BLOCK, jnp.bfloat16)
    mean = jnp.dot(high, spread, preferred_element_type=jnp.float32)
    mean = mean + jnp.dot(low, spread, preferred_element_type=jnp.float32) + 4e-06
    scale = (mean * lax.rsqrt(mean)).astype(jnp.bfloat16).astype(jnp.float32)
    codes = jnp.clip(delta * pl.reciprocal(scale), -1.0, 1.0).astype(jnp.bfloat16)
    decoded = codes.astype(jnp.float32) * scale
    size = blocks * rows
    parts = [decoded[r * size : (r + 1) * size] for r in range(SIDE)]
    grad = ((parts[0] + parts[2]) + (parts[1] + parts[3])) * 0.25
    speed = 0.9 * stacked(momentum[...]) + grad
    anchored = base - 0.7 * (grad + 0.9 * speed)
    blend = 0.5 * local + 0.5 * jnp.concatenate([anchored] * SIDE, axis=0)
    for i in range(blocks):
        cols = slice(i * BLOCK, (i + 1) * BLOCK)
        outer_grad[:, cols] = grad[i * rows : (i + 1) * rows]
        column = [blend[r * size + i * rows : r * size + (i + 1) * rows] for r in range(SIDE)]
        merged[0, :, cols] = jnp.concatenate(column, axis=0).astype(merged.dtype)


def merge(replica, anchor, momentum, gathered):
    rows, width = anchor.shape
    share = rows // SIDE
    steps = width // MERGE_COLS
    per_half = steps // 2
    own = pl.BlockSpec((share, MERGE_COLS), lambda i, replica_ref: (replica_ref[0], i))
    return pl.pallas_call(
        merge_body,
        grid_spec=pltpu.PrefetchScalarGridSpec(
            num_scalar_prefetch=1,
            grid=(steps,),
            in_specs=[own, own, pl.BlockSpec((rows, MERGE_COLS), lambda i, replica_ref: (0, i))],
            out_specs=[
                pl.BlockSpec((share, MERGE_COLS), lambda i, replica_ref: (0, i)),
                pl.BlockSpec((1, rows, MERGE_COLS), lambda i, replica_ref: (i // per_half, 0, i % per_half)),
            ],
        ),
        out_shape=[
            jax.ShapeDtypeStruct((share, width), jnp.float32),
            jax.ShapeDtypeStruct((2, rows, width // 2), jnp.bfloat16),
        ],
        compiler_params=pltpu.CompilerParams(vmem_limit_bytes=12 * MIB),
        name="merge",
    )(replica, anchor, momentum, gathered)


def update_body(anchor, momentum, local, outer_grad, new_anchor, new_momentum, merged):
    grad = outer_grad[...]
    speed = 0.9 * momentum[...] + grad
    anchored = anchor[...] - 0.7 * (grad + 0.9 * speed)
    new_momentum[...] = speed
    new_anchor[...] = anchored
    merged[...] = (0.5 * local[...].astype(jnp.float32) + 0.5 * anchored).astype(merged.dtype)


def update(anchor, momentum, local, outer_grad):
    rows, width = anchor.shape
    tile = pl.BlockSpec((rows, 2 * MERGE_COLS), lambda i: (0, i))
    wide = jax.ShapeDtypeStruct((rows, width), jnp.float32)
    return pl.pallas_call(
        update_body,
        grid=(width // (2 * MERGE_COLS),),
        in_specs=[tile] * 4,
        out_specs=[tile] * 3,
        out_shape=[wide, wide, jax.ShapeDtypeStruct((rows, width), jnp.bfloat16)],
        compiler_params=pltpu.CompilerParams(vmem_limit_bytes=12 * MIB),
        name="update",
    )(anchor, momentum, local, outer_grad)


def load_body(core_ref, tokens, half, sem):
    width = half.shape[1]
    start = pl.multiple_of(core_ref[0] * width, width)
    copy = pltpu.make_async_copy(tokens.at[:, pl.ds(start, width)], half, sem)
    copy.start()
    copy.wait()


def load_half(core, tokens):
    count, width = tokens.shape
    return pl.pallas_call(
        load_body,
        in_specs=[pl.BlockSpec(memory_space=pltpu.SMEM), pl.BlockSpec(memory_space=pltpu.HBM)],
        out_specs=pl.BlockSpec(memory_space=pltpu.VMEM),
        out_shape=jax.ShapeDtypeStruct((count, width // 2), tokens.dtype),
        scratch_shapes=[pltpu.SemaphoreType.DMA(())],
        compiler_params=pltpu.CompilerParams(vmem_limit_bytes=12 * MIB),
        name="load_half",
    )(core, tokens)


def partial_body(per_block, tokens, *refs):
    weights, out = refs[:-1], refs[-1]
    for block in range(out.shape[0]):
        start, total = 0, None
        for piece in weights[block * per_block : (block + 1) * per_block]:
            term = lax.dot_general(
                tokens[:, start : start + piece.shape[1]],
                piece[...],
                (((1,), (1,)), ((), ())),
                preferred_element_type=jnp.float32,
            )
            total = term if total is None else total + term
            start += piece.shape[1]
        out[block] = total.astype(out.dtype)


def partial_sums(tokens, weights):
    count, half = tokens.shape
    blocks, per_block = len(weights), len(weights[0])
    units = weights[0][0].shape[0]
    return pl.pallas_call(
        functools.partial(partial_body, per_block),
        in_specs=[pl.BlockSpec(memory_space=pltpu.VMEM)] * (1 + blocks * per_block),
        out_specs=pl.BlockSpec(memory_space=pltpu.VMEM),
        out_shape=jax.ShapeDtypeStruct((blocks, count, units), jnp.bfloat16),
        compiler_params=pltpu.CompilerParams(vmem_limit_bytes=20 * MIB),
        cost_estimate=pl.CostEstimate(
            flops=2 * count * units * blocks * half,
            bytes_accessed=2 * (count + units * blocks) * half,
            transcendentals=0,
        ),
        name="partial_sums",
    )(tokens, *[piece for block in weights for piece in block])


COMBINE_ROWS = 128


def combine_body(held, out):
    rows = pl.ds(pl.multiple_of(pl.program_id(0) * COMBINE_ROWS, COMBINE_ROWS), COMBINE_ROWS)
    low = lax.broadcasted_iota(jnp.int32, (COMBINE_ROWS, BLOCK), 1) < BLOCK // 2
    for tile in range(out.shape[1] // BLOCK):
        y, x = tile // 2, 2 * (tile % 2)
        cols = slice((y // 2) * BLOCK, (y // 2 + 1) * BLOCK)
        left = held[1, x, rows, cols].astype(jnp.float32)
        right = held[1, x + 1, rows, cols].astype(jnp.float32)
        if y % 2 == 0:
            right = pltpu.roll(right, BLOCK // 2, 1)
        else:
            left = pltpu.roll(left, BLOCK // 2, 1)
        natural = held[0, y, rows, slice((tile % 2) * BLOCK, (tile % 2 + 1) * BLOCK)].astype(jnp.float32)
        out[:, tile * BLOCK : (tile + 1) * BLOCK] = (natural + jnp.where(low, left, right)).astype(out.dtype)


def combine(held):
    _, _, count, units = held.shape
    return pl.pallas_call(
        combine_body,
        grid=(count // COMBINE_ROWS,),
        in_specs=[pl.BlockSpec(memory_space=pltpu.VMEM)],
        out_specs=pl.BlockSpec((COMBINE_ROWS, units * SIDE), lambda i: (i, 0)),
        out_shape=jax.ShapeDtypeStruct((count, units * SIDE), jnp.bfloat16),
        compiler_params=pltpu.CompilerParams(vmem_limit_bytes=12 * MIB),
        name="combine",
    )(held)


def after(value, *others):
    return lax.optimization_barrier((value, *others))[0]


def on_device(anchor, momentum, local_weights, tokens):
    rows, width = anchor.shape
    half = width // 2
    part = half // CHUNKS
    replica = lax.axis_index("replica")
    core = lax.axis_index("core")
    chip = lax.axis_index("chip")
    x = chip % SIDE
    y = chip // SIDE
    core_array = core.astype(jnp.int32).reshape(1)
    first_base = jnp.where(core == 0, x, y)
    second_base = jnp.where(core == 0, y, x)
    local = local_weights[0]
    batch = tokens[0]

    mate_batch = to_mate(batch)
    gathered = lax.all_to_all(local, "replica", 0, 0, tiled=True)
    outer_part, merged_parts = merge(replica.astype(jnp.int32).reshape(1), anchor, momentum, gathered)
    pair = lax.all_to_all(merged_parts.reshape(2 * rows, half), ("core", "replica"), 0, 0, tiled=True)

    blocks = []
    for c in range(CHUNKS):
        piece = pair[:, c * part : (c + 1) * part]
        block = jnp.zeros((SIDE, 2 * rows, part), jnp.bfloat16)
        pieces = [piece] + [to_ring(piece, step, False) for step in (1, 2, 3)]
        for step, piece in enumerate(pieces):
            block = lax.dynamic_update_slice(block, piece[None], ((first_base - step) % SIDE, 0, 0))
        block = block.reshape(SIDE * 2 * rows, part)
        before = to_ring(block, 1, True)
        following = to_ring(block, SIDE - 1, True)
        low = to_ring(before[:, : part // 2], 1, True)
        high = to_ring(following[:, part // 2 :], SIDE - 1, True)
        blocks.append((block, following, before, low, high))

    own_half = load_half(after(core_array, pair), batch)
    mate_half = load_half(core_array, mate_batch)
    first = [[b[0] for b in blocks]]
    middle = [[b[1] for b in blocks], [b[2] for b in blocks]]
    last = [[piece for b in blocks for piece in b[3:]]]
    held = jnp.zeros((2, SIDE, tokens.shape[1], rows * 2 * SIDE), jnp.bfloat16)
    for weights, steps in ((first, (0,)), (middle, (1, 3)), (last, (2,))):
        got = to_mate(partial_sums(mate_half, weights))
        own = partial_sums(own_half, weights)
        for i, step in enumerate(steps):
            held = lax.dynamic_update_slice(held, own[i][None, None], (core, (second_base + step) % SIDE, 0, 0))
            held = lax.dynamic_update_slice(held, got[i][None, None], (1 - core, (first_base + step) % SIDE, 0, 0))
    gate_out = combine(held)

    outer_part = after(outer_part, blocks[0][0])
    outer_grad = jnp.zeros((rows, width), jnp.float32)
    for step in range(SIDE):
        share = to_replica(outer_part, step) if step else outer_part
        outer_grad = lax.dynamic_update_slice(outer_grad, share, (((replica - step) % SIDE) * share.shape[0], 0))
    new_anchor, new_momentum, merged = update(anchor, momentum, local, outer_grad)
    return (new_anchor, new_momentum, merged[None], gate_out[None])


def solution(mesh):
    split = jax.sharding.Mesh(mesh.devices.reshape(SIDE, SIDE * SIDE, 2), ("replica", "chip", "core"))
    fsdp = ("chip", "core")
    return jax.shard_map(
        on_device,
        mesh=split,
        in_specs=(
            P(fsdp, None),
            P(fsdp, None),
            P("replica", fsdp, None),
            P("replica", fsdp, None),
        ),
        out_specs=(
            P(fsdp, None),
            P(fsdp, None),
            P("replica", fsdp, None),
            P("replica", fsdp, None),
        ),
        check_vma=False,
    )
```

time: 157 us -> 131 us (0.83)
  waiting for transfers between devices: 95.9 us -> 38.4 us
  starting transfers between devices: 0.08 us -> 41 us
  Pallas kernels: 0 us -> 30.4 us
  matrix products: 23.4 us -> 0 us
  between operations: 14.1 us -> 1.12 us
  blocking collectives: 11.3 us -> 0 us
  local copies, waits for them, and re-layouts: 4.14 us -> 13.2 us
  other arithmetic: 8.07 us -> 6.09 us
    all_gather x2 -> x0, waiting for transfers between devices: 95.8 us -> none  [the longest x1 72.8 us: on_device(): lax.all_gather(merged[0], 'fsdp', axis=0, tiled=True)]
    ppermute x0 -> x21, starting transfers between devices: none -> 31.4 us  [the longest x14 22 us: to_ring(): return lax.ppermute(value, ('chip', 'core'), ring_pairs(step, second))]
    pallas_call x0 -> x9, Pallas kernels: none -> 30.4 us  [the longest x4 15.1 us: partial_sums(): pl.pallas_call(functools.partial(partial_body, per_block), in_specs=[pl.B...]
    dot_general x1 -> x0, matrix products: 23.4 us -> none  [on_device(): lax.dot_general(batch, lax.all_gather(merged[0], 'fsdp', axis=0, tiled=Tr...]
    ppermute x0 -> x21, waiting for transfers between devices: none -> 19.7 us  [the longest x14 10.1 us: to_ring(): return lax.ppermute(value, ('chip', 'core'), ring_pairs(step, second))]
    all_to_all x0 -> x2, waiting for transfers between devices: none -> 18.7 us  [the longest x1 9.37 us: on_device(): lax.all_to_all(merged_parts.reshape(2 * rows, half), ('core', 'replica'),...]
    all_gather x1 -> x0, blocking collectives: 11.3 us -> none  [on_device(): lax.all_gather(block_scale, 'replica', axis=0, tiled=True)]
    all_to_all x0 -> x2, starting transfers between devices: none -> 9.66 us  [the longest x1 5.11 us: on_device(): gathered = lax.all_to_all(local, 'replica', 0, 0, tiled=True)]
  transfers between devices with their start and end apart: 2 -> 23, of which waited for: 2 -> 8; matrix products, arithmetic and copies ran while one was open for 0% -> 8% of each run, Pallas kernels for 0% -> 21%
where the time goes in v1:
time: 131 us; the launch traced here: 130 us
  starting transfers between devices  41 us (31%)
  waiting for transfers between devices  38.4 us (29%)
  Pallas kernels  30.4 us (23%)
  local copies, waits for them, and re-layouts  13.2 us (10%)
  other arithmetic  6.09 us (5%)
    ppermute x14, starting transfers between devices, to_ring(): return lax.ppermute(value, ('chip', 'core'), ring_pairs(step, second))  22 us
    pallas_call x4, Pallas kernels, partial_sums(): pl.pallas_call(functools.partial(partial_body, per_block), in_specs=[pl.B...  15.1 us
    ppermute x14, waiting for transfers between devices, to_ring(): return lax.ppermute(value, ('chip', 'core'), ring_pairs(step, second))  10.1 us
    ppermute x3, waiting for transfers between devices, to_replica(): lax.ppermute(value, 'replica', [(i, (i + step) % SIDE) for i in range(SID...  9.63 us
    all_to_all x1, waiting for transfers between devices, on_device(): lax.all_to_all(merged_parts.reshape(2 * rows, half), ('core', 'replica'),...  9.37 us
    all_to_all x1, waiting for transfers between devices, on_device(): gathered = lax.all_to_all(local, 'replica', 0, 0, tiled=True)  9.3 us
    unnamed x36, local copies, waits for them, and re-layouts  9.25 us
    ppermute x4, starting transfers between devices, to_mate(): return lax.ppermute(value, 'core', [(0, 1), (1, 0)])  7.63 us
  transfers between devices with their start and end apart: 23, of which 8 were waited for; matrix products, arithmetic and copies ran while one was open for 8% of the time, Pallas kernels for 21%

profile of v1, /device:TPU:1, one launch (start us, length us, event | category | flops | bytes accessed | tf_op | source)
XLA Modules:
  0.0 130.2 jit_solution(10925363590709267299)
XLA Ops:
  0.6 1.5 %collective-permute-start.9 = (bf16[1024,8192]{1,0:T(8,128)(2,1)}, bf16[1024,8192]{1,0:T(8,128)(2,1)}, u32[]{:S(2)}, u32[]{:S(2)}) collective-permute-start(bf16[1024,8192]{1,0:T(8,128)(2,1)} %bitcast.52), channel_id=1, source_target_pairs={{0,1},{1,0},{2,3},{3,2},{4,5},{5,4},{6,7},{7,6},{8,9},{9,8},{10,11... | collective-permute-start | bytes 50331656 | tf_op jit(solution)/shard_map/ppermute | solution.py:33
  2.1 5.1 %all-to-all-start = ((bf16[4,8,8192]{2,1,0:T(8,128)(2,1)}), bf16[4,8,8192]{2,1,0:T(8,128)(2,1)S(1)}, u32[]{:S(2)}, u32[]{:S(2)}) async-start(bf16[4,8,8192]{2,1,0:T(8,128)(2,1)} %bitcast.62), calls=%async_computation | async-start | bytes 1048576 | tf_op jit(solution)/shard_map/all_to_all | solution.py:235
  7.2 9.3 %all-to-all-done = bf16[4,8,8192]{2,1,0:T(8,128)(2,1)S(1)} async-done(((bf16[4,8,8192]{2,1,0:T(8,128)(2,1)}), bf16[4,8,8192]{2,1,0:T(8,128)(2,1)S(1)}, u32[]{:S(2)}, u32[]{:S(2)}) %all-to-all-start) | async-done | bytes 524320 | tf_op jit(solution)/shard_map/all_to_all | solution.py:235
  16.5 1.2 copy-done.1
  17.8 1.2 copy-done.3
  19.0 3.7 %merge.1 = (f32[8,8192]{1,0:T(8,128)S(1)}, bf16[2,32,4096]{2,1,0:T(8,128)(2,1)}) custom-call(s32[1]{0:T(128)} %bitcast.1.replica_ref, f32[32,8192]{1,0:T(8,128)S(1)} %copy-done.1, f32[32,8192]{1,0:T(8,128)S(1)} %copy-done.3, bf16[32,8192]{1,0:T(8,128)(2,1)S(1)} %bitcast.64), custom_call_target="tpu_custom_call" | custom-call | tf_op jit(solution)/shard_map/merge/pallas_call | solution.py:83
  22.7 4.6 %all-to-all-start.1 = ((bf16[8,8,4096]{2,1,0:T(8,128)(2,1)}), bf16[8,8,4096]{2,1,0:T(8,128)(2,1)S(1)}, u32[]{:S(2)}, u32[]{:S(2)}) async-start(bf16[8,8,4096]{2,1,0:T(8,128)(2,1)} %bitcast.4), calls=%async_computation.1 | async-start | bytes 1048576 | tf_op jit(solution)/shard_map/all_to_all | solution.py:237
  27.3 9.4 %all-to-all-done.1 = bf16[8,8,4096]{2,1,0:T(8,128)(2,1)S(1)} async-done(((bf16[8,8,4096]{2,1,0:T(8,128)(2,1)}), bf16[8,8,4096]{2,1,0:T(8,128)(2,1)S(1)}, u32[]{:S(2)}, u32[]{:S(2)}) %all-to-all-start.1) | async-done | bytes 524320 | tf_op jit(solution)/shard_map/all_to_all | solution.py:237
  36.7 1.4 %collective-permute-start.6 = (bf16[64,2048]{1,0:T(8,128)(2,1)S(1)}, bf16[64,2048]{1,0:T(8,128)(2,1)S(1)}, u32[]{:S(2)}, u32[]{:S(2)}) collective-permute-start(bf16[64,2048]{1,0:T(8,128)(2,1)S(1)} %get-tuple-element.18), channel_id=1, source_target_pairs={{0,2},{1,9},{2,4},{3,11},{4,6},{5,13},{6,0},{7,15},{8,10},{9,17},{... | collective-permute-start | bytes 786440 | tf_op jit(solution)/shard_map/ppermute | solution.py:37
  38.1 2.6 %collective-permute-start.7 = (bf16[64,2048]{1,0:T(8,128)(2,1)S(1)}, bf16[64,2048]{1,0:T(8,128)(2,1)S(1)}, u32[]{:S(2)}, u32[]{:S(2)}) collective-permute-start(bf16[64,2048]{1,0:T(8,128)(2,1)S(1)} %get-tuple-element.18), channel_id=1, source_target_pairs={{0,4},{1,17},{2,6},{3,19},{4,0},{5,21},{6,2},{7,23},{8,12},{9,25},... | collective-permute-start | bytes 786440 | tf_op jit(solution)/shard_map/ppermute | solution.py:37
  40.7 1.1 collective-permute-start.8
  41.7 0.4 collective-permute-start
  42.1 5.8 %copy-done = bf16[1,1024,8192]{2,1,0:T(8,128)(2,1)S(1)} copy-done((bf16[1,1024,8192]{2,1,0:T(8,128)(2,1)S(1)}, bf16[1,1024,8192]{2,1,0:T(8,128)(2,1)}, u32[]{:S(2)}) %copy-start) | copy-done | bytes 16777240
  47.9 2.1 %load_half.2.tokens = bf16[1024,4096]{1,0:T(8,128)(2,1)S(1)} custom-call(s32[1]{0:T(128)} %bitcast.12.core_ref, bf16[1024,8192]{1,0:T(8,128)(2,1)S(1)} %bitcast.53), custom_call_target="tpu_custom_call" | custom-call | tf_op jit(solution)/shard_map/load_half/pallas_call | solution.py:137
  50.3 0.9 collective-permute-start.1
  51.2 1.7 %collective-permute-start.2 = (bf16[64,2048]{1,0:T(8,128)(2,1)S(1)}, bf16[64,2048]{1,0:T(8,128)(2,1)S(1)}, u32[]{:S(2)}, u32[]{:S(2)}) collective-permute-start(bf16[64,2048]{1,0:T(8,128)(2,1)S(1)} %get-tuple-element.19), channel_id=1, source_target_pairs={{0,6},{1,25},{2,0},{3,27},{4,2},{5,29},{6,4},{7,31},{8,14},{9,1},{... | collective-permute-start | bytes 786440 | tf_op jit(solution)/shard_map/ppermute | solution.py:37
  53.0 1.3 collective-permute-start.14
  54.2 1.5 %collective-permute-start.12 = (bf16[256,2048]{1,0:T(8,128)(2,1)S(1)}, bf16[256,2048]{1,0:T(8,128)(2,1)S(1)}, u32[]{:S(2)}, u32[]{:S(2)}) collective-permute-start(bf16[256,2048]{1,0:T(8,128)(2,1)S(1)} %bitcast.59), channel_id=1, source_target_pairs={{0,24},{1,7},{2,26},{3,1},{4,28},{5,3},{6,30},{7,5},{8,0},{9,15},{... | collective-permute-start | bytes 3145736 | tf_op jit(solution)/shard_map/ppermute | solution.py:37
  55.7 1.7 %collective-permute-done.1 = bf16[64,2048]{1,0:T(8,128)(2,1)S(1)} collective-permute-done((bf16[64,2048]{1,0:T(8,128)(2,1)S(1)}, bf16[64,2048]{1,0:T(8,128)(2,1)S(1)}, u32[]{:S(2)}, u32[]{:S(2)}) %collective-permute-start.1) | collective-permute-done | bytes 262176 | tf_op jit(solution)/shard_map/ppermute | solution.py:37
  57.4 3.5 %collective-permute-done.2 = bf16[64,2048]{1,0:T(8,128)(2,1)S(1)} collective-permute-done((bf16[64,2048]{1,0:T(8,128)(2,1)S(1)}, bf16[64,2048]{1,0:T(8,128)(2,1)S(1)}, u32[]{:S(2)}, u32[]{:S(2)}) %collective-permute-start.2) | collective-permute-done | bytes 262176 | tf_op jit(solution)/shard_map/ppermute | solution.py:37
  61.0 0.8 collective-permute-start.3
  61.8 0.9 collective-permute-start.4
  62.8 0.3 broadcast_in_dim.42
  63.1 2.4 %partial_sums.11 = bf16[2,4,1024,256]{3,2,1,0:T(8,128)(2,1)S(1)} fusion(bf16[2,4,1024,256]{3,2,1,0:T(8,128)(2,1)S(1)} %broadcast_in_dim.42, s32[]{:T(128)S(6)} %select_n.168, s32[]{:T(128)S(6)} %select_n.171, bf16[1024,4096]{1,0:T(8,128)(2,1)S(1)} %load_half.2.tokens, bf16[256,2048]{1,0:T(8,128)(2,1)S(1)} %bitcast.54, bf16[256,2048]{1,0:T(8,128)(2,1)S(1)} %bitcast.60), kind=kCustom, calls=%fused_computation.11 | custom fusion | flops 2147483648 | bytes 11010056 | tf_op jit(solution)/shard_map/partial_sums/pallas_call | solution.py:168
  65.5 4.8 %collective-permute-done.3 = f32[8,8192]{1,0:T(8,128)S(1)} collective-permute-done((f32[8,8192]{1,0:T(8,128)S(1)}, f32[8,8192]{1,0:T(8,128)S(1)}, u32[]{:S(2)}, u32[]{:S(2)}) %collective-permute-start.3) | collective-permute-done | bytes 262176 | tf_op jit(solution)/shard_map/ppermute | solution.py:41
  70.3 3.1 %collective-permute-start.13 = (bf16[256,2048]{1,0:T(8,128)(2,1)S(1)}, bf16[256,2048]{1,0:T(8,128)(2,1)S(1)}, u32[]{:S(2)}, u32[]{:S(2)}) collective-permute-start(bf16[256,2048]{1,0:T(8,128)(2,1)S(1)} %bitcast.55), channel_id=1, source_target_pairs={{0,8},{1,3},{2,10},{3,5},{4,12},{5,7},{6,14},{7,1},{8,16},{9,11},{... | collective-permute-start | bytes 3145736 | tf_op jit(solution)/shard_map/ppermute | solution.py:37
  73.4 4.8 %collective-permute-done.5 = f32[8,8192]{1,0:T(8,128)S(1)} collective-permute-done((f32[8,8192]{1,0:T(8,128)S(1)}, f32[8,8192]{1,0:T(8,128)S(1)}, u32[]{:S(2)}, u32[]{:S(2)}) %collective-permute-start.5) | collective-permute-done | bytes 262176 | tf_op jit(solution)/shard_map/ppermute | solution.py:41
  78.2 2.2 %collective-permute-start.11 = (bf16[256,2048]{1,0:T(8,128)(2,1)S(1)}, bf16[256,2048]{1,0:T(8,128)(2,1)S(1)}, u32[]{:S(2)}, u32[]{:S(2)}) collective-permute-start(bf16[256,2048]{1,0:T(8,128)(2,1)S(1)} %bitcast.56), channel_id=1, source_target_pairs={{0,24},{1,7},{2,26},{3,1},{4,28},{5,3},{6,30},{7,5},{8,0},{9,15},{... | collective-permute-start | bytes 3145736 | tf_op jit(solution)/shard_map/ppermute | solution.py:37
  80.5 2.2 %update.1 = (f32[32,8192]{1,0:T(8,128)}, f32[32,8192]{1,0:T(8,128)}, bf16[32,8192]{1,0:T(8,128)(2,1)}) custom-call(f32[32,8192]{1,0:T(8,128)S(1)} %copy-done.2, f32[32,8192]{1,0:T(8,128)S(1)} %copy-done.4, bf16[32,8192]{1,0:T(8,128)(2,1)S(1)} %bitcast.63, f32[32,8192]{1,0:T(8,128)S(1)} %constant_dynamic-update-slice_fusion.outer_grad), custom_call_target="tpu_custom_call" | custom-call | tf_op jit(solution)/shard_map/update/pallas_call | solution.py:116
  82.9 1.0 slice.49
  83.9 2.5 %collective-permute-start.19 = (bf16[256,1024]{1,0:T(8,128)(2,1)}, bf16[256,1024]{1,0:T(8,128)(2,1)}, u32[]{:S(2)}, u32[]{:S(2)}) collective-permute-start(bf16[256,1024]{1,0:T(8,128)(2,1)} %slice.49), channel_id=1, source_target_pairs={{0,24},{1,7},{2,26},{3,1},{4,28},{5,3},{6,30},{7,5},{8,0},{9,15},{... | collective-permute-start | bytes 1572872 | tf_op jit(solution)/shard_map/ppermute | solution.py:37
  86.4 1.4 %collective-permute-done.13.refs_2_ = bf16[256,2048]{1,0:T(8,128)(2,1)S(1)} collective-permute-done((bf16[256,2048]{1,0:T(8,128)(2,1)S(1)}, bf16[256,2048]{1,0:T(8,128)(2,1)S(1)}, u32[]{:S(2)}, u32[]{:S(2)}) %collective-permute-start.13) | collective-permute-done | bytes 1048608 | tf_op jit(solution)/shard_map/ppermute | solution.py:37
  87.8 0.9 slice.46
  88.7 3.5 %collective-permute-done.11.refs_0_ = bf16[256,2048]{1,0:T(8,128)(2,1)S(1)} collective-permute-done((bf16[256,2048]{1,0:T(8,128)(2,1)S(1)}, bf16[256,2048]{1,0:T(8,128)(2,1)S(1)}, u32[]{:S(2)}, u32[]{:S(2)}) %collective-permute-start.11) | collective-permute-done | bytes 1048608 | tf_op jit(solution)/shard_map/ppermute | solution.py:37
  92.2 0.9 slice.47
  93.1 3.4 %collective-permute-start.17 = (bf16[256,1024]{1,0:T(8,128)(2,1)}, bf16[256,1024]{1,0:T(8,128)(2,1)}, u32[]{:S(2)}, u32[]{:S(2)}) collective-permute-start(bf16[256,1024]{1,0:T(8,128)(2,1)} %slice.47), channel_id=1, source_target_pairs={{0,24},{1,7},{2,26},{3,1},{4,28},{5,3},{6,30},{7,5},{8,0},{9,15},{... | collective-permute-start | bytes 1572872 | tf_op jit(solution)/shard_map/ppermute | solution.py:37
  96.6 3.5 %load_half.3.tokens = bf16[1024,4096]{1,0:T(8,128)(2,1)S(1)} custom-call(s32[1]{0:T(128)} %bitcast.12.core_ref, bf16[1024,8192]{1,0:T(8,128)(2,1)} %collective-permute-done.9.tokens), custom_call_target="tpu_custom_call" | custom-call | tf_op jit(solution)/shard_map/load_half/pallas_call | solution.py:137
  100.1 0.3 copy-done.10
  100.4 0.3 copy-done.13
  100.8 0.3 copy-done.16
  101.1 4.5 %partial_sums.8 = bf16[2,1024,256]{2,1,0:T(8,128)(2,1)S(1)} custom-call(bf16[1024,4096]{1,0:T(8,128)(2,1)S(1)} %load_half.3.tokens, bf16[256,2048]{1,0:T(8,128)(2,1)S(1)} %copy-done.16, bf16[256,2048]{1,0:T(8,128)(2,1)S(1)} %copy-done.10, bf16[256,2048]{1,0:T(8,128)(2,1)S(1)} %copy-done.13, bf16[256,2048]{1,0:T(8,128)(2,1)S(1)} %copy-done.7), custom_call_target="tpu_custom_call" | custom-call | flops 4294967296 | bytes 12582912 | tf_op jit(solution)/shard_map/partial_sums/pallas_call | solution.py:168
  105.6 5.5 %collective-permute-start.15 = (bf16[2,1024,256]{2,1,0:T(8,128)(2,1)S(1)}, bf16[2,1024,256]{2,1,0:T(8,128)(2,1)S(1)}, u32[]{:S(2)}, u32[]{:S(2)}) collective-permute-start(bf16[2,1024,256]{2,1,0:T(8,128)(2,1)S(1)} %partial_sums.8), channel_id=1, source_target_pairs={{0,1},{1,0},{2,3},{3,2},{4,5},{5,4},{6,7},{7,6},{8,9},{9,8},{10,11... | collective-permute-start | bytes 3145736 | tf_op jit(solution)/shard_map/ppermute | solution.py:33
  111.1 2.4 %partial_sums.6 = bf16[1,1024,256]{2,1,0:T(8,128)(2,1)S(1)} custom-call(bf16[1024,4096]{1,0:T(8,128)(2,1)S(1)} %load_half.3.tokens, bf16[256,2048]{1,0:T(8,128)(2,1)S(1)} %bitcast.57, bf16[256,2048]{1,0:T(8,128)(2,1)S(1)} %bitcast.61), custom_call_target="tpu_custom_call" | custom-call | flops 2147483648 | bytes 10485760 | tf_op jit(solution)/shard_map/partial_sums/pallas_call | solution.py:168
  113.6 4.5 %partial_sums.7 = bf16[2,1024,256]{2,1,0:T(8,128)(2,1)S(1)} custom-call(bf16[1024,4096]{1,0:T(8,128)(2,1)S(1)} %load_half.2.tokens, bf16[256,2048]{1,0:T(8,128)(2,1)S(1)} %copy-done.17, bf16[256,2048]{1,0:T(8,128)(2,1)S(1)} %copy-done.11, bf16[256,2048]{1,0:T(8,128)(2,1)S(1)} %copy-done.14, bf16[256,2048]{1,0:T(8,128)(2,1)S(1)} %copy-done.8), custom_call_target="tpu_custom_call" | custom-call | flops 4294967296 | bytes 12582912 | tf_op jit(solution)/shard_map/partial_sums/pallas_call | solution.py:168
  118.2 3.7 %partial_sums.9 = bf16[1,1024,256]{2,1,0:T(8,128)(2,1)S(1)} custom-call(bf16[1024,4096]{1,0:T(8,128)(2,1)S(1)} %load_half.3.tokens, bf16[256,1024]{1,0:T(8,128)(2,1)} %collective-permute-done.16.refs_0_, bf16[256,1024]{1,0:T(8,128)(2,1)} %collective-permute-done.17.refs_1_, bf16[256,1024]{1,0:T(8,128)(2,1)S(1)} %collective-permute-done.18.refs_2_, ...), custom_call_target="tpu_custom_call" | custom-call | flops 2147483648 | bytes 10485760 | tf_op jit(solution)/shard_map/partial_sums/pallas_call | solution.py:168
  121.9 0.5 collective-permute-start.20
  122.7 3.7 %partial_sums.10 = bf16[2,4,1024,256]{3,2,1,0:T(8,128)(2,1)S(1)} fusion(bf16[2,4,1024,256]{3,2,1,0:T(8,128)(2,1)S(1)} %fusion, s32[]{:T(128)S(6)} %select_n.168, s32[]{:T(128)S(6)} %select_n.182, bf16[1024,4096]{1,0:T(8,128)(2,1)S(1)} %load_half.2.tokens, bf16[256,1024]{1,0:T(8,128)(2,1)} %collective-permute-done.16.refs_0_, ...), kind=kCustom, calls=%fused_computation.9 | custom fusion | flops 2147483648 | bytes 11010056 | tf_op jit(solution)/shard_map/partial_sums/pallas_call | solution.py:168
  126.5 3.7 %combine.1 = bf16[1024,1024]{1,0:T(8,128)(2,1)} custom-call(bf16[2,4,1024,256]{3,2,1,0:T(8,128)(2,1)S(1)} %bitcast_dynamic-update-slice_fusion.held), custom_call_target="tpu_custom_call" | custom-call | tf_op jit(solution)/shard_map/combine/pallas_call | solution.py:204
  (72 shorter events, 1.2 us)
Async XLA Ops:
  0.6 95.9 %collective-permute-start.9 = (bf16[1024,8192]{1,0:T(8,128)(2,1)}, bf16[1024,8192]{1,0:T(8,128)(2,1)}, u32[]{:S(2)}, u32[]{:S(2)}) collective-permute-start(bf16[1024,8192]{1,0:T(8,128)(2,1)} %bitcast.52), channel_id=1, source_target_pairs={{0,1},{1,0},{2,3},{3,2},{4,5},{5,4},{6,7},{7,6},{8,9},{9,8},{10,11... | collective-permute-start | bytes 50331656 | tf_op jit(solution)/shard_map/ppermute | solution.py:33
  2.1 14.4 %all-to-all-start = ((bf16[4,8,8192]{2,1,0:T(8,128)(2,1)}), bf16[4,8,8192]{2,1,0:T(8,128)(2,1)S(1)}, u32[]{:S(2)}, u32[]{:S(2)}) async-start(bf16[4,8,8192]{2,1,0:T(8,128)(2,1)} %bitcast.62), calls=%async_computation | async-start | bytes 1048576 | tf_op jit(solution)/shard_map/all_to_all | solution.py:235
  16.5 1.2 copy-start.1
  17.8 1.2 copy-start.3
  22.7 13.9 %all-to-all-start.1 = ((bf16[8,8,4096]{2,1,0:T(8,128)(2,1)}), bf16[8,8,4096]{2,1,0:T(8,128)(2,1)S(1)}, u32[]{:S(2)}, u32[]{:S(2)}) async-start(bf16[8,8,4096]{2,1,0:T(8,128)(2,1)} %bitcast.4), calls=%async_computation.1 | async-start | bytes 1048576 | tf_op jit(solution)/shard_map/all_to_all | solution.py:237
  36.7 13.6 %collective-permute-start.6 = (bf16[64,2048]{1,0:T(8,128)(2,1)S(1)}, bf16[64,2048]{1,0:T(8,128)(2,1)S(1)}, u32[]{:S(2)}, u32[]{:S(2)}) collective-permute-start(bf16[64,2048]{1,0:T(8,128)(2,1)S(1)} %get-tuple-element.18), channel_id=1, source_target_pairs={{0,2},{1,9},{2,4},{3,11},{4,6},{5,13},{6,0},{7,15},{8,10},{9,17},{... | collective-permute-start | bytes 786440 | tf_op jit(solution)/shard_map/ppermute | solution.py:37
  38.1 13.1 %collective-permute-start.7 = (bf16[64,2048]{1,0:T(8,128)(2,1)S(1)}, bf16[64,2048]{1,0:T(8,128)(2,1)S(1)}, u32[]{:S(2)}, u32[]{:S(2)}) collective-permute-start(bf16[64,2048]{1,0:T(8,128)(2,1)S(1)} %get-tuple-element.18), channel_id=1, source_target_pairs={{0,4},{1,17},{2,6},{3,19},{4,0},{5,21},{6,2},{7,23},{8,12},{9,25},... | collective-permute-start | bytes 786440 | tf_op jit(solution)/shard_map/ppermute | solution.py:37
  40.7 12.2 %collective-permute-start.8 = (bf16[64,2048]{1,0:T(8,128)(2,1)S(1)}, bf16[64,2048]{1,0:T(8,128)(2,1)S(1)}, u32[]{:S(2)}, u32[]{:S(2)}) collective-permute-start(bf16[64,2048]{1,0:T(8,128)(2,1)S(1)} %get-tuple-element.18), channel_id=1, source_target_pairs={{0,6},{1,25},{2,0},{3,27},{4,2},{5,29},{6,4},{7,31},{8,14},{9,1},{... | collective-permute-start | bytes 786440 | tf_op jit(solution)/shard_map/ppermute | solution.py:37
  41.7 12.5 %collective-permute-start = (bf16[64,2048]{1,0:T(8,128)(2,1)S(1)}, bf16[64,2048]{1,0:T(8,128)(2,1)S(1)}, u32[]{:S(2)}, u32[]{:S(2)}) collective-permute-start(bf16[64,2048]{1,0:T(8,128)(2,1)S(1)} %get-tuple-element.19), channel_id=1, source_target_pairs={{0,2},{1,9},{2,4},{3,11},{4,6},{5,13},{6,0},{7,15},{8,10},{9,17},{... | collective-permute-start | bytes 786440 | tf_op jit(solution)/shard_map/ppermute | solution.py:37
  42.1 5.8 %copy-start = (bf16[1,1024,8192]{2,1,0:T(8,128)(2,1)S(1)}, bf16[1,1024,8192]{2,1,0:T(8,128)(2,1)}, u32[]{:S(2)}) copy-start(bf16[1,1024,8192]{2,1,0:T(8,128)(2,1)} %param.7) | copy-start | bytes 50331652
  50.3 7.1 %collective-permute-start.1 = (bf16[64,2048]{1,0:T(8,128)(2,1)S(1)}, bf16[64,2048]{1,0:T(8,128)(2,1)S(1)}, u32[]{:S(2)}, u32[]{:S(2)}) collective-permute-start(bf16[64,2048]{1,0:T(8,128)(2,1)S(1)} %get-tuple-element.19), channel_id=1, source_target_pairs={{0,4},{1,17},{2,6},{3,19},{4,0},{5,21},{6,2},{7,23},{8,12},{9,25},... | collective-permute-start | bytes 786440 | tf_op jit(solution)/shard_map/ppermute | solution.py:37
  51.2 9.7 %collective-permute-start.2 = (bf16[64,2048]{1,0:T(8,128)(2,1)S(1)}, bf16[64,2048]{1,0:T(8,128)(2,1)S(1)}, u32[]{:S(2)}, u32[]{:S(2)}) collective-permute-start(bf16[64,2048]{1,0:T(8,128)(2,1)S(1)} %get-tuple-element.19), channel_id=1, source_target_pairs={{0,6},{1,25},{2,0},{3,27},{4,2},{5,29},{6,4},{7,31},{8,14},{9,1},{... | collective-permute-start | bytes 786440 | tf_op jit(solution)/shard_map/ppermute | solution.py:37
  53.0 29.8 %collective-permute-start.14 = (bf16[256,2048]{1,0:T(8,128)(2,1)S(1)}, bf16[256,2048]{1,0:T(8,128)(2,1)S(1)}, u32[]{:S(2)}, u32[]{:S(2)}) collective-permute-start(bf16[256,2048]{1,0:T(8,128)(2,1)S(1)} %bitcast.58), channel_id=1, source_target_pairs={{0,8},{1,3},{2,10},{3,5},{4,12},{5,7},{6,14},{7,1},{8,16},{9,11},{... | collective-permute-start | bytes 3145736 | tf_op jit(solution)/shard_map/ppermute | solution.py:37
  54.2 28.6 %collective-permute-start.12 = (bf16[256,2048]{1,0:T(8,128)(2,1)S(1)}, bf16[256,2048]{1,0:T(8,128)(2,1)S(1)}, u32[]{:S(2)}, u32[]{:S(2)}) collective-permute-start(bf16[256,2048]{1,0:T(8,128)(2,1)S(1)} %bitcast.59), channel_id=1, source_target_pairs={{0,24},{1,7},{2,26},{3,1},{4,28},{5,3},{6,30},{7,5},{8,0},{9,15},{... | collective-permute-start | bytes 3145736 | tf_op jit(solution)/shard_map/ppermute | solution.py:37
  61.0 9.3 %collective-permute-start.3 = (f32[8,8192]{1,0:T(8,128)S(1)}, f32[8,8192]{1,0:T(8,128)S(1)}, u32[]{:S(2)}, u32[]{:S(2)}) collective-permute-start(f32[8,8192]{1,0:T(8,128)S(1)} %get-tuple-element.13), channel_id=1, source_target_pairs={{0,32},{32,64},{64,96},{96,0},{1,33},{33,65},{65,97},{97,1},{2,34}... | collective-permute-start | bytes 786440 | tf_op jit(solution)/shard_map/ppermute | solution.py:41
  61.8 8.6 %collective-permute-start.4 = (f32[8,8192]{1,0:T(8,128)S(1)}, f32[8,8192]{1,0:T(8,128)S(1)}, u32[]{:S(2)}, u32[]{:S(2)}) collective-permute-start(f32[8,8192]{1,0:T(8,128)S(1)} %get-tuple-element.13), channel_id=1, source_target_pairs={{0,64},{32,96},{64,0},{96,32},{1,65},{33,97},{65,1},{97,33},{2,66}... | collective-permute-start | bytes 786440 | tf_op jit(solution)/shard_map/ppermute | solution.py:41
  63.1 17.4 %copy-start.2 = (f32[32,8192]{1,0:T(8,128)S(1)}, f32[32,8192]{1,0:T(8,128)}, u32[]{:S(2)}) copy-start(f32[32,8192]{1,0:T(8,128)} %anchor.3) | copy-start | bytes 3145732
  63.1 17.4 %copy-start.4 = (f32[32,8192]{1,0:T(8,128)S(1)}, f32[32,8192]{1,0:T(8,128)}, u32[]{:S(2)}) copy-start(f32[32,8192]{1,0:T(8,128)} %momentum.3) | copy-start | bytes 3145732
  63.1 17.4 %copy-start.5 = (bf16[1,32,8192]{2,1,0:T(8,128)(2,1)S(1)}, bf16[1,32,8192]{2,1,0:T(8,128)(2,1)}, u32[]{:S(2)}) copy-start(bf16[1,32,8192]{2,1,0:T(8,128)(2,1)} %param.6) | copy-start | bytes 1572868
  70.3 7.9 %collective-permute-start.5 = (f32[8,8192]{1,0:T(8,128)S(1)}, f32[8,8192]{1,0:T(8,128)S(1)}, u32[]{:S(2)}, u32[]{:S(2)}) collective-permute-start(f32[8,8192]{1,0:T(8,128)S(1)} %get-tuple-element.13), channel_id=1, source_target_pairs={{0,96},{32,0},{64,32},{96,64},{1,97},{33,1},{65,33},{97,65},{2,98}... | collective-permute-start | bytes 786440 | tf_op jit(solution)/shard_map/ppermute | solution.py:41
  70.3 17.5 %collective-permute-start.13 = (bf16[256,2048]{1,0:T(8,128)(2,1)S(1)}, bf16[256,2048]{1,0:T(8,128)(2,1)S(1)}, u32[]{:S(2)}, u32[]{:S(2)}) collective-permute-start(bf16[256,2048]{1,0:T(8,128)(2,1)S(1)} %bitcast.55), channel_id=1, source_target_pairs={{0,8},{1,3},{2,10},{3,5},{4,12},{5,7},{6,14},{7,1},{8,16},{9,11},{... | collective-permute-start | bytes 3145736 | tf_op jit(solution)/shard_map/ppermute | solution.py:37
  78.2 13.9 %collective-permute-start.11 = (bf16[256,2048]{1,0:T(8,128)(2,1)S(1)}, bf16[256,2048]{1,0:T(8,128)(2,1)S(1)}, u32[]{:S(2)}, u32[]{:S(2)}) collective-permute-start(bf16[256,2048]{1,0:T(8,128)(2,1)S(1)} %bitcast.56), channel_id=1, source_target_pairs={{0,24},{1,7},{2,26},{3,1},{4,28},{5,3},{6,30},{7,5},{8,0},{9,15},{... | collective-permute-start | bytes 3145736 | tf_op jit(solution)/shard_map/ppermute | solution.py:37
  82.8 13.7 %copy-start.6 = (bf16[256,2048]{1,0:T(8,128)(2,1)}, bf16[256,2048]{1,0:T(8,128)(2,1)S(1)}, u32[]{:S(2)}) copy-start(bf16[256,2048]{1,0:T(8,128)(2,1)S(1)} %collective-permute-done.14.refs_3_) | copy-start | bytes 3145732
  82.8 30.7 %collective-permute-start.18 = (bf16[256,1024]{1,0:T(8,128)(2,1)S(1)}, bf16[256,1024]{1,0:T(8,128)(2,1)S(1)}, u32[]{:S(2)}, u32[]{:S(2)}) collective-permute-start(bf16[256,1024]{1,0:T(8,128)(2,1)S(1)} %slice.48), channel_id=1, source_target_pairs={{0,8},{1,3},{2,10},{3,5},{4,12},{5,7},{6,14},{7,1},{8,16},{9,11},{... | collective-permute-start | bytes 1572872 | tf_op jit(solution)/shard_map/ppermute | solution.py:37
  82.9 13.6 %copy-start.9 = (bf16[256,2048]{1,0:T(8,128)(2,1)}, bf16[256,2048]{1,0:T(8,128)(2,1)S(1)}, u32[]{:S(2)}) copy-start(bf16[256,2048]{1,0:T(8,128)(2,1)S(1)} %collective-permute-done.12.refs_1_) | copy-start | bytes 3145732
  83.9 34.3 %collective-permute-start.19 = (bf16[256,1024]{1,0:T(8,128)(2,1)}, bf16[256,1024]{1,0:T(8,128)(2,1)}, u32[]{:S(2)}, u32[]{:S(2)}) collective-permute-start(bf16[256,1024]{1,0:T(8,128)(2,1)} %slice.49), channel_id=1, source_target_pairs={{0,24},{1,7},{2,26},{3,1},{4,28},{5,3},{6,30},{7,5},{8,0},{9,15},{... | collective-permute-start | bytes 1572872 | tf_op jit(solution)/shard_map/ppermute | solution.py:37
  87.8 8.7 %copy-start.12 = (bf16[256,2048]{1,0:T(8,128)(2,1)}, bf16[256,2048]{1,0:T(8,128)(2,1)S(1)}, u32[]{:S(2)}) copy-start(bf16[256,2048]{1,0:T(8,128)(2,1)S(1)} %collective-permute-done.13.refs_2_) | copy-start | bytes 3145732
  88.7 29.5 %collective-permute-start.16 = (bf16[256,1024]{1,0:T(8,128)(2,1)}, bf16[256,1024]{1,0:T(8,128)(2,1)}, u32[]{:S(2)}, u32[]{:S(2)}) collective-permute-start(bf16[256,1024]{1,0:T(8,128)(2,1)} %slice.46), channel_id=1, source_target_pairs={{0,8},{1,3},{2,10},{3,5},{4,12},{5,7},{6,14},{7,1},{8,16},{9,11},{... | collective-permute-start | bytes 1572872 | tf_op jit(solution)/shard_map/ppermute | solution.py:37
  92.2 4.3 %copy-start.15 = (bf16[256,2048]{1,0:T(8,128)(2,1)}, bf16[256,2048]{1,0:T(8,128)(2,1)S(1)}, u32[]{:S(2)}) copy-start(bf16[256,2048]{1,0:T(8,128)(2,1)S(1)} %collective-permute-done.11.refs_0_) | copy-start | bytes 3145732
  93.1 25.1 %collective-permute-start.17 = (bf16[256,1024]{1,0:T(8,128)(2,1)}, bf16[256,1024]{1,0:T(8,128)(2,1)}, u32[]{:S(2)}, u32[]{:S(2)}) collective-permute-start(bf16[256,1024]{1,0:T(8,128)(2,1)} %slice.47), channel_id=1, source_target_pairs={{0,24},{1,7},{2,26},{3,1},{4,28},{5,3},{6,30},{7,5},{8,0},{9,15},{... | collective-permute-start | bytes 1572872 | tf_op jit(solution)/shard_map/ppermute | solution.py:37
  96.5 3.6 %copy-start.7 = (bf16[256,2048]{1,0:T(8,128)(2,1)S(1)}, bf16[256,2048]{1,0:T(8,128)(2,1)}, u32[]{:S(2)}) copy-start(bf16[256,2048]{1,0:T(8,128)(2,1)} %copy-done.6) | copy-start | bytes 3145732
  96.5 3.9 %copy-start.10 = (bf16[256,2048]{1,0:T(8,128)(2,1)S(1)}, bf16[256,2048]{1,0:T(8,128)(2,1)}, u32[]{:S(2)}) copy-start(bf16[256,2048]{1,0:T(8,128)(2,1)} %copy-done.9) | copy-start | bytes 3145732
  96.5 4.2 %copy-start.13 = (bf16[256,2048]{1,0:T(8,128)(2,1)S(1)}, bf16[256,2048]{1,0:T(8,128)(2,1)}, u32[]{:S(2)}) copy-start(bf16[256,2048]{1,0:T(8,128)(2,1)} %copy-done.12) | copy-start | bytes 3145732
  96.5 4.5 %copy-start.16 = (bf16[256,2048]{1,0:T(8,128)(2,1)S(1)}, bf16[256,2048]{1,0:T(8,128)(2,1)}, u32[]{:S(2)}) copy-start(bf16[256,2048]{1,0:T(8,128)(2,1)} %copy-done.15) | copy-start | bytes 3145732
  105.6 8.0 %copy-start.8 = (bf16[256,2048]{1,0:T(8,128)(2,1)S(1)}, bf16[256,2048]{1,0:T(8,128)(2,1)}, u32[]{:S(2)}) copy-start(bf16[256,2048]{1,0:T(8,128)(2,1)} %copy-done.6) | copy-start | bytes 3145732
  105.6 8.0 %copy-start.11 = (bf16[256,2048]{1,0:T(8,128)(2,1)S(1)}, bf16[256,2048]{1,0:T(8,128)(2,1)}, u32[]{:S(2)}) copy-start(bf16[256,2048]{1,0:T(8,128)(2,1)} %copy-done.9) | copy-start | bytes 3145732
  105.6 8.0 %copy-start.14 = (bf16[256,2048]{1,0:T(8,128)(2,1)S(1)}, bf16[256,2048]{1,0:T(8,128)(2,1)}, u32[]{:S(2)}) copy-start(bf16[256,2048]{1,0:T(8,128)(2,1)} %copy-done.12) | copy-start | bytes 3145732
  105.6 8.0 %copy-start.17 = (bf16[256,2048]{1,0:T(8,128)(2,1)S(1)}, bf16[256,2048]{1,0:T(8,128)(2,1)}, u32[]{:S(2)}) copy-start(bf16[256,2048]{1,0:T(8,128)(2,1)} %copy-done.15) | copy-start | bytes 3145732
  105.6 16.9 %collective-permute-start.15 = (bf16[2,1024,256]{2,1,0:T(8,128)(2,1)S(1)}, bf16[2,1024,256]{2,1,0:T(8,128)(2,1)S(1)}, u32[]{:S(2)}, u32[]{:S(2)}) collective-permute-start(bf16[2,1024,256]{2,1,0:T(8,128)(2,1)S(1)} %partial_sums.8), channel_id=1, source_target_pairs={{0,1},{1,0},{2,3},{3,2},{4,5},{5,4},{6,7},{7,6},{8,9},{9,8},{10,11... | collective-permute-start | bytes 3145736 | tf_op jit(solution)/shard_map/ppermute | solution.py:33
  113.5 9.0 %collective-permute-start.10 = (bf16[1,1024,256]{2,1,0:T(8,128)(2,1)S(1)}, bf16[1,1024,256]{2,1,0:T(8,128)(2,1)S(1)}, u32[]{:S(2)}, u32[]{:S(2)}) collective-permute-start(bf16[1,1024,256]{2,1,0:T(8,128)(2,1)S(1)} %partial_sums.6), channel_id=1, source_target_pairs={{0,1},{1,0},{2,3},{3,2},{4,5},{5,4},{6,7},{7,6},{8,9},{9,8},{10,11... | collective-permute-start | bytes 1572872 | tf_op jit(solution)/shard_map/ppermute | solution.py:33
  121.9 4.5 %collective-permute-start.20 = (bf16[1,1024,256]{2,1,0:T(8,128)(2,1)S(1)}, bf16[1,1024,256]{2,1,0:T(8,128)(2,1)S(1)}, u32[]{:S(2)}, u32[]{:S(2)}) collective-permute-start(bf16[1,1024,256]{2,1,0:T(8,128)(2,1)S(1)} %partial_sums.9), channel_id=1, source_target_pairs={{0,1},{1,0},{2,3},{3,2},{4,5},{5,4},{6,7},{7,6},{8,9},{9,8},{10,11... | collective-permute-start | bytes 1572872 | tf_op jit(solution)/shard_map/ppermute | solution.py:33

commit v2 on v1

v2 whole, which is shorter than its diff:
```python
import functools

import jax
import jax.numpy as jnp
from jax import lax
from jax.experimental import pallas as pl
from jax.experimental.pallas import tpu as pltpu
from jax.sharding import PartitionSpec as P

SIDE = 4
BLOCK = 128
CHUNKS = 2
MERGE_COLS = 512
UPDATE_COLS = 2048
MIB = 1024 * 1024


def fsdp_index(y, x, core):
    return ((y % SIDE) * SIDE + x % SIDE) * 2 + core


def ring_pairs(step, second):
    pairs = []
    for y in range(SIDE):
        for x in range(SIDE):
            for core in range(2):
                along_x = (core == 0) != second
                target = (y, x + step) if along_x else (y + step, x)
                pairs.append((fsdp_index(y, x, core), fsdp_index(*target, core)))
    return pairs


def in_hbm(value):
    return pltpu.with_memory_space_constraint(value, pltpu.HBM)


def in_vmem(value):
    return pltpu.with_memory_space_constraint(value, pltpu.VMEM)


def to_mate(value):
    return lax.ppermute(value, "core", [(0, 1), (1, 0)])


def to_ring(value, step, second):
    return lax.ppermute(value, ("chip", "core"), ring_pairs(step, second))


def to_replica(value, step):
    return lax.ppermute(value, "replica", [(i, (i + step) % SIDE) for i in range(SIDE)])


def merge_body(anchor, momentum, gathered, outer_grad, merged):
    rows, width = anchor.shape
    blocks = MERGE_COLS // BLOCK
    size = blocks * rows
    spread = jnp.full((BLOCK, BLOCK), 4.0 / BLOCK, jnp.bfloat16)

    def stacked(value):
        return jnp.concatenate([value[:, i * BLOCK : (i + 1) * BLOCK] for i in range(blocks)], axis=0)

    for start in range(0, width, MERGE_COLS):
        cols = slice(start, start + MERGE_COLS)
        local = gathered[:, cols].astype(jnp.float32)
        local = jnp.concatenate([stacked(local[r * rows : (r + 1) * rows]) for r in range(SIDE)], axis=0)
        base = stacked(anchor[:, cols])
        delta = jnp.concatenate([base] * SIDE, axis=0) - local
        square = delta * delta
        high = square.astype(jnp.bfloat16)
        low = (square - high.astype(jnp.float32)).astype(jnp.bfloat16)
        mean = jnp.dot(high, spread, preferred_element_type=jnp.float32)
        mean = mean + jnp.dot(low, spread, preferred_element_type=jnp.float32) + 4e-06
        scale = (mean * lax.rsqrt(mean)).astype(jnp.bfloat16).astype(jnp.float32)
        codes = jnp.clip(delta * pl.reciprocal(scale), -1.0, 1.0).astype(jnp.bfloat16)
        decoded = codes.astype(jnp.float32) * scale
        parts = [decoded[r * size : (r + 1) * size] for r in range(SIDE)]
        grad = ((parts[0] + parts[2]) + (parts[1] + parts[3])) * 0.25
        speed = 0.9 * stacked(momentum[:, cols]) + grad
        anchored = base - 0.7 * (grad + 0.9 * speed)
        blend = (0.5 * local + 0.5 * jnp.concatenate([anchored] * SIDE, axis=0)).astype(merged.dtype)
        for i in range(blocks):
            place = slice(start + i * BLOCK, start + (i + 1) * BLOCK)
            outer_grad[:, place] = grad[i * rows : (i + 1) * rows]
            for r in range(SIDE):
                merged[r * rows : (r + 1) * rows, place] = blend[r * size + i * rows : r * size + (i + 1) * rows]


def merge(anchor, momentum, gathered):
    vmem = pl.BlockSpec(memory_space=pltpu.VMEM)
    return pl.pallas_call(
        merge_body,
        in_specs=[vmem] * 3,
        out_specs=[vmem] * 2,
        out_shape=[
            jax.ShapeDtypeStruct(anchor.shape, jnp.float32),
            jax.ShapeDtypeStruct(gathered.shape, jnp.bfloat16),
        ],
        compiler_params=pltpu.CompilerParams(vmem_limit_bytes=8 * MIB),
        name="merge",
    )(in_vmem(anchor), in_vmem(momentum), in_vmem(gathered))


def update_body(anchor, momentum, local, outer_grad, new_anchor, new_momentum, merged):
    grad = outer_grad[...]
    speed = 0.9 * momentum[...] + grad
    anchored = anchor[...] - 0.7 * (grad + 0.9 * speed)
    new_momentum[...] = speed
    new_anchor[...] = anchored
    merged[...] = (0.5 * local[...].astype(jnp.float32) + 0.5 * anchored).astype(merged.dtype)


def update(anchor, momentum, local, outer_grad):
    rows, width = anchor.shape
    tile = pl.BlockSpec((rows, UPDATE_COLS), lambda i: (0, i))
    wide = jax.ShapeDtypeStruct((rows, width), jnp.float32)
    return pl.pallas_call(
        update_body,
        grid=(width // (UPDATE_COLS),),
        in_specs=[tile] * 4,
        out_specs=[tile] * 3,
        out_shape=[wide, wide, jax.ShapeDtypeStruct((rows, width), jnp.bfloat16)],
        compiler_params=pltpu.CompilerParams(vmem_limit_bytes=12 * MIB),
        name="update",
    )(in_hbm(anchor), in_hbm(momentum), in_hbm(local), outer_grad)


def load_body(start_ref, tokens, *refs):
    half, sem = refs[-2:]
    start = pl.multiple_of(start_ref[0], half.shape[1])
    copy = pltpu.make_async_copy(tokens.at[:, pl.ds(start, half.shape[1])], half, sem)
    copy.start()
    copy.wait()


def load_columns(start, tokens, width, *earlier):
    anywhere = pl.BlockSpec(memory_space=pl.ANY)
    return pl.pallas_call(
        load_body,
        in_specs=[pl.BlockSpec(memory_space=pltpu.SMEM), pl.BlockSpec(memory_space=pltpu.HBM)]
        + [anywhere] * len(earlier),
        out_specs=pl.BlockSpec(memory_space=pltpu.VMEM),
        out_shape=pltpu.VMEM((tokens.shape[0], width), tokens.dtype),
        scratch_shapes=[pltpu.SemaphoreType.DMA(())],
        compiler_params=pltpu.CompilerParams(vmem_limit_bytes=2 * MIB),
        name="load_columns",
    )(start.astype(jnp.int32).reshape(1), in_hbm(tokens), *earlier)


def partial_body(per_block, tokens, *refs):
    weights, out = refs[:-1], refs[-1]
    for block in range(out.shape[0]):
        start, total = 0, None
        for piece in weights[block * per_block : (block + 1) * per_block]:
            term = lax.dot_general(
                tokens[:, start : start + piece.shape[1]],
                piece[...],
                (((1,), (1,)), ((), ())),
                preferred_element_type=jnp.float32,
            )
            total = term if total is None else total + term
            start += piece.shape[1]
        out[block] = total.astype(out.dtype)


def partial_sums(tokens, weights):
    count, half = tokens.shape
    blocks, per_block = len(weights), len(weights[0])
    units = weights[0][0].shape[0]
    vmem = pl.BlockSpec(memory_space=pltpu.VMEM)
    return pl.pallas_call(
        functools.partial(partial_body, per_block),
        in_specs=[vmem] * (1 + blocks * per_block),
        out_specs=vmem,
        out_shape=jax.ShapeDtypeStruct((blocks, count, units), jnp.bfloat16),
        compiler_params=pltpu.CompilerParams(vmem_limit_bytes=16 * MIB),
        cost_estimate=pl.CostEstimate(
            flops=2 * count * units * blocks * half,
            bytes_accessed=2 * (count + units * blocks) * half,
            transcendentals=0,
        ),
        name="partial_sums",
    )(in_vmem(tokens), *[in_vmem(piece) for block in weights for piece in block])


COMBINE_ROWS = 256


def combine_body(held, out):
    rows = pl.ds(pl.multiple_of(pl.program_id(0) * COMBINE_ROWS, COMBINE_ROWS), COMBINE_ROWS)
    low = lax.broadcasted_iota(jnp.int32, (COMBINE_ROWS, BLOCK), 1) < BLOCK // 2
    for x in (0, 2):
        for k in range(SIDE // 2):
            cols = slice(k * BLOCK, (k + 1) * BLOCK)
            left = held[1, x, rows, cols].astype(jnp.float32)
            right = held[1, x + 1, rows, cols].astype(jnp.float32)
            crossed = pltpu.roll(jnp.where(low, right, left), BLOCK // 2, 1)
            for y, term in ((2 * k, jnp.where(low, left, crossed)), (2 * k + 1, jnp.where(low, crossed, right))):
                natural = held[0, y, rows, slice(x // 2 * BLOCK, (x // 2 + 1) * BLOCK)].astype(jnp.float32)
                start = (2 * y + x // 2) * BLOCK
                out[:, start : start + BLOCK] = (natural + term).astype(out.dtype)


def combine(held):
    _, _, count, units = held.shape
    return pl.pallas_call(
        combine_body,
        grid=(count // COMBINE_ROWS,),
        in_specs=[pl.BlockSpec(memory_space=pltpu.VMEM)],
        out_specs=pl.BlockSpec((COMBINE_ROWS, units * SIDE), lambda i: (i, 0)),
        out_shape=jax.ShapeDtypeStruct((count, units * SIDE), jnp.bfloat16),
        compiler_params=pltpu.CompilerParams(vmem_limit_bytes=12 * MIB),
        name="combine",
    )(held)


def on_device(anchor, momentum, local_weights, tokens):
    rows, width = anchor.shape
    half = width // 2
    part = half // CHUNKS
    replica = lax.axis_index("replica")
    core = lax.axis_index("core")
    chip = lax.axis_index("chip")
    x = chip % SIDE
    y = chip // SIDE
    first_base = jnp.where(core == 0, x, y)
    second_base = jnp.where(core == 0, y, x)
    local = local_weights[0]
    batch = tokens[0]

    share = rows // SIDE
    mine, other = core * half, (1 - core) * half
    row = replica * share

    def both_cores(own, got):
        return jnp.where(core == 0, jnp.stack([own, got]), jnp.stack([got, own]))

    def columns(value, start):
        return lax.dynamic_slice(value, (0, start), (value.shape[0], half))

    state = jnp.concatenate(
        [lax.dynamic_slice(value, (row, 0), (share, width)) for value in (anchor, momentum)], axis=0
    )
    local_pair = both_cores(columns(local, mine), to_mate(columns(local, other)))
    state_pair = both_cores(columns(state, mine), to_mate(columns(state, other)))
    local_pair = local_pair.reshape(2, SIDE, share, half).transpose(1, 0, 2, 3)
    own_anchor, own_momentum = state_pair.reshape(2, 2, share, half).transpose(1, 0, 2, 3).reshape(2, 2 * share, half)

    def share_of(value, step):
        return lax.dynamic_slice(value, ((replica + step) % SIDE, 0, 0, 0), (1,) + value.shape[1:])

    def exchange(value):
        pieces = [(step, to_replica(share_of(value, step), step)) for step in (1, 3, 2)]
        return [(0, share_of(value, 0))] + pieces

    gathered = jnp.zeros_like(local_pair)
    received = exchange(local_pair)
    mate_half = to_mate(load_columns(other, batch, half, received[1][1], own_anchor))
    for step, piece in received:
        gathered = lax.dynamic_update_slice(gathered, piece, ((replica - step) % SIDE, 0, 0, 0))
    gathered = gathered.reshape(SIDE * 2 * share, half)
    outer_part, merged_parts = merge(own_anchor, own_momentum, gathered)
    pair = jnp.zeros((2, SIDE, share, half), jnp.bfloat16)
    for step, piece in exchange(merged_parts.reshape(SIDE, 2, share, half)):
        pair = lax.dynamic_update_slice(pair, piece.reshape(2, 1, share, half), (0, (replica - step) % SIDE, 0, 0))
    pair = pair.reshape(2 * rows, half)

    own_half = load_columns(mine, batch, half, pair)
    block = jnp.zeros((SIDE, 2 * rows, half), jnp.bfloat16)
    pieces = [pair] + [to_ring(pair, step, False) for step in (1, 3, 2)]
    for step, piece in zip((0, 1, 3, 2), pieces):
        block = lax.dynamic_update_slice(block, piece[None], ((first_base - step) % SIDE, 0, 0))
    whole = block.reshape(SIDE * 2 * rows, half)
    blocks = []
    for c in range(CHUNKS):
        block = whole[:, c * part : (c + 1) * part]
        before = to_ring(block, 1, True)
        following = to_ring(block, SIDE - 1, True)
        low = to_ring(before[:, : part // 2], 1, True)
        high = to_ring(following[:, part // 2 :], SIDE - 1, True)
        blocks.append((block, following, before, low, high))

    first = [[b[0] for b in blocks]]
    middle = [[b[1] for b in blocks], [b[2] for b in blocks]]
    last = [[piece for b in blocks for piece in b[3:]]]
    held = jnp.zeros((2, SIDE, tokens.shape[1], rows * 2 * SIDE), jnp.bfloat16)

    def place(held, which, base, steps, sums):
        for i, step in enumerate(steps):
            held = lax.dynamic_update_slice(held, sums[i][None, None], (which, (base + step) % SIDE, 0, 0))
        return held

    held = place(held, core, second_base, (0,), partial_sums(own_half, first))
    got = to_mate(partial_sums(mate_half, first + middle))
    held = place(held, core, second_base, (1, 3), partial_sums(own_half, middle))
    held = place(held, 1 - core, first_base, (0, 1, 3), got)
    got = to_mate(partial_sums(mate_half, last))
    held = place(held, core, second_base, (2,), partial_sums(own_half, last))
    held = place(held, 1 - core, first_base, (2,), got)
    gate_out = combine(held)

    grads = jnp.zeros((SIDE, 2, share, half), jnp.float32)
    outer_part = outer_part.reshape(1, 2, share, half)
    grads = lax.dynamic_update_slice(grads, outer_part, (replica, 0, 0, 0))
    neighbour = lax.ppermute(outer_part, "replica", [(i, i ^ 1) for i in range(SIDE)])
    grads = lax.dynamic_update_slice(grads, neighbour, (replica ^ 1, 0, 0, 0))
    both = jnp.concatenate([outer_part, neighbour])
    opposite = lax.ppermute(both, "replica", [(i, i ^ 3) for i in range(SIDE)])
    grads = lax.dynamic_update_slice(grads, opposite[:1], (replica ^ 3, 0, 0, 0))
    grads = lax.dynamic_update_slice(grads, opposite[1:], (replica ^ 2, 0, 0, 0))

    def rows_of(which):
        return lax.dynamic_slice(grads, (0, which, 0, 0), (SIDE, 1, share, half)).reshape(rows, half)

    own_grad, mate_grad = rows_of(core), to_mate(rows_of(1 - core))
    outer_grad = jnp.where(
        core == 0, jnp.concatenate([own_grad, mate_grad], axis=1), jnp.concatenate([mate_grad, own_grad], axis=1)
    )
    new_anchor, new_momentum, merged = update(anchor, momentum, local, outer_grad)
    return (new_anchor, new_momentum, merged[None], gate_out[None])


def solution(mesh):
    split = jax.sharding.Mesh(mesh.devices.reshape(SIDE, SIDE * SIDE, 2), ("replica", "chip", "core"))
    fsdp = ("chip", "core")
    return jax.shard_map(
        on_device,
        mesh=split,
        in_specs=(
            P(fsdp, None),
            P(fsdp, None),
            P("replica", fsdp, None),
            P("replica", fsdp, None),
        ),
        out_specs=(
            P(fsdp, None),
            P(fsdp, None),
            P("replica", fsdp, None),
            P("replica", fsdp, None),
        ),
        check_vma=False,
    )
```

time: 131 us -> 108 us (0.82)
  local copies, waits for them, and re-layouts: 13.2 us -> 3.93 us
  waiting for transfers between devices: 38.4 us -> 31.7 us
  starting transfers between devices: 41 us -> 38.2 us
  Pallas kernels: 30.4 us -> 27.7 us
    all_to_all x2 -> x0, waiting for transfers between devices: 18.7 us -> none  [the longest x1 9.37 us: on_device(): lax.all_to_all(merged_parts.reshape(2 * rows, half), ('core', 'replica'),...]
    ppermute x14 -> x11, waiting for transfers between devices: 10.1 us -> 25.6 us  [to_ring(): return lax.ppermute(value, ('chip', 'core'), ring_pairs(step, second))]
    all_to_all x2 -> x0, starting transfers between devices: 9.66 us -> none  [the longest x1 5.11 us: on_device(): gathered = lax.all_to_all(local, 'replica', 0, 0, tiled=True)]
    unnamed x36 -> x0, local copies, waits for them, and re-layouts: 9.25 us -> none
    ppermute x3 -> x6, starting transfers between devices: 1.74 us -> 8.09 us  [to_replica(): lax.ppermute(value, 'replica', [(i, (i + step) % SIDE) for i in range(SID...]
    ppermute x14 -> x11, starting transfers between devices: 22 us -> 15.8 us  [to_ring(): return lax.ppermute(value, ('chip', 'core'), ring_pairs(step, second))]
    ppermute x3 -> x6, waiting for transfers between devices: 9.63 us -> 6.08 us  [to_replica(): lax.ppermute(value, 'replica', [(i, (i + step) % SIDE) for i in range(SID...]
    ppermute x0 -> x2, starting transfers between devices: none -> 3.5 us  [the longest x1 2.35 us: on_device(): opposite = lax.ppermute(both, 'replica', [(i, i ^ 3) for i in range(SIDE)])]
  transfers between devices with their start and end apart: 23 -> 25, of which waited for: 8 -> 7; matrix products, arithmetic and copies ran while one was open for 8% -> 7% of each run, Pallas kernels for 21% -> 22%
where the time goes in v2:
time: 108 us
  starting transfers between devices  38.2 us (35%)
  waiting for transfers between devices  31.7 us (29%)
  Pallas kernels  27.7 us (26%)
  other arithmetic  5.03 us (5%)
  local copies, waits for them, and re-layouts  3.93 us (4%)
  between operations  1.49 us (1%)
    ppermute x11, waiting for transfers between devices, to_ring(): return lax.ppermute(value, ('chip', 'core'), ring_pairs(step, second))  25.6 us
    ppermute x11, starting transfers between devices, to_ring(): return lax.ppermute(value, ('chip', 'core'), ring_pairs(step, second))  15.8 us
    pallas_call x3, Pallas kernels, partial_sums(): pl.pallas_call(functools.partial(partial_body, per_block), in_specs=[vmem...  13.6 us
    ppermute x6, starting transfers between devices, to_mate(): return lax.ppermute(value, 'core', [(0, 1), (1, 0)])  10.8 us
    ppermute x6, starting transfers between devices, to_replica(): lax.ppermute(value, 'replica', [(i, (i + step) % SIDE) for i in range(SID...  8.09 us
    pallas_call x2, Pallas kernels, load_columns(): pl.pallas_call(load_body, in_specs=[pl.BlockSpec(memory_space=pltpu.SMEM)...  6.78 us
    ppermute x6, waiting for transfers between devices, to_replica(): lax.ppermute(value, 'replica', [(i, (i + step) % SIDE) for i in range(SID...  6.08 us
    pallas_call x2, other arithmetic, partial_sums(): pl.pallas_call(functools.partial(partial_body, per_block), in_specs=[vmem...  4.73 us
  transfers between devices with their start and end apart: 25, of which 7 were waited for; matrix products, arithmetic and copies ran while one was open for 7% of the time, Pallas kernels for 22%

profile of v2, /device:TPU:1, one launch (start us, length us, event | category | flops | bytes accessed | tf_op | source)
XLA Modules:
  0.0 108.1 jit_solution(16463057658075196415)
XLA Ops:
  0.6 1.1 dynamic-slice_bitcast_fusion.3
  1.7 1.5 %collective-permute-start.1 = (bf16[32,4096]{1,0:T(8,128)(2,1)S(1)}, bf16[32,4096]{1,0:T(8,128)(2,1)S(1)}, u32[]{:S(2)}, u32[]{:S(2)}) collective-permute-start(bf16[32,4096]{1,0:T(8,128)(2,1)S(1)} %get-tuple-element.25), channel_id=1, source_target_pairs={{0,1},{1,0},{2,3},{3,2},{4,5},{5,4},{6,7},{7,6},{8,9},{9,8},{10,11... | collective-permute-start | bytes 786440 | tf_op jit(solution)/shard_map/ppermute | solution.py:42
  3.2 1.1 constant_dynamic-slice_fusion.3
  4.3 0.1 collective-permute-start
  4.9 1.8 %collective-permute-start.2 = (bf16[1,2,8,4096]{3,2,1,0:T(8,128)(2,1)S(1)}, bf16[1,2,8,4096]{3,2,1,0:T(8,128)(2,1)S(1)}, u32[]{:S(2)}, u32[]{:S(2)}) collective-permute-start(bf16[1,2,8,4096]{3,2,1,0:T(8,128)(2,1)S(1)} %get-tuple-element.23), channel_id=1, source_target_pairs={{0,32},{32,64},{64,96},{96,0},{1,33},{33,65},{65,97},{97,1},{2,34}... | collective-permute-start | bytes 393224 | tf_op jit(solution)/shard_map/ppermute | solution.py:50
  6.7 2.2 %collective-permute-start.3 = (bf16[1,2,8,4096]{3,2,1,0:T(8,128)(2,1)S(1)}, bf16[1,2,8,4096]{3,2,1,0:T(8,128)(2,1)S(1)}, u32[]{:S(2)}, u32[]{:S(2)}) collective-permute-start(bf16[1,2,8,4096]{3,2,1,0:T(8,128)(2,1)S(1)} %get-tuple-element.22), channel_id=1, source_target_pairs={{0,96},{32,0},{64,32},{96,64},{1,97},{33,1},{65,33},{97,65},{2,98}... | collective-permute-start | bytes 393224 | tf_op jit(solution)/shard_map/ppermute | solution.py:50
  8.9 1.2 %collective-permute-start.4 = (bf16[1,2,8,4096]{3,2,1,0:T(8,128)(2,1)S(1)}, bf16[1,2,8,4096]{3,2,1,0:T(8,128)(2,1)S(1)}, u32[]{:S(2)}, u32[]{:S(2)}) collective-permute-start(bf16[1,2,8,4096]{3,2,1,0:T(8,128)(2,1)S(1)} %get-tuple-element.21), channel_id=1, source_target_pairs={{0,64},{32,96},{64,0},{96,32},{1,65},{33,97},{65,1},{97,33},{2,66}... | collective-permute-start | bytes 393224 | tf_op jit(solution)/shard_map/ppermute | solution.py:50
  10.3 2.3 %collective-permute-done.2.refs_0_ = bf16[1,2,8,4096]{3,2,1,0:T(8,128)(2,1)S(1)} collective-permute-done((bf16[1,2,8,4096]{3,2,1,0:T(8,128)(2,1)S(1)}, bf16[1,2,8,4096]{3,2,1,0:T(8,128)(2,1)S(1)}, u32[]{:S(2)}, u32[]{:S(2)}) %collective-permute-start.2) | collective-permute-done | bytes 131104 | tf_op jit(solution)/shard_map/ppermute | solution.py:50
  12.7 3.8 %collective-permute-done.4 = bf16[1,2,8,4096]{3,2,1,0:T(8,128)(2,1)S(1)} collective-permute-done((bf16[1,2,8,4096]{3,2,1,0:T(8,128)(2,1)S(1)}, bf16[1,2,8,4096]{3,2,1,0:T(8,128)(2,1)S(1)}, u32[]{:S(2)}, u32[]{:S(2)}) %collective-permute-start.4) | collective-permute-done | bytes 131104 | tf_op jit(solution)/shard_map/ppermute | solution.py:50
  16.5 1.0 merge.1
  17.5 0.6 collective-permute-start.8
  18.1 2.1 %collective-permute-start.9 = (bf16[1,2,8,4096]{3,2,1,0:T(8,128)(2,1)S(1)}, bf16[1,2,8,4096]{3,2,1,0:T(8,128)(2,1)S(1)}, u32[]{:S(2)}, u32[]{:S(2)}) collective-permute-start(bf16[1,2,8,4096]{3,2,1,0:T(8,128)(2,1)S(1)} %get-tuple-element.19), channel_id=1, source_target_pairs={{0,96},{32,0},{64,32},{96,64},{1,97},{33,1},{65,33},{97,65},{2,98}... | collective-permute-start | bytes 393224 | tf_op jit(solution)/shard_map/ppermute | solution.py:50
  20.2 0.1 collective-permute-start.10
  20.3 3.4 %load_columns.3 = bf16[1024,4096]{1,0:T(8,128)(2,1)S(1)} custom-call(s32[1]{0:T(128)} %bitcast.40.start_ref, bf16[1024,8192]{1,0:T(8,128)(2,1)} %bitcast.97, bf16[1,2,8,4096]{3,2,1,0:T(8,128)(2,1)S(1)} %collective-permute-done.2.refs_0_, f32[16,4096]{1,0:T(8,128)S(1)} %get-tuple-element.27.anchor.refs_1_), custom_call_target="tpu_custom_call" | custom-call | tf_op jit(solution)/shard_map/load_columns/pallas_call | solution.py:137
  23.7 1.5 %collective-permute-start.18 = (bf16[1024,4096]{1,0:T(8,128)(2,1)S(1)}, bf16[1024,4096]{1,0:T(8,128)(2,1)S(1)}, u32[]{:S(2)}, u32[]{:S(2)}) collective-permute-start(bf16[1024,4096]{1,0:T(8,128)(2,1)S(1)} %load_columns.3), channel_id=1, source_target_pairs={{0,1},{1,0},{2,3},{3,2},{4,5},{5,4},{6,7},{7,6},{8,9},{9,8},{10,11... | collective-permute-start | bytes 25165832 | tf_op jit(solution)/shard_map/ppermute | solution.py:42
  25.2 1.2 %collective-permute-start.5 = (f32[1,2,8,4096]{3,2,0,1:T(8,128)S(1)}, f32[1,2,8,4096]{3,2,0,1:T(8,128)S(1)}, u32[]{:S(2)}, u32[]{:S(2)}) collective-permute-start(f32[1,2,8,4096]{3,2,0,1:T(8,128)S(1)} %bitcast.93), channel_id=1, source_target_pairs={{0,32},{32,0},{64,96},{96,64},{1,33},{33,1},{65,97},{97,65},{2,34}... | collective-permute-start | bytes 786440 | tf_op jit(solution)/shard_map/ppermute | solution.py:304
  26.7 1.4 %collective-permute-start.11 = (bf16[64,4096]{1,0:T(8,128)(2,1)S(1)}, bf16[64,4096]{1,0:T(8,128)(2,1)S(1)}, u32[]{:S(2)}, u32[]{:S(2)}) collective-permute-start(bf16[64,4096]{1,0:T(8,128)(2,1)S(1)} %bitcast.87), channel_id=1, source_target_pairs={{0,2},{1,9},{2,4},{3,11},{4,6},{5,13},{6,0},{7,15},{8,10},{9,17},{... | collective-permute-start | bytes 1572872 | tf_op jit(solution)/shard_map/ppermute | solution.py:46
  28.0 1.5 %collective-permute-start.12 = (bf16[64,4096]{1,0:T(8,128)(2,1)S(1)}, bf16[64,4096]{1,0:T(8,128)(2,1)S(1)}, u32[]{:S(2)}, u32[]{:S(2)}) collective-permute-start(bf16[64,4096]{1,0:T(8,128)(2,1)S(1)} %bitcast.88), channel_id=1, source_target_pairs={{0,6},{1,25},{2,0},{3,27},{4,2},{5,29},{6,4},{7,31},{8,14},{9,1},{... | collective-permute-start | bytes 1572872 | tf_op jit(solution)/shard_map/ppermute | solution.py:46
  29.5 1.6 %collective-permute-start.13 = (bf16[64,4096]{1,0:T(8,128)(2,1)S(1)}, bf16[64,4096]{1,0:T(8,128)(2,1)S(1)}, u32[]{:S(2)}, u32[]{:S(2)}) collective-permute-start(bf16[64,4096]{1,0:T(8,128)(2,1)S(1)} %bitcast.89), channel_id=1, source_target_pairs={{0,4},{1,17},{2,6},{3,19},{4,0},{5,21},{6,2},{7,23},{8,12},{9,25},... | collective-permute-start | bytes 1572872 | tf_op jit(solution)/shard_map/ppermute | solution.py:46
  31.1 3.4 %load_columns.2.tokens = bf16[1024,4096]{1,0:T(8,128)(2,1)S(1)} custom-call(s32[1]{0:T(128)} %bitcast.22.start_ref, bf16[1024,8192]{1,0:T(8,128)(2,1)} %bitcast.98, bf16[64,4096]{1,0:T(8,128)(2,1)S(1)} %bitcast.90), custom_call_target="tpu_custom_call" | custom-call | tf_op jit(solution)/shard_map/load_columns/pallas_call | solution.py:137
  34.5 0.2 broadcast_in_dim.35
  34.8 2.3 %collective-permute-start.6 = (f32[2,2,8,4096]{3,2,0,1:T(8,128)S(1)}, f32[2,2,8,4096]{3,2,0,1:T(8,128)S(1)}, u32[]{:S(2)}, u32[]{:S(2)}) collective-permute-start(f32[2,2,8,4096]{3,2,0,1:T(8,128)S(1)} %pad_maximum_fusion), channel_id=1, source_target_pairs={{0,96},{32,64},{64,32},{96,0},{1,97},{33,65},{65,33},{97,1},{2,98}... | collective-permute-start | bytes 1572872 | tf_op jit(solution)/shard_map/ppermute | solution.py:307
  37.3 4.0 %collective-permute-done.12 = bf16[64,4096]{1,0:T(8,128)(2,1)S(1)} collective-permute-done((bf16[64,4096]{1,0:T(8,128)(2,1)S(1)}, bf16[64,4096]{1,0:T(8,128)(2,1)S(1)}, u32[]{:S(2)}, u32[]{:S(2)}) %collective-permute-start.12) | collective-permute-done | bytes 524320 | tf_op jit(solution)/shard_map/ppermute | solution.py:46
  41.3 1.8 %collective-permute-done.13 = bf16[64,4096]{1,0:T(8,128)(2,1)S(1)} collective-permute-done((bf16[64,4096]{1,0:T(8,128)(2,1)S(1)}, bf16[64,4096]{1,0:T(8,128)(2,1)S(1)}, u32[]{:S(2)}, u32[]{:S(2)}) %collective-permute-start.13) | collective-permute-done | bytes 524320 | tf_op jit(solution)/shard_map/ppermute | solution.py:46
  43.2 0.2 fusion.9
  43.4 1.0 collective-permute-start.16
  44.3 1.8 %collective-permute-start.14 = (bf16[256,2048]{1,0:T(8,128)(2,1)S(1)}, bf16[256,2048]{1,0:T(8,128)(2,1)S(1)}, u32[]{:S(2)}, u32[]{:S(2)}) collective-permute-start(bf16[256,2048]{1,0:T(8,128)(2,1)S(1)} %get-tuple-element.15.refs_0_), channel_id=1, source_target_pairs={{0,24},{1,7},{2,26},{3,1},{4,28},{5,3},{6,30},{7,5},{8,0},{9,15},{... | collective-permute-start | bytes 3145736 | tf_op jit(solution)/shard_map/ppermute | solution.py:46
  46.1 0.3 broadcast_in_dim.33
  46.4 2.4 %partial_sums.9 = bf16[2,4,1024,256]{3,2,1,0:T(8,128)(2,1)S(1)} fusion(bf16[2,4,1024,256]{3,2,1,0:T(8,128)(2,1)S(1)} %broadcast_in_dim.33, s32[]{:T(128)S(6)} %select_n.263, s32[]{:T(128)S(6)} %select_n.279, bf16[1024,4096]{1,0:T(8,128)(2,1)S(1)} %load_columns.2.tokens, bf16[256,2048]{1,0:T(8,128)(2,1)S(1)} %get-tuple-element.15.refs_0_, ...), kind=kCustom, calls=%fused_computation.21 | custom fusion | flops 2147483648 | bytes 11010056 | tf_op jit(solution)/shard_map/partial_sums/pallas_call | solution.py:170
  48.8 2.8 %collective-permute-start.15 = (bf16[256,2048]{1,0:T(8,128)(2,1)S(1)}, bf16[256,2048]{1,0:T(8,128)(2,1)S(1)}, u32[]{:S(2)}, u32[]{:S(2)}) collective-permute-start(bf16[256,2048]{1,0:T(8,128)(2,1)S(1)} %get-tuple-element.14.refs_1_), channel_id=1, source_target_pairs={{0,24},{1,7},{2,26},{3,1},{4,28},{5,3},{6,30},{7,5},{8,0},{9,15},{... | collective-permute-start | bytes 3145736 | tf_op jit(solution)/shard_map/ppermute | solution.py:46
  51.6 0.1 dynamic-slice_bitcast_fusion.1
  51.7 6.9 %collective-permute-done.16.refs_2_.refs_4_ = bf16[256,2048]{1,0:T(8,128)(2,1)S(1)} collective-permute-done((bf16[256,2048]{1,0:T(8,128)(2,1)S(1)}, bf16[256,2048]{1,0:T(8,128)(2,1)S(1)}, u32[]{:S(2)}, u32[]{:S(2)}) %collective-permute-start.16) | collective-permute-done | bytes 1048608 | tf_op jit(solution)/shard_map/ppermute | solution.py:46
  58.6 2.9 %collective-permute-start.7 = (f32[32,4096]{1,0:T(8,128)S(1)}, f32[32,4096]{1,0:T(8,128)S(1)}, u32[]{:S(2)}, u32[]{:S(2)}) collective-permute-start(f32[32,4096]{1,0:T(8,128)S(1)} %get-tuple-element.17), channel_id=1, source_target_pairs={{0,1},{1,0},{2,3},{3,2},{4,5},{5,4},{6,7},{7,6},{8,9},{9,8},{10,11... | collective-permute-start | bytes 1572872 | tf_op jit(solution)/shard_map/ppermute | solution.py:42
  61.5 8.3 %collective-permute-done.17.refs_3_.refs_5_ = bf16[256,2048]{1,0:T(8,128)(2,1)S(1)} collective-permute-done((bf16[256,2048]{1,0:T(8,128)(2,1)S(1)}, bf16[256,2048]{1,0:T(8,128)(2,1)S(1)}, u32[]{:S(2)}, u32[]{:S(2)}) %collective-permute-start.17) | collective-permute-done | bytes 1048608 | tf_op jit(solution)/shard_map/ppermute | solution.py:46
  69.8 6.7 %partial_sums.6 = bf16[3,1024,256]{2,1,0:T(8,128)(2,1)S(1)} custom-call(bf16[1024,4096]{1,0:T(8,128)(2,1)S(1)} %collective-permute-done.18.tokens, bf16[256,2048]{1,0:T(8,128)(2,1)S(1)} %get-tuple-element.15.refs_0_, bf16[256,2048]{1,0:T(8,128)(2,1)S(1)} %get-tuple-element.14.refs_1_, bf16[256,2048]{1,0:T(8,128)(2,1)S(1)} %collective-permute-done.14.refs_0_.refs_2_, ...), custom_call_target="tpu_custom_call" | custom-call | flops 6442450944 | bytes 14680064 | tf_op jit(solution)/shard_map/partial_sums/pallas_call | solution.py:170
  76.5 3.3 %collective-permute-start.19 = (bf16[3,1024,256]{2,1,0:T(8,128)(2,1)S(1)}, bf16[3,1024,256]{2,1,0:T(8,128)(2,1)S(1)}, u32[]{:S(2)}, u32[]{:S(2)}) collective-permute-start(bf16[3,1024,256]{2,1,0:T(8,128)(2,1)S(1)} %partial_sums.6), channel_id=1, source_target_pairs={{0,1},{1,0},{2,3},{3,2},{4,5},{5,4},{6,7},{7,6},{8,9},{9,8},{10,11... | collective-permute-start | bytes 4718600 | tf_op jit(solution)/shard_map/ppermute | solution.py:42
  79.9 0.1 maximum_select_fusion.outer_grad
  80.0 4.0 %update.1 = (f32[32,8192]{1,0:T(8,128)}, f32[32,8192]{1,0:T(8,128)}, bf16[32,8192]{1,0:T(8,128)(2,1)}) custom-call(f32[32,8192]{1,0:T(8,128)} %anchor.1, f32[32,8192]{1,0:T(8,128)} %momentum.1, bf16[32,8192]{1,0:T(8,128)(2,1)} %bitcast.101, f32[32,8192]{1,0:T(8,128)S(1)} %maximum_select_fusion.outer_grad), custom_call_target="tpu_custom_call" | custom-call | tf_op jit(solution)/shard_map/update/pallas_call | solution.py:116
  84.0 1.2 %collective-permute-start.20 = (bf16[256,1024]{1,0:T(8,128)(2,1)S(1)}, bf16[256,1024]{1,0:T(8,128)(2,1)S(1)}, u32[]{:S(2)}, u32[]{:S(2)}) collective-permute-start(bf16[256,1024]{1,0:T(8,128)(2,1)S(1)} %slice.63), channel_id=1, source_target_pairs={{0,8},{1,3},{2,10},{3,5},{4,12},{5,7},{6,14},{7,1},{8,16},{9,11},{... | collective-permute-start | bytes 1572872 | tf_op jit(solution)/shard_map/ppermute | solution.py:46
  85.3 1.6 %collective-permute-start.21 = (bf16[256,1024]{1,0:T(8,128)(2,1)S(1)}, bf16[256,1024]{1,0:T(8,128)(2,1)S(1)}, u32[]{:S(2)}, u32[]{:S(2)}) collective-permute-start(bf16[256,1024]{1,0:T(8,128)(2,1)S(1)} %slice.64), channel_id=1, source_target_pairs={{0,24},{1,7},{2,26},{3,1},{4,28},{5,3},{6,30},{7,5},{8,0},{9,15},{... | collective-permute-start | bytes 1572872 | tf_op jit(solution)/shard_map/ppermute | solution.py:46
  86.9 0.1 collective-permute-start.22
  87.1 3.0 %collective-permute-start.23 = (bf16[256,1024]{1,0:T(8,128)(2,1)S(1)}, bf16[256,1024]{1,0:T(8,128)(2,1)S(1)}, u32[]{:S(2)}, u32[]{:S(2)}) collective-permute-start(bf16[256,1024]{1,0:T(8,128)(2,1)S(1)} %slice.66), channel_id=1, source_target_pairs={{0,24},{1,7},{2,26},{3,1},{4,28},{5,3},{6,30},{7,5},{8,0},{9,15},{... | collective-permute-start | bytes 1572872 | tf_op jit(solution)/shard_map/ppermute | solution.py:46
  90.0 4.5 %partial_sums.5 = bf16[2,1024,256]{2,1,0:T(8,128)(2,1)S(1)} custom-call(bf16[1024,4096]{1,0:T(8,128)(2,1)S(1)} %load_columns.2.tokens, bf16[256,2048]{1,0:T(8,128)(2,1)S(1)} %collective-permute-done.14.refs_0_.refs_2_, bf16[256,2048]{1,0:T(8,128)(2,1)S(1)} %collective-permute-done.15.refs_1_.refs_3_, ...), custom_call_target="tpu_custom_call" | custom-call | flops 4294967296 | bytes 12582912 | tf_op jit(solution)/shard_map/partial_sums/pallas_call | solution.py:170
  94.7 4.6 %collective-permute-done.22.refs_2_ = bf16[256,1024]{1,0:T(8,128)(2,1)S(1)} collective-permute-done((bf16[256,1024]{1,0:T(8,128)(2,1)S(1)}, bf16[256,1024]{1,0:T(8,128)(2,1)S(1)}, u32[]{:S(2)}, u32[]{:S(2)}) %collective-permute-start.22) | collective-permute-done | bytes 524320 | tf_op jit(solution)/shard_map/ppermute | solution.py:46
  99.3 2.4 %partial_sums.7 = bf16[1,1024,256]{2,1,0:T(8,128)(2,1)S(1)} custom-call(bf16[1024,4096]{1,0:T(8,128)(2,1)S(1)} %collective-permute-done.18.tokens, bf16[256,1024]{1,0:T(8,128)(2,1)S(1)} %collective-permute-done.20.refs_0_, bf16[256,1024]{1,0:T(8,128)(2,1)S(1)} %collective-permute-done.21.refs_1_, bf16[256,1024]{1,0:T(8,128)(2,1)S(1)} %collective-permute-done.22.refs_2_, ...), custom_call_target="tpu_custom_call" | custom-call | flops 2147483648 | bytes 10485760 | tf_op jit(solution)/shard_map/partial_sums/pallas_call | solution.py:170
  101.7 1.4 %collective-permute-start.24 = (bf16[1,1024,256]{2,1,0:T(8,128)(2,1)S(1)}, bf16[1,1024,256]{2,1,0:T(8,128)(2,1)S(1)}, u32[]{:S(2)}, u32[]{:S(2)}) collective-permute-start(bf16[1,1024,256]{2,1,0:T(8,128)(2,1)S(1)} %partial_sums.7), channel_id=1, source_target_pairs={{0,1},{1,0},{2,3},{3,2},{4,5},{5,4},{6,7},{7,6},{8,9},{9,8},{10,11... | collective-permute-start | bytes 1572872 | tf_op jit(solution)/shard_map/ppermute | solution.py:42
  103.2 2.4 %partial_sums.8 = bf16[2,4,1024,256]{3,2,1,0:T(8,128)(2,1)S(1)} fusion(bf16[2,4,1024,256]{3,2,1,0:T(8,128)(2,1)S(1)} %fusion, s32[]{:T(128)S(6)} %select_n.263, s32[]{:T(128)S(6)} %select_n.289, bf16[1024,4096]{1,0:T(8,128)(2,1)S(1)} %load_columns.2.tokens, bf16[256,1024]{1,0:T(8,128)(2,1)S(1)} %collective-permute-done.20.refs_0_, ...), kind=kCustom, calls=%fused_computation.20 | custom fusion | flops 2147483648 | bytes 11010056 | tf_op jit(solution)/shard_map/partial_sums/pallas_call | solution.py:170
  105.6 2.4 %combine.1 = bf16[1024,1024]{1,0:T(8,128)(2,1)} custom-call(bf16[2,4,1024,256]{3,2,1,0:T(8,128)(2,1)S(1)} %bitcast_dynamic-update-slice_fusion.held), custom_call_target="tpu_custom_call" | custom-call | tf_op jit(solution)/shard_map/combine/pallas_call | solution.py:205
  (55 shorter events, 1.3 us)
Async XLA Ops:
  1.7 3.1 %collective-permute-start.1 = (bf16[32,4096]{1,0:T(8,128)(2,1)S(1)}, bf16[32,4096]{1,0:T(8,128)(2,1)S(1)}, u32[]{:S(2)}, u32[]{:S(2)}) collective-permute-start(bf16[32,4096]{1,0:T(8,128)(2,1)S(1)} %get-tuple-element.25), channel_id=1, source_target_pairs={{0,1},{1,0},{2,3},{3,2},{4,5},{5,4},{6,7},{7,6},{8,9},{9,8},{10,11... | collective-permute-start | bytes 786440 | tf_op jit(solution)/shard_map/ppermute | solution.py:42
  4.3 5.8 %collective-permute-start = (f32[16,4096]{1,0:T(8,128)S(1)}, f32[16,4096]{1,0:T(8,128)S(1)}, u32[]{:S(2)}, u32[]{:S(2)}) collective-permute-start(f32[16,4096]{1,0:T(8,128)S(1)} %get-tuple-element.29), channel_id=1, source_target_pairs={{0,1},{1,0},{2,3},{3,2},{4,5},{5,4},{6,7},{7,6},{8,9},{9,8},{10,11... | collective-permute-start | bytes 786440 | tf_op jit(solution)/shard_map/ppermute | solution.py:42
  4.9 7.7 %collective-permute-start.2 = (bf16[1,2,8,4096]{3,2,1,0:T(8,128)(2,1)S(1)}, bf16[1,2,8,4096]{3,2,1,0:T(8,128)(2,1)S(1)}, u32[]{:S(2)}, u32[]{:S(2)}) collective-permute-start(bf16[1,2,8,4096]{3,2,1,0:T(8,128)(2,1)S(1)} %get-tuple-element.23), channel_id=1, source_target_pairs={{0,32},{32,64},{64,96},{96,0},{1,33},{33,65},{65,97},{97,1},{2,34}... | collective-permute-start | bytes 393224 | tf_op jit(solution)/shard_map/ppermute | solution.py:50
  6.7 5.9 %collective-permute-start.3 = (bf16[1,2,8,4096]{3,2,1,0:T(8,128)(2,1)S(1)}, bf16[1,2,8,4096]{3,2,1,0:T(8,128)(2,1)S(1)}, u32[]{:S(2)}, u32[]{:S(2)}) collective-permute-start(bf16[1,2,8,4096]{3,2,1,0:T(8,128)(2,1)S(1)} %get-tuple-element.22), channel_id=1, source_target_pairs={{0,96},{32,0},{64,32},{96,64},{1,97},{33,1},{65,33},{97,65},{2,98}... | collective-permute-start | bytes 393224 | tf_op jit(solution)/shard_map/ppermute | solution.py:50
  8.9 7.5 %collective-permute-start.4 = (bf16[1,2,8,4096]{3,2,1,0:T(8,128)(2,1)S(1)}, bf16[1,2,8,4096]{3,2,1,0:T(8,128)(2,1)S(1)}, u32[]{:S(2)}, u32[]{:S(2)}) collective-permute-start(bf16[1,2,8,4096]{3,2,1,0:T(8,128)(2,1)S(1)} %get-tuple-element.21), channel_id=1, source_target_pairs={{0,64},{32,96},{64,0},{96,32},{1,65},{33,97},{65,1},{97,33},{2,66}... | collective-permute-start | bytes 393224 | tf_op jit(solution)/shard_map/ppermute | solution.py:50
  17.5 9.1 %collective-permute-start.8 = (bf16[1,2,8,4096]{3,2,1,0:T(8,128)(2,1)S(1)}, bf16[1,2,8,4096]{3,2,1,0:T(8,128)(2,1)S(1)}, u32[]{:S(2)}, u32[]{:S(2)}) collective-permute-start(bf16[1,2,8,4096]{3,2,1,0:T(8,128)(2,1)S(1)} %get-tuple-element.20), channel_id=1, source_target_pairs={{0,32},{32,64},{64,96},{96,0},{1,33},{33,65},{65,97},{97,1},{2,34}... | collective-permute-start | bytes 393224 | tf_op jit(solution)/shard_map/ppermute | solution.py:50
  18.1 8.5 %collective-permute-start.9 = (bf16[1,2,8,4096]{3,2,1,0:T(8,128)(2,1)S(1)}, bf16[1,2,8,4096]{3,2,1,0:T(8,128)(2,1)S(1)}, u32[]{:S(2)}, u32[]{:S(2)}) collective-permute-start(bf16[1,2,8,4096]{3,2,1,0:T(8,128)(2,1)S(1)} %get-tuple-element.19), channel_id=1, source_target_pairs={{0,96},{32,0},{64,32},{96,64},{1,97},{33,1},{65,33},{97,65},{2,98}... | collective-permute-start | bytes 393224 | tf_op jit(solution)/shard_map/ppermute | solution.py:50
  20.2 6.4 %collective-permute-start.10 = (bf16[1,2,8,4096]{3,2,1,0:T(8,128)(2,1)S(1)}, bf16[1,2,8,4096]{3,2,1,0:T(8,128)(2,1)S(1)}, u32[]{:S(2)}, u32[]{:S(2)}) collective-permute-start(bf16[1,2,8,4096]{3,2,1,0:T(8,128)(2,1)S(1)} %get-tuple-element.18), channel_id=1, source_target_pairs={{0,64},{32,96},{64,0},{96,32},{1,65},{33,97},{65,1},{97,33},{2,66}... | collective-permute-start | bytes 393224 | tf_op jit(solution)/shard_map/ppermute | solution.py:50
  23.7 46.1 %collective-permute-start.18 = (bf16[1024,4096]{1,0:T(8,128)(2,1)S(1)}, bf16[1024,4096]{1,0:T(8,128)(2,1)S(1)}, u32[]{:S(2)}, u32[]{:S(2)}) collective-permute-start(bf16[1024,4096]{1,0:T(8,128)(2,1)S(1)} %load_columns.3), channel_id=1, source_target_pairs={{0,1},{1,0},{2,3},{3,2},{4,5},{5,4},{6,7},{7,6},{8,9},{9,8},{10,11... | collective-permute-start | bytes 25165832 | tf_op jit(solution)/shard_map/ppermute | solution.py:42
  25.2 9.6 %collective-permute-start.5 = (f32[1,2,8,4096]{3,2,0,1:T(8,128)S(1)}, f32[1,2,8,4096]{3,2,0,1:T(8,128)S(1)}, u32[]{:S(2)}, u32[]{:S(2)}) collective-permute-start(f32[1,2,8,4096]{3,2,0,1:T(8,128)S(1)} %bitcast.93), channel_id=1, source_target_pairs={{0,32},{32,0},{64,96},{96,64},{1,33},{33,1},{65,97},{97,65},{2,34}... | collective-permute-start | bytes 786440 | tf_op jit(solution)/shard_map/ppermute | solution.py:304
  26.7 10.6 %collective-permute-start.11 = (bf16[64,4096]{1,0:T(8,128)(2,1)S(1)}, bf16[64,4096]{1,0:T(8,128)(2,1)S(1)}, u32[]{:S(2)}, u32[]{:S(2)}) collective-permute-start(bf16[64,4096]{1,0:T(8,128)(2,1)S(1)} %bitcast.87), channel_id=1, source_target_pairs={{0,2},{1,9},{2,4},{3,11},{4,6},{5,13},{6,0},{7,15},{8,10},{9,17},{... | collective-permute-start | bytes 1572872 | tf_op jit(solution)/shard_map/ppermute | solution.py:46
  28.0 13.3 %collective-permute-start.12 = (bf16[64,4096]{1,0:T(8,128)(2,1)S(1)}, bf16[64,4096]{1,0:T(8,128)(2,1)S(1)}, u32[]{:S(2)}, u32[]{:S(2)}) collective-permute-start(bf16[64,4096]{1,0:T(8,128)(2,1)S(1)} %bitcast.88), channel_id=1, source_target_pairs={{0,6},{1,25},{2,0},{3,27},{4,2},{5,29},{6,4},{7,31},{8,14},{9,1},{... | collective-permute-start | bytes 1572872 | tf_op jit(solution)/shard_map/ppermute | solution.py:46
  29.5 13.6 %collective-permute-start.13 = (bf16[64,4096]{1,0:T(8,128)(2,1)S(1)}, bf16[64,4096]{1,0:T(8,128)(2,1)S(1)}, u32[]{:S(2)}, u32[]{:S(2)}) collective-permute-start(bf16[64,4096]{1,0:T(8,128)(2,1)S(1)} %bitcast.89), channel_id=1, source_target_pairs={{0,4},{1,17},{2,6},{3,19},{4,0},{5,21},{6,2},{7,23},{8,12},{9,25},... | collective-permute-start | bytes 1572872 | tf_op jit(solution)/shard_map/ppermute | solution.py:46
  34.8 13.9 %collective-permute-start.6 = (f32[2,2,8,4096]{3,2,0,1:T(8,128)S(1)}, f32[2,2,8,4096]{3,2,0,1:T(8,128)S(1)}, u32[]{:S(2)}, u32[]{:S(2)}) collective-permute-start(f32[2,2,8,4096]{3,2,0,1:T(8,128)S(1)} %pad_maximum_fusion), channel_id=1, source_target_pairs={{0,96},{32,64},{64,32},{96,0},{1,97},{33,65},{65,33},{97,1},{2,98}... | collective-permute-start | bytes 1572872 | tf_op jit(solution)/shard_map/ppermute | solution.py:307
  43.4 15.2 %collective-permute-start.16 = (bf16[256,2048]{1,0:T(8,128)(2,1)S(1)}, bf16[256,2048]{1,0:T(8,128)(2,1)S(1)}, u32[]{:S(2)}, u32[]{:S(2)}) collective-permute-start(bf16[256,2048]{1,0:T(8,128)(2,1)S(1)} %get-tuple-element.15.refs_0_), channel_id=1, source_target_pairs={{0,8},{1,3},{2,10},{3,5},{4,12},{5,7},{6,14},{7,1},{8,16},{9,11},{... | collective-permute-start | bytes 3145736 | tf_op jit(solution)/shard_map/ppermute | solution.py:46
  44.3 17.2 %collective-permute-start.14 = (bf16[256,2048]{1,0:T(8,128)(2,1)S(1)}, bf16[256,2048]{1,0:T(8,128)(2,1)S(1)}, u32[]{:S(2)}, u32[]{:S(2)}) collective-permute-start(bf16[256,2048]{1,0:T(8,128)(2,1)S(1)} %get-tuple-element.15.refs_0_), channel_id=1, source_target_pairs={{0,24},{1,7},{2,26},{3,1},{4,28},{5,3},{6,30},{7,5},{8,0},{9,15},{... | collective-permute-start | bytes 3145736 | tf_op jit(solution)/shard_map/ppermute | solution.py:46
  46.1 23.7 %collective-permute-start.17 = (bf16[256,2048]{1,0:T(8,128)(2,1)S(1)}, bf16[256,2048]{1,0:T(8,128)(2,1)S(1)}, u32[]{:S(2)}, u32[]{:S(2)}) collective-permute-start(bf16[256,2048]{1,0:T(8,128)(2,1)S(1)} %get-tuple-element.14.refs_1_), channel_id=1, source_target_pairs={{0,8},{1,3},{2,10},{3,5},{4,12},{5,7},{6,14},{7,1},{8,16},{9,11},{... | collective-permute-start | bytes 3145736 | tf_op jit(solution)/shard_map/ppermute | solution.py:46
  48.8 21.1 %collective-permute-start.15 = (bf16[256,2048]{1,0:T(8,128)(2,1)S(1)}, bf16[256,2048]{1,0:T(8,128)(2,1)S(1)}, u32[]{:S(2)}, u32[]{:S(2)}) collective-permute-start(bf16[256,2048]{1,0:T(8,128)(2,1)S(1)} %get-tuple-element.14.refs_1_), channel_id=1, source_target_pairs={{0,24},{1,7},{2,26},{3,1},{4,28},{5,3},{6,30},{7,5},{8,0},{9,15},{... | collective-permute-start | bytes 3145736 | tf_op jit(solution)/shard_map/ppermute | solution.py:46
  58.6 21.3 %collective-permute-start.7 = (f32[32,4096]{1,0:T(8,128)S(1)}, f32[32,4096]{1,0:T(8,128)S(1)}, u32[]{:S(2)}, u32[]{:S(2)}) collective-permute-start(f32[32,4096]{1,0:T(8,128)S(1)} %get-tuple-element.17), channel_id=1, source_target_pairs={{0,1},{1,0},{2,3},{3,2},{4,5},{5,4},{6,7},{7,6},{8,9},{9,8},{10,11... | collective-permute-start | bytes 1572872 | tf_op jit(solution)/shard_map/ppermute | solution.py:42
  76.5 26.6 %collective-permute-start.19 = (bf16[3,1024,256]{2,1,0:T(8,128)(2,1)S(1)}, bf16[3,1024,256]{2,1,0:T(8,128)(2,1)S(1)}, u32[]{:S(2)}, u32[]{:S(2)}) collective-permute-start(bf16[3,1024,256]{2,1,0:T(8,128)(2,1)S(1)} %partial_sums.6), channel_id=1, source_target_pairs={{0,1},{1,0},{2,3},{3,2},{4,5},{5,4},{6,7},{7,6},{8,9},{9,8},{10,11... | collective-permute-start | bytes 4718600 | tf_op jit(solution)/shard_map/ppermute | solution.py:42
  84.0 10.6 %collective-permute-start.20 = (bf16[256,1024]{1,0:T(8,128)(2,1)S(1)}, bf16[256,1024]{1,0:T(8,128)(2,1)S(1)}, u32[]{:S(2)}, u32[]{:S(2)}) collective-permute-start(bf16[256,1024]{1,0:T(8,128)(2,1)S(1)} %slice.63), channel_id=1, source_target_pairs={{0,8},{1,3},{2,10},{3,5},{4,12},{5,7},{6,14},{7,1},{8,16},{9,11},{... | collective-permute-start | bytes 1572872 | tf_op jit(solution)/shard_map/ppermute | solution.py:46
  85.3 9.4 %collective-permute-start.21 = (bf16[256,1024]{1,0:T(8,128)(2,1)S(1)}, bf16[256,1024]{1,0:T(8,128)(2,1)S(1)}, u32[]{:S(2)}, u32[]{:S(2)}) collective-permute-start(bf16[256,1024]{1,0:T(8,128)(2,1)S(1)} %slice.64), channel_id=1, source_target_pairs={{0,24},{1,7},{2,26},{3,1},{4,28},{5,3},{6,30},{7,5},{8,0},{9,15},{... | collective-permute-start | bytes 1572872 | tf_op jit(solution)/shard_map/ppermute | solution.py:46
  86.9 12.3 %collective-permute-start.22 = (bf16[256,1024]{1,0:T(8,128)(2,1)S(1)}, bf16[256,1024]{1,0:T(8,128)(2,1)S(1)}, u32[]{:S(2)}, u32[]{:S(2)}) collective-permute-start(bf16[256,1024]{1,0:T(8,128)(2,1)S(1)} %slice.65), channel_id=1, source_target_pairs={{0,8},{1,3},{2,10},{3,5},{4,12},{5,7},{6,14},{7,1},{8,16},{9,11},{... | collective-permute-start | bytes 1572872 | tf_op jit(solution)/shard_map/ppermute | solution.py:46
  87.1 12.2 %collective-permute-start.23 = (bf16[256,1024]{1,0:T(8,128)(2,1)S(1)}, bf16[256,1024]{1,0:T(8,128)(2,1)S(1)}, u32[]{:S(2)}, u32[]{:S(2)}) collective-permute-start(bf16[256,1024]{1,0:T(8,128)(2,1)S(1)} %slice.66), channel_id=1, source_target_pairs={{0,24},{1,7},{2,26},{3,1},{4,28},{5,3},{6,30},{7,5},{8,0},{9,15},{... | collective-permute-start | bytes 1572872 | tf_op jit(solution)/shard_map/ppermute | solution.py:46
  101.7 3.9 %collective-permute-start.24 = (bf16[1,1024,256]{2,1,0:T(8,128)(2,1)S(1)}, bf16[1,1024,256]{2,1,0:T(8,128)(2,1)S(1)}, u32[]{:S(2)}, u32[]{:S(2)}) collective-permute-start(bf16[1,1024,256]{2,1,0:T(8,128)(2,1)S(1)} %partial_sums.7), channel_id=1, source_target_pairs={{0,1},{1,0},{2,3},{3,2},{4,5},{5,4},{6,7},{7,6},{8,9},{9,8},{10,11... | collective-permute-start | bytes 1572872 | tf_op jit(solution)/shard_map/ppermute | solution.py:42

commit v3 on v2

--- a/solution.py
+++ b/solution.py
@@ -12,6 +12,7 @@
 CHUNKS = 2
 MERGE_COLS = 512
 UPDATE_COLS = 2048
+CHEAP = pl.CostEstimate(flops=1024, bytes_accessed=1024, transcendentals=0)
 MIB = 1024 * 1024
 
 
@@ -96,6 +97,7 @@
             jax.ShapeDtypeStruct(gathered.shape, jnp.bfloat16),
         ],
         compiler_params=pltpu.CompilerParams(vmem_limit_bytes=8 * MIB),
+        cost_estimate=CHEAP,
         name="merge",
     )(in_vmem(anchor), in_vmem(momentum), in_vmem(gathered))
 
@@ -120,35 +122,37 @@
         out_specs=[tile] * 3,
         out_shape=[wide, wide, jax.ShapeDtypeStruct((rows, width), jnp.bfloat16)],
         compiler_params=pltpu.CompilerParams(vmem_limit_bytes=12 * MIB),
+        cost_estimate=CHEAP,
         name="update",
     )(in_hbm(anchor), in_hbm(momentum), in_hbm(local), outer_grad)
 
 
-def load_body(start_ref, tokens, *refs):
+def load_body(entry, place, tokens, *refs):
     half, sem = refs[-2:]
-    start = pl.multiple_of(start_ref[0], half.shape[1])
+    start = pl.multiple_of(place[entry], half.shape[1])
     copy = pltpu.make_async_copy(tokens.at[:, pl.ds(start, half.shape[1])], half, sem)
     copy.start()
     copy.wait()
 
 
-def load_columns(start, tokens, width, *earlier):
+def load_columns(place, entry, tokens, width, *earlier):
     anywhere = pl.BlockSpec(memory_space=pl.ANY)
     return pl.pallas_call(
-        load_body,
+        functools.partial(load_body, entry),
         in_specs=[pl.BlockSpec(memory_space=pltpu.SMEM), pl.BlockSpec(memory_space=pltpu.HBM)]
         + [anywhere] * len(earlier),
         out_specs=pl.BlockSpec(memory_space=pltpu.VMEM),
         out_shape=pltpu.VMEM((tokens.shape[0], width), tokens.dtype),
         scratch_shapes=[pltpu.SemaphoreType.DMA(())],
-        compiler_params=pltpu.CompilerParams(vmem_limit_bytes=2 * MIB),
+        compiler_params=pltpu.CompilerParams(vmem_limit_bytes=9 * MIB),
+        cost_estimate=CHEAP,
         name="load_columns",
-    )(start.astype(jnp.int32).reshape(1), in_hbm(tokens), *earlier)
-
-
-def partial_body(per_block, tokens, *refs):
-    weights, out = refs[:-1], refs[-1]
-    for block in range(out.shape[0]):
+    )(place, in_hbm(tokens), *earlier)
+
+
+def partial_body(per_block, first, count, tokens, *refs):
+    weights, out = refs[: count * per_block], refs[-1]
+    for block in range(count):
         start, total = 0, None
         for piece in weights[block * per_block : (block + 1) * per_block]:
             term = lax.dot_general(
@@ -159,58 +163,86 @@
             )
             total = term if total is None else total + term
             start += piece.shape[1]
-        out[block] = total.astype(out.dtype)
-
-
-def partial_sums(tokens, weights):
+        out[first + block] = total.astype(out.dtype)
+
+
+def partial_sums(tokens, weights, size=None, filled=None, earlier=(), cost=CHEAP):
     count, half = tokens.shape
     blocks, per_block = len(weights), len(weights[0])
     units = weights[0][0].shape[0]
+    size = size or blocks
     vmem = pl.BlockSpec(memory_space=pltpu.VMEM)
-    return pl.pallas_call(
-        functools.partial(partial_body, per_block),
-        in_specs=[vmem] * (1 + blocks * per_block),
+    anywhere = pl.BlockSpec(memory_space=pl.ANY)
+    more = list(earlier) if filled is None else [*earlier, filled]
+    operands = 1 + blocks * per_block
+    return pl.pallas_call(
+        functools.partial(partial_body, per_block, 0 if filled is None else size - blocks, blocks),
+        in_specs=[vmem] * operands + [anywhere] * len(earlier) + ([] if filled is None else [vmem]),
         out_specs=vmem,
-        out_shape=jax.ShapeDtypeStruct((blocks, count, units), jnp.bfloat16),
-        compiler_params=pltpu.CompilerParams(vmem_limit_bytes=16 * MIB),
-        cost_estimate=pl.CostEstimate(
-            flops=2 * count * units * blocks * half,
-            bytes_accessed=2 * (count + units * blocks) * half,
-            transcendentals=0,
-        ),
+        out_shape=jax.ShapeDtypeStruct((size, count, units), jnp.bfloat16),
+        input_output_aliases={} if filled is None else {operands + len(earlier): 0},
+        compiler_params=pltpu.CompilerParams(vmem_limit_bytes=12 * MIB),
+        cost_estimate=cost,
         name="partial_sums",
-    )(in_vmem(tokens), *[in_vmem(piece) for block in weights for piece in block])
+    )(in_vmem(tokens), *[in_vmem(piece) for block in weights for piece in block], *more)
 
 
 COMBINE_ROWS = 256
 
 
-def combine_body(held, out):
-    rows = pl.ds(pl.multiple_of(pl.program_id(0) * COMBINE_ROWS, COMBINE_ROWS), COMBINE_ROWS)
+def combine_body(place, own_first, own_mid, own_last, got_first, got_mid, got_last, out, held):
+    core = place[0]
+    for side, base, first, mid, last in (
+        (core, place[1], own_first, own_mid, own_last),
+        (1 - core, place[2], got_first, got_mid, got_last),
+    ):
+        for step, source in ((0, first[0]), (1, mid[0]), (3, mid[1]), (2, last[0])):
+            held[side, lax.rem(base + step, SIDE)] = source
     low = lax.broadcasted_iota(jnp.int32, (COMBINE_ROWS, BLOCK), 1) < BLOCK // 2
     for x in (0, 2):
         for k in range(SIDE // 2):
             cols = slice(k * BLOCK, (k + 1) * BLOCK)
-            left = held[1, x, rows, cols].astype(jnp.float32)
-            right = held[1, x + 1, rows, cols].astype(jnp.float32)
+            left = held[1, x, :, cols].astype(jnp.float32)
+            right = held[1, x + 1, :, cols].astype(jnp.float32)
             crossed = pltpu.roll(jnp.where(low, right, left), BLOCK // 2, 1)
             for y, term in ((2 * k, jnp.where(low, left, crossed)), (2 * k + 1, jnp.where(low, crossed, right))):
-                natural = held[0, y, rows, slice(x // 2 * BLOCK, (x // 2 + 1) * BLOCK)].astype(jnp.float32)
+                natural = held[0, y, :, slice(x // 2 * BLOCK, (x // 2 + 1) * BLOCK)].astype(jnp.float32)
                 start = (2 * y + x // 2) * BLOCK
                 out[:, start : start + BLOCK] = (natural + term).astype(out.dtype)
 
 
-def combine(held):
-    _, _, count, units = held.shape
+def combine(place, *sums):
+    _, count, units = sums[0].shape
     return pl.pallas_call(
         combine_body,
         grid=(count // COMBINE_ROWS,),
-        in_specs=[pl.BlockSpec(memory_space=pltpu.VMEM)],
+        in_specs=[pl.BlockSpec(memory_space=pltpu.SMEM)] + [pl.BlockSpec((value.shape[0], COMBINE_ROWS, units), lambda i: (0, i, 0)) for value in sums],
         out_specs=pl.BlockSpec((COMBINE_ROWS, units * SIDE), lambda i: (i, 0)),
         out_shape=jax.ShapeDtypeStruct((count, units * SIDE), jnp.bfloat16),
-        compiler_params=pltpu.CompilerParams(vmem_limit_bytes=12 * MIB),
+        scratch_shapes=[pltpu.VMEM((2, SIDE, COMBINE_ROWS, units), jnp.bfloat16)],
+        compiler_params=pltpu.CompilerParams(vmem_limit_bytes=6 * MIB),
+        cost_estimate=CHEAP,
         name="combine",
-    )(held)
+    )(place, *sums)
+
+
+def follow_body(*refs):
+    pass
+
+
+def follow(values, *earlier):
+    vmem = pl.BlockSpec(memory_space=pltpu.VMEM)
+    anywhere = pl.BlockSpec(memory_space=pl.ANY)
+    return pl.pallas_call(
+        follow_body,
+        in_specs=[vmem] * len(values) + [anywhere] * len(earlier),
+        out_specs=[vmem] * len(values),
+        out_shape=[pltpu.VMEM(value.shape, value.dtype) for value in values],
+        input_output_aliases={i: i for i in range(len(values))},
+        compiler_params=pltpu.CompilerParams(vmem_limit_bytes=4 * MIB),
+        cost_estimate=CHEAP,
+        name="follow",
+    )(*[in_vmem(value) for value in values], *earlier)
 
 
 def on_device(anchor, momentum, local_weights, tokens):
@@ -230,6 +262,7 @@
     share = rows // SIDE
     mine, other = core * half, (1 - core) * half
     row = replica * share
+    place = jnp.stack([core, second_base, first_base, mine, other]).astype(jnp.int32)
 
     def both_cores(own, got):
         return jnp.where(core == 0, jnp.stack([own, got]), jnp.stack([got, own]))
@@ -254,17 +287,23 @@
 
     gathered = jnp.zeros_like(local_pair)
     received = exchange(local_pair)
-    mate_half = to_mate(load_columns(other, batch, half, received[1][1], own_anchor))
+    mate_half = to_mate(load_columns(place, 4, batch, half, received[1][1], own_anchor))
     for step, piece in received:
         gathered = lax.dynamic_update_slice(gathered, piece, ((replica - step) % SIDE, 0, 0, 0))
     gathered = gathered.reshape(SIDE * 2 * share, half)
     outer_part, merged_parts = merge(own_anchor, own_momentum, gathered)
+    outer_part = outer_part.reshape(2, share, half)
+    own_part, mate_part = (lax.dynamic_slice(outer_part, (which, 0, 0), (1, share, half))[0] for which in (core, 1 - core))
+    mate_part = to_mate(mate_part)
+    outer_part = jnp.where(
+        core == 0, jnp.concatenate([own_part, mate_part], axis=1), jnp.concatenate([mate_part, own_part], axis=1)
+    )
     pair = jnp.zeros((2, SIDE, share, half), jnp.bfloat16)
     for step, piece in exchange(merged_parts.reshape(SIDE, 2, share, half)):
         pair = lax.dynamic_update_slice(pair, piece.reshape(2, 1, share, half), (0, (replica - step) % SIDE, 0, 0))
     pair = pair.reshape(2 * rows, half)
 
-    own_half = load_columns(mine, batch, half, pair)
+    own_half = load_columns(place, 3, batch, half, pair)
     block = jnp.zeros((SIDE, 2 * rows, half), jnp.bfloat16)
     pieces = [pair] + [to_ring(pair, step, False) for step in (1, 3, 2)]
     for step, piece in zip((0, 1, 3, 2), pieces):
@@ -273,49 +312,35 @@
     blocks = []
     for c in range(CHUNKS):
         block = whole[:, c * part : (c + 1) * part]
-        before = to_ring(block, 1, True)
-        following = to_ring(block, SIDE - 1, True)
-        low = to_ring(before[:, : part // 2], 1, True)
-        high = to_ring(following[:, part // 2 :], SIDE - 1, True)
-        blocks.append((block, following, before, low, high))
-
+        blocks.append((block, to_ring(block, SIDE - 1, True), to_ring(block, 1, True)))
+
+    outer_grad = jnp.zeros((rows, width), jnp.float32)
+    outer_grad = lax.dynamic_update_slice(outer_grad, outer_part, (row, 0))
+    neighbour = lax.ppermute(outer_part, "replica", [(i, i ^ 1) for i in range(SIDE)])
+    outer_grad = lax.dynamic_update_slice(outer_grad, neighbour, ((replica ^ 1) * share, 0))
+    both = jnp.concatenate([outer_part, neighbour])
+    opposite = lax.ppermute(both, "replica", [(i, i ^ 3) for i in range(SIDE)])
+    outer_grad = lax.dynamic_update_slice(outer_grad, opposite[:share], ((replica ^ 3) * share, 0))
+    outer_grad = lax.dynamic_update_slice(outer_grad, opposite[share:], ((replica ^ 2) * share, 0))
+    new_anchor, new_momentum, merged = update(anchor, momentum, local, outer_grad)
     first = [[b[0] for b in blocks]]
     middle = [[b[1] for b in blocks], [b[2] for b in blocks]]
-    last = [[piece for b in blocks for piece in b[3:]]]
-    held = jnp.zeros((2, SIDE, tokens.shape[1], rows * 2 * SIDE), jnp.bfloat16)
-
-    def place(held, which, base, steps, sums):
-        for i, step in enumerate(steps):
-            held = lax.dynamic_update_slice(held, sums[i][None, None], (which, (base + step) % SIDE, 0, 0))
-        return held
-
-    held = place(held, core, second_base, (0,), partial_sums(own_half, first))
-    got = to_mate(partial_sums(mate_half, first + middle))
-    held = place(held, core, second_base, (1, 3), partial_sums(own_half, middle))
-    held = place(held, 1 - core, first_base, (0, 1, 3), got)
-    got = to_mate(partial_sums(mate_half, last))
-    held = place(held, core, second_base, (2,), partial_sums(own_half, last))
-    held = place(held, 1 - core, first_base, (2,), got)
-    gate_out = combine(held)
-
-    grads = jnp.zeros((SIDE, 2, share, half), jnp.float32)
-    outer_part = outer_part.reshape(1, 2, share, half)
-    grads = lax.dynamic_update_slice(grads, outer_part, (replica, 0, 0, 0))
-    neighbour = lax.ppermute(outer_part, "replica", [(i, i ^ 1) for i in range(SIDE)])
-    grads = lax.dynamic_update_slice(grads, neighbour, (replica ^ 1, 0, 0, 0))
-    both = jnp.concatenate([outer_part, neighbour])
-    opposite = lax.ppermute(both, "replica", [(i, i ^ 3) for i in range(SIDE)])
-    grads = lax.dynamic_update_slice(grads, opposite[:1], (replica ^ 3, 0, 0, 0))
-    grads = lax.dynamic_update_slice(grads, opposite[1:], (replica ^ 2, 0, 0, 0))
-
-    def rows_of(which):
-        return lax.dynamic_slice(grads, (0, which, 0, 0), (SIDE, 1, share, half)).reshape(rows, half)
-
-    own_grad, mate_grad = rows_of(core), to_mate(rows_of(1 - core))
-    outer_grad = jnp.where(
-        core == 0, jnp.concatenate([own_grad, mate_grad], axis=1), jnp.concatenate([mate_grad, own_grad], axis=1)
-    )
-    new_anchor, new_momentum, merged = update(anchor, momentum, local, outer_grad)
+    sums = [partial_sums(mate_half, first)]
+    own_sums = [partial_sums(own_half, first)]
+    last = []
+    for c, (_, following, before) in enumerate(blocks):
+        low, high = before[:, : part // 2], following[:, part // 2 :]
+        if c == 0:
+            low, high = follow([low, high], own_sums[0], merged)
+        last += [to_ring(low, 1, True), to_ring(high, SIDE - 1, True)]
+    sums.append(partial_sums(mate_half, middle))
+    own_sums.append(partial_sums(own_half, middle))
+    sums = follow(sums, last[2], own_sums[1])
+    got = [to_mate(value) for value in sums]
+    cost = pl.CostEstimate(flops=2 * tokens.shape[1] * 2 * rows * SIDE * half, bytes_accessed=2 * tokens.shape[1] * half, transcendentals=0)
+    got.append(to_mate(partial_sums(mate_half, [last], cost=cost)))
+    own_sums.append(partial_sums(own_half, [last], cost=cost))
+    gate_out = combine(place, *own_sums, *got)
     return (new_anchor, new_momentum, merged[None], gate_out[None])
 
 

time: 108 us -> 100 us (0.926)
  waiting for transfers between devices: 31.7 us -> 23 us
  Pallas kernels: 27.7 us -> 34.5 us
  other arithmetic: 5.03 us -> 0.21 us
  local copies, waits for them, and re-layouts: 3.93 us -> 2.39 us
    ppermute x11, waiting for transfers between devices: 25.6 us -> 7.7 us  [to_ring(): return lax.ppermute(value, ('chip', 'core'), ring_pairs(step, second))]
    pallas_call x5 -> x10, Pallas kernels: 20.3 us -> 26.3 us  [the longest x6 18.5 us: partial_sums(): pl.pallas_call(functools.partial(partial_body, per_block, 0 if filled is...]
    ppermute x1, waiting for transfers between devices: 0.01 us -> 4.75 us  [on_device(): lax.ppermute(outer_part, 'replica', [(i, i ^ 1) for i in range(SIDE)])]
    pallas_call x2 -> x0, other arithmetic: 4.73 us -> none  [partial_sums(): pl.pallas_call(functools.partial(partial_body, per_block), in_specs=[vmem...]
    ppermute x6 -> x7, starting transfers between devices: 10.8 us -> 7.17 us  [to_mate(): return lax.ppermute(value, 'core', [(0, 1), (1, 0)])]
    ppermute x1, waiting for transfers between devices: 0.01 us -> 3.33 us  [on_device(): opposite = lax.ppermute(both, 'replica', [(i, i ^ 3) for i in range(SIDE)])]
    ppermute x6, starting transfers between devices: 8.09 us -> 9.69 us  [to_replica(): lax.ppermute(value, 'replica', [(i, (i + step) % SIDE) for i in range(SID...]
    ppermute x11, starting transfers between devices: 15.8 us -> 17.3 us  [to_ring(): return lax.ppermute(value, ('chip', 'core'), ring_pairs(step, second))]
  transfers between devices with their start and end apart: 25 -> 26, of which waited for: 7 -> 10; matrix products, arithmetic and copies ran while one was open for 7% -> 1% of each run, Pallas kernels for 22% -> 30%
where the time goes in v3:
time: 100 us
  starting transfers between devices  38.7 us (39%)
  Pallas kernels  34.5 us (34%)
  waiting for transfers between devices  23 us (23%)
  local copies, waits for them, and re-layouts  2.39 us (2%)
  between operations  1.31 us (1%)
    pallas_call x6, Pallas kernels, partial_sums(): pl.pallas_call(functools.partial(partial_body, per_block, 0 if filled is...  18.5 us
    ppermute x11, starting transfers between devices, to_ring(): return lax.ppermute(value, ('chip', 'core'), ring_pairs(step, second))  17.3 us
    ppermute x6, starting transfers between devices, to_replica(): lax.ppermute(value, 'replica', [(i, (i + step) % SIDE) for i in range(SID...  9.69 us
    pallas_call x2, Pallas kernels, load_columns(): pl.pallas_call(functools.partial(load_body, entry), in_specs=[pl.BlockSpe...  7.87 us
    ppermute x11, waiting for transfers between devices, to_ring(): return lax.ppermute(value, ('chip', 'core'), ring_pairs(step, second))  7.7 us
    ppermute x7, starting transfers between devices, to_mate(): return lax.ppermute(value, 'core', [(0, 1), (1, 0)])  7.17 us
    ppermute x6, waiting for transfers between devices, to_replica(): lax.ppermute(value, 'replica', [(i, (i + step) % SIDE) for i in range(SID...  6.09 us
    ppermute x1, waiting for transfers between devices, on_device(): lax.ppermute(outer_part, 'replica', [(i, i ^ 1) for i in range(SIDE)])  4.75 us
  transfers between devices with their start and end apart: 26, of which 10 were waited for; matrix products, arithmetic and copies ran while one was open for 1% of the time, Pallas kernels for 30%

profile of v3, /device:TPU:1, one launch (start us, length us, event | category | flops | bytes accessed | tf_op | source)
XLA Modules:
  0.0 100.1 jit_solution(14400506906790143419)
XLA Ops:
  0.7 1.1 %constant_dynamic-slice_fusion.3 = (f32[8,8192]{1,0:T(8,128)S(1)}, f32[8,8192]{1,0:T(8,128)S(1)}) fusion(f32[32,8192]{1,0:T(8,128)} %momentum.1, s32[]{:T(128)S(6)} %select_n.177, f32[32,8192]{1,0:T(8,128)} %anchor.1), kind=kLoop, calls=%fused_computation.40 | loop fusion | bytes 1048580 | tf_op jit(solution)/shard_map/dynamic_slice | solution.py:274
  1.8 1.5 %collective-permute-start = (f32[16,4096]{1,0:T(8,128)S(1)}, f32[16,4096]{1,0:T(8,128)S(1)}, u32[]{:S(2)}, u32[]{:S(2)}) collective-permute-start(f32[16,4096]{1,0:T(8,128)S(1)} %get-tuple-element.37), channel_id=1, source_target_pairs={{0,1},{1,0},{2,3},{3,2},{4,5},{5,4},{6,7},{7,6},{8,9},{9,8},{10,11... | collective-permute-start | bytes 786440 | tf_op jit(solution)/shard_map/ppermute | solution.py:43
  3.8 0.7 collective-permute-done
  4.6 0.4 collective-permute-done.1
  5.1 3.8 %collective-permute-start.4 = (bf16[1,2,8,4096]{3,2,1,0:T(8,128)(2,1)S(1)}, bf16[1,2,8,4096]{3,2,1,0:T(8,128)(2,1)S(1)}, u32[]{:S(2)}, u32[]{:S(2)}) collective-permute-start(bf16[1,2,8,4096]{3,2,1,0:T(8,128)(2,1)S(1)} %get-tuple-element.29), channel_id=1, source_target_pairs={{0,64},{32,96},{64,0},{96,32},{1,65},{33,97},{65,1},{97,33},{2,66}... | collective-permute-start | bytes 393224 | tf_op jit(solution)/shard_map/ppermute | solution.py:51
  8.8 0.4 collective-permute-start.3
  9.3 1.0 %collective-permute-start.2 = (bf16[1,2,8,4096]{3,2,1,0:T(8,128)(2,1)S(1)}, bf16[1,2,8,4096]{3,2,1,0:T(8,128)(2,1)S(1)}, u32[]{:S(2)}, u32[]{:S(2)}) collective-permute-start(bf16[1,2,8,4096]{3,2,1,0:T(8,128)(2,1)S(1)} %get-tuple-element.31), channel_id=1, source_target_pairs={{0,32},{32,64},{64,96},{96,0},{1,33},{33,65},{65,97},{97,1},{2,34}... | collective-permute-start | bytes 393224 | tf_op jit(solution)/shard_map/ppermute | solution.py:51
  10.4 4.3 %collective-permute-done.2.refs_0_ = bf16[1,2,8,4096]{3,2,1,0:T(8,128)(2,1)S(1)} collective-permute-done((bf16[1,2,8,4096]{3,2,1,0:T(8,128)(2,1)S(1)}, bf16[1,2,8,4096]{3,2,1,0:T(8,128)(2,1)S(1)}, u32[]{:S(2)}, u32[]{:S(2)}) %collective-permute-start.2) | collective-permute-done | bytes 131104 | tf_op jit(solution)/shard_map/ppermute | solution.py:51
  14.7 1.1 %collective-permute-done.3 = bf16[1,2,8,4096]{3,2,1,0:T(8,128)(2,1)S(1)} collective-permute-done((bf16[1,2,8,4096]{3,2,1,0:T(8,128)(2,1)S(1)}, bf16[1,2,8,4096]{3,2,1,0:T(8,128)(2,1)S(1)}, u32[]{:S(2)}, u32[]{:S(2)}) %collective-permute-start.3) | collective-permute-done | bytes 131104 | tf_op jit(solution)/shard_map/ppermute | solution.py:51
  15.9 0.9 merge.1
  16.9 0.9 collective-permute-start.8
  17.8 1.3 %collective-permute-start.5 = (f32[8,4096]{1,0:T(8,128)S(1)}, f32[8,4096]{1,0:T(8,128)S(1)}, u32[]{:S(2)}, u32[]{:S(2)}) collective-permute-start(f32[8,4096]{1,0:T(8,128)S(1)} %get-tuple-element.38), channel_id=1, source_target_pairs={{0,1},{1,0},{2,3},{3,2},{4,5},{5,4},{6,7},{7,6},{8,9},{9,8},{10,11... | collective-permute-start | bytes 393224 | tf_op jit(solution)/shard_map/ppermute | solution.py:43
  19.2 2.8 %collective-permute-start.10 = (bf16[1,2,8,4096]{3,2,1,0:T(8,128)(2,1)S(1)}, bf16[1,2,8,4096]{3,2,1,0:T(8,128)(2,1)S(1)}, u32[]{:S(2)}, u32[]{:S(2)}) collective-permute-start(bf16[1,2,8,4096]{3,2,1,0:T(8,128)(2,1)S(1)} %get-tuple-element.26), channel_id=1, source_target_pairs={{0,64},{32,96},{64,0},{96,32},{1,65},{33,97},{65,1},{97,33},{2,66}... | collective-permute-start | bytes 393224 | tf_op jit(solution)/shard_map/ppermute | solution.py:51
  22.0 0.8 collective-permute-start.9
  22.7 3.9 %load_columns.3 = bf16[1024,4096]{1,0:T(8,128)(2,1)S(1)} custom-call(s32[5]{0:T(128)S(1)} %stack.59.place, bf16[1024,8192]{1,0:T(8,128)(2,1)} %bitcast.71, bf16[1,2,8,4096]{3,2,1,0:T(8,128)(2,1)S(1)} %collective-permute-done.2.refs_0_, f32[16,4096]{1,0:T(8,128)S(1)} %get-tuple-element.35.anchor.refs_1_), custom_call_target="tpu_custom_call" | custom-call | flops 1024 | bytes 1024 | tf_op jit(solution)/shard_map/load_columns/pallas_call | solution.py:140
  26.7 0.7 collective-permute-start.22
  27.4 0.7 collective-permute-done.9
  28.1 3.0 %collective-permute-start.13 = (bf16[64,4096]{1,0:T(8,128)(2,1)S(1)}, bf16[64,4096]{1,0:T(8,128)(2,1)S(1)}, u32[]{:S(2)}, u32[]{:S(2)}) collective-permute-start(bf16[64,4096]{1,0:T(8,128)(2,1)S(1)} %bitcast.61), channel_id=1, source_target_pairs={{0,4},{1,17},{2,6},{3,19},{4,0},{5,21},{6,2},{7,23},{8,12},{9,25},... | collective-permute-start | bytes 1572872 | tf_op jit(solution)/shard_map/ppermute | solution.py:47
  31.1 0.8 collective-permute-start.12
  31.9 0.7 collective-permute-start.11
  32.6 3.9 %load_columns.2.tokens = bf16[1024,4096]{1,0:T(8,128)(2,1)S(1)} custom-call(s32[5]{0:T(128)S(1)} %stack.59.place, bf16[1024,8192]{1,0:T(8,128)(2,1)} %bitcast.72, bf16[64,4096]{1,0:T(8,128)(2,1)S(1)} %bitcast.64), custom_call_target="tpu_custom_call" | custom-call | flops 1024 | bytes 1024 | tf_op jit(solution)/shard_map/load_columns/pallas_call | solution.py:140
  36.7 1.8 %collective-permute-start.6 = (f32[8,8192]{1,0:T(8,128)S(1)}, f32[8,8192]{1,0:T(8,128)S(1)}, u32[]{:S(2)}, u32[]{:S(2)}) collective-permute-start(f32[8,8192]{1,0:T(8,128)S(1)} %get-tuple-element.23), channel_id=1, source_target_pairs={{0,32},{32,0},{64,96},{96,64},{1,33},{33,1},{65,97},{97,65},{2,34}... | collective-permute-start | bytes 786440 | tf_op jit(solution)/shard_map/ppermute | solution.py:319
  38.5 0.2 broadcast_in_dim.31
  38.7 4.7 %collective-permute-done.6 = f32[8,8192]{1,0:T(8,128)S(1)} collective-permute-done((f32[8,8192]{1,0:T(8,128)S(1)}, f32[8,8192]{1,0:T(8,128)S(1)}, u32[]{:S(2)}, u32[]{:S(2)}) %collective-permute-start.6) | collective-permute-done | bytes 262176 | tf_op jit(solution)/shard_map/ppermute | solution.py:319
  43.5 2.8 %collective-permute-start.7 = (f32[16,8192]{1,0:T(8,128)S(1)}, f32[16,8192]{1,0:T(8,128)S(1)}, u32[]{:S(2)}, u32[]{:S(2)}) collective-permute-start(f32[16,8192]{1,0:T(8,128)S(1)} %pad_maximum_fusion), channel_id=1, source_target_pairs={{0,96},{32,64},{64,32},{96,0},{1,97},{33,65},{65,33},{97,1},{2,98}... | collective-permute-start | bytes 1572872 | tf_op jit(solution)/shard_map/ppermute | solution.py:322
  46.5 0.1 fusion.4
  46.7 2.3 %collective-permute-start.17 = (bf16[256,2048]{1,0:T(8,128)(2,1)S(1)}, bf16[256,2048]{1,0:T(8,128)(2,1)S(1)}, u32[]{:S(2)}, u32[]{:S(2)}) collective-permute-start(bf16[256,2048]{1,0:T(8,128)(2,1)S(1)} %get-tuple-element.24.refs_1_), channel_id=1, source_target_pairs={{0,8},{1,3},{2,10},{3,5},{4,12},{5,7},{6,14},{7,1},{8,16},{9,11},{... | collective-permute-start | bytes 3145736 | tf_op jit(solution)/shard_map/ppermute | solution.py:47
  49.0 0.8 collective-permute-start.15
  49.8 0.7 collective-permute-start.16
  50.4 2.4 %partial_sums.6.refs_2_.own_first = bf16[1,1024,256]{2,1,0:T(8,128)(2,1)S(1)} custom-call(bf16[1024,4096]{1,0:T(8,128)(2,1)S(1)} %load_columns.2.tokens, bf16[256,2048]{1,0:T(8,128)(2,1)S(1)} %get-tuple-element.25.refs_0_, bf16[256,2048]{1,0:T(8,128)(2,1)S(1)} %get-tuple-element.24.refs_1_), custom_call_target="tpu_custom_call" | custom-call | flops 1024 | bytes 1024 | tf_op jit(solution)/shard_map/partial_sums/pallas_call | solution.py:178
  52.8 3.3 %collective-permute-done.7 = f32[16,8192]{1,0:T(8,128)S(1)} collective-permute-done((f32[16,8192]{1,0:T(8,128)S(1)}, f32[16,8192]{1,0:T(8,128)S(1)}, u32[]{:S(2)}, u32[]{:S(2)}) %collective-permute-start.7) | collective-permute-done | bytes 524320 | tf_op jit(solution)/shard_map/ppermute | solution.py:322
  56.1 3.3 %collective-permute-start.14 = (bf16[256,2048]{1,0:T(8,128)(2,1)S(1)}, bf16[256,2048]{1,0:T(8,128)(2,1)S(1)}, u32[]{:S(2)}, u32[]{:S(2)}) collective-permute-start(bf16[256,2048]{1,0:T(8,128)(2,1)S(1)} %get-tuple-element.25.refs_0_), channel_id=1, source_target_pairs={{0,24},{1,7},{2,26},{3,1},{4,28},{5,3},{6,30},{7,5},{8,0},{9,15},{... | collective-permute-start | bytes 3145736 | tf_op jit(solution)/shard_map/ppermute | solution.py:47
  59.5 2.7 %collective-permute-done.17.refs_3_ = bf16[256,2048]{1,0:T(8,128)(2,1)S(1)} collective-permute-done((bf16[256,2048]{1,0:T(8,128)(2,1)S(1)}, bf16[256,2048]{1,0:T(8,128)(2,1)S(1)}, u32[]{:S(2)}, u32[]{:S(2)}) %collective-permute-start.17) | collective-permute-done | bytes 1048608 | tf_op jit(solution)/shard_map/ppermute | solution.py:47
  62.2 0.8 collective-permute-start.20
  63.1 4.0 %update.1 = (f32[32,8192]{1,0:T(8,128)}, f32[32,8192]{1,0:T(8,128)}, bf16[32,8192]{1,0:T(8,128)(2,1)}) custom-call(f32[32,8192]{1,0:T(8,128)} %anchor.1, f32[32,8192]{1,0:T(8,128)} %momentum.1, bf16[32,8192]{1,0:T(8,128)(2,1)} %bitcast.75, f32[32,8192]{1,0:T(8,128)S(1)} %slice_dynamic-update-slice_fusion.outer_grad), custom_call_target="tpu_custom_call" | custom-call | flops 1024 | bytes 1024 | tf_op jit(solution)/shard_map/update/pallas_call | solution.py:118
  67.1 2.0 %collective-permute-start.21 = (bf16[256,1024]{1,0:T(8,128)(2,1)S(1)}, bf16[256,1024]{1,0:T(8,128)(2,1)S(1)}, u32[]{:S(2)}, u32[]{:S(2)}) collective-permute-start(bf16[256,1024]{1,0:T(8,128)(2,1)S(1)} %slice.41), channel_id=1, source_target_pairs={{0,24},{1,7},{2,26},{3,1},{4,28},{5,3},{6,30},{7,5},{8,0},{9,15},{... | collective-permute-start | bytes 1572872 | tf_op jit(solution)/shard_map/ppermute | solution.py:47
  69.1 4.3 %collective-permute-done.16.refs_2_ = bf16[256,2048]{1,0:T(8,128)(2,1)S(1)} collective-permute-done((bf16[256,2048]{1,0:T(8,128)(2,1)S(1)}, bf16[256,2048]{1,0:T(8,128)(2,1)S(1)}, u32[]{:S(2)}, u32[]{:S(2)}) %collective-permute-start.16) | collective-permute-done | bytes 1048608 | tf_op jit(solution)/shard_map/ppermute | solution.py:47
  73.4 0.7 collective-permute-done.14.refs_0_
  74.2 1.3 %collective-permute-start.18 = (bf16[256,1024]{1,0:T(8,128)(2,1)S(1)}, bf16[256,1024]{1,0:T(8,128)(2,1)S(1)}, u32[]{:S(2)}, u32[]{:S(2)}) collective-permute-start(bf16[256,1024]{1,0:T(8,128)(2,1)S(1)} %get-tuple-element.18), channel_id=1, source_target_pairs={{0,8},{1,3},{2,10},{3,5},{4,12},{5,7},{6,14},{7,1},{8,16},{9,11},{... | collective-permute-start | bytes 1572872 | tf_op jit(solution)/shard_map/ppermute | solution.py:47
  75.6 1.6 %collective-permute-start.19 = (bf16[256,1024]{1,0:T(8,128)(2,1)S(1)}, bf16[256,1024]{1,0:T(8,128)(2,1)S(1)}, u32[]{:S(2)}, u32[]{:S(2)}) collective-permute-start(bf16[256,1024]{1,0:T(8,128)(2,1)S(1)} %get-tuple-element.19), channel_id=1, source_target_pairs={{0,24},{1,7},{2,26},{3,1},{4,28},{5,3},{6,30},{7,5},{8,0},{9,15},{... | collective-permute-start | bytes 1572872 | tf_op jit(solution)/shard_map/ppermute | solution.py:47
  77.1 4.5 %partial_sums.7.refs_3_.own_mid = bf16[2,1024,256]{2,1,0:T(8,128)(2,1)S(1)} custom-call(bf16[1024,4096]{1,0:T(8,128)(2,1)S(1)} %load_columns.2.tokens, bf16[256,2048]{1,0:T(8,128)(2,1)S(1)} %collective-permute-done.14.refs_0_, bf16[256,2048]{1,0:T(8,128)(2,1)S(1)} %collective-permute-done.15.refs_1_, bf16[256,2048]{1,0:T(8,128)(2,1)S(1)} %collective-permute-done.16.refs_2_, ...), custom_call_target="tpu_custom_call" | custom-call | flops 1024 | bytes 1024 | tf_op jit(solution)/shard_map/partial_sums/pallas_call | solution.py:178
  81.7 4.5 %partial_sums.10.refs_1_ = bf16[2,1024,256]{2,1,0:T(8,128)(2,1)S(1)} custom-call(bf16[1024,4096]{1,0:T(8,128)(2,1)S(1)} %collective-permute-done.22.tokens, bf16[256,2048]{1,0:T(8,128)(2,1)S(1)} %collective-permute-done.14.refs_0_, bf16[256,2048]{1,0:T(8,128)(2,1)S(1)} %collective-permute-done.15.refs_1_, ...), custom_call_target="tpu_custom_call" | custom-call | flops 1024 | bytes 1024 | tf_op jit(solution)/shard_map/partial_sums/pallas_call | solution.py:178
  86.2 2.4 %partial_sums.9.refs_0_ = bf16[1,1024,256]{2,1,0:T(8,128)(2,1)S(1)} custom-call(bf16[1024,4096]{1,0:T(8,128)(2,1)S(1)} %collective-permute-done.22.tokens, bf16[256,2048]{1,0:T(8,128)(2,1)S(1)} %get-tuple-element.25.refs_0_, bf16[256,2048]{1,0:T(8,128)(2,1)S(1)} %get-tuple-element.24.refs_1_), custom_call_target="tpu_custom_call" | custom-call | flops 1024 | bytes 1024 | tf_op jit(solution)/shard_map/partial_sums/pallas_call | solution.py:178
  88.6 2.9 %collective-permute-start.24 = (bf16[2,1024,256]{2,1,0:T(8,128)(2,1)S(1)}, bf16[2,1024,256]{2,1,0:T(8,128)(2,1)S(1)}, u32[]{:S(2)}, u32[]{:S(2)}) collective-permute-start(bf16[2,1024,256]{2,1,0:T(8,128)(2,1)S(1)} %get-tuple-element.21), channel_id=1, source_target_pairs={{0,1},{1,0},{2,3},{3,2},{4,5},{5,4},{6,7},{7,6},{8,9},{9,8},{10,11... | collective-permute-start | bytes 3145736 | tf_op jit(solution)/shard_map/ppermute | solution.py:43
  91.6 2.4 %partial_sums.11 = bf16[1,1024,256]{2,1,0:T(8,128)(2,1)S(1)} custom-call(bf16[1024,4096]{1,0:T(8,128)(2,1)S(1)} %collective-permute-done.22.tokens, bf16[256,1024]{1,0:T(8,128)(2,1)S(1)} %collective-permute-done.18.refs_0_, bf16[256,1024]{1,0:T(8,128)(2,1)S(1)} %collective-permute-done.19.refs_1_, bf16[256,1024]{1,0:T(8,128)(2,1)S(1)} %collective-permute-done.20.refs_2_, ...), custom_call_target="tpu_custom_call" | custom-call | flops 2147483648 | bytes 8388608 | tf_op jit(solution)/shard_map/partial_sums/pallas_call | solution.py:178
  94.0 0.5 collective-permute-start.25
  94.5 2.4 %partial_sums.8.own_last = bf16[1,1024,256]{2,1,0:T(8,128)(2,1)S(1)} custom-call(bf16[1024,4096]{1,0:T(8,128)(2,1)S(1)} %load_columns.2.tokens, bf16[256,1024]{1,0:T(8,128)(2,1)S(1)} %collective-permute-done.18.refs_0_, bf16[256,1024]{1,0:T(8,128)(2,1)S(1)} %collective-permute-done.19.refs_1_, bf16[256,1024]{1,0:T(8,128)(2,1)S(1)} %collective-permute-done.20.refs_2_, ...), custom_call_target="tpu_custom_call" | custom-call | flops 2147483648 | bytes 8388608 | tf_op jit(solution)/shard_map/partial_sums/pallas_call | solution.py:178
  96.9 3.2 %combine.1 = bf16[1024,1024]{1,0:T(8,128)(2,1)} custom-call(s32[5]{0:T(128)S(1)} %stack.59.place, bf16[1,1024,256]{2,1,0:T(8,128)(2,1)S(1)} %partial_sums.6.refs_2_.own_first, bf16[2,1024,256]{2,1,0:T(8,128)(2,1)S(1)} %partial_sums.7.refs_3_.own_mid, bf16[1,1024,256]{2,1,0:T(8,128)(2,1)S(1)} %partial_sums.8.own_last, ...), custom_call_target="tpu_custom_call" | custom-call | flops 1024 | bytes 1024 | tf_op jit(solution)/shard_map/combine/pallas_call | solution.py:216
  (57 shorter events, 1.4 us)
Async XLA Ops:
  0.6 2.7 %copy-start.1 = (bf16[1,32,8192]{2,1,0:T(8,128)(2,1)S(1)}, bf16[1,32,8192]{2,1,0:T(8,128)(2,1)}, u32[]{:S(2)}) copy-start(bf16[1,32,8192]{2,1,0:T(8,128)(2,1)} %param.6) | copy-start | bytes 1572868
  1.8 2.7 %collective-permute-start = (f32[16,4096]{1,0:T(8,128)S(1)}, f32[16,4096]{1,0:T(8,128)S(1)}, u32[]{:S(2)}, u32[]{:S(2)}) collective-permute-start(f32[16,4096]{1,0:T(8,128)S(1)} %get-tuple-element.37), channel_id=1, source_target_pairs={{0,1},{1,0},{2,3},{3,2},{4,5},{5,4},{6,7},{7,6},{8,9},{9,8},{10,11... | collective-permute-start | bytes 786440 | tf_op jit(solution)/shard_map/ppermute | solution.py:43
  3.4 1.6 %collective-permute-start.1 = (bf16[32,4096]{1,0:T(8,128)(2,1)S(1)}, bf16[32,4096]{1,0:T(8,128)(2,1)S(1)}, u32[]{:S(2)}, u32[]{:S(2)}) collective-permute-start(bf16[32,4096]{1,0:T(8,128)(2,1)S(1)} %get-tuple-element.33), channel_id=1, source_target_pairs={{0,1},{1,0},{2,3},{3,2},{4,5},{5,4},{6,7},{7,6},{8,9},{9,8},{10,11... | collective-permute-start | bytes 786440 | tf_op jit(solution)/shard_map/ppermute | solution.py:43
  5.1 10.7 %collective-permute-start.4 = (bf16[1,2,8,4096]{3,2,1,0:T(8,128)(2,1)S(1)}, bf16[1,2,8,4096]{3,2,1,0:T(8,128)(2,1)S(1)}, u32[]{:S(2)}, u32[]{:S(2)}) collective-permute-start(bf16[1,2,8,4096]{3,2,1,0:T(8,128)(2,1)S(1)} %get-tuple-element.29), channel_id=1, source_target_pairs={{0,64},{32,96},{64,0},{96,32},{1,65},{33,97},{65,1},{97,33},{2,66}... | collective-permute-start | bytes 393224 | tf_op jit(solution)/shard_map/ppermute | solution.py:51
  8.8 7.0 %collective-permute-start.3 = (bf16[1,2,8,4096]{3,2,1,0:T(8,128)(2,1)S(1)}, bf16[1,2,8,4096]{3,2,1,0:T(8,128)(2,1)S(1)}, u32[]{:S(2)}, u32[]{:S(2)}) collective-permute-start(bf16[1,2,8,4096]{3,2,1,0:T(8,128)(2,1)S(1)} %get-tuple-element.30), channel_id=1, source_target_pairs={{0,96},{32,0},{64,32},{96,64},{1,97},{33,1},{65,33},{97,65},{2,98}... | collective-permute-start | bytes 393224 | tf_op jit(solution)/shard_map/ppermute | solution.py:51
  9.3 5.4 %collective-permute-start.2 = (bf16[1,2,8,4096]{3,2,1,0:T(8,128)(2,1)S(1)}, bf16[1,2,8,4096]{3,2,1,0:T(8,128)(2,1)S(1)}, u32[]{:S(2)}, u32[]{:S(2)}) collective-permute-start(bf16[1,2,8,4096]{3,2,1,0:T(8,128)(2,1)S(1)} %get-tuple-element.31), channel_id=1, source_target_pairs={{0,32},{32,64},{64,96},{96,0},{1,33},{33,65},{65,97},{97,1},{2,34}... | collective-permute-start | bytes 393224 | tf_op jit(solution)/shard_map/ppermute | solution.py:51
  16.9 10.6 %collective-permute-start.8 = (bf16[1,2,8,4096]{3,2,1,0:T(8,128)(2,1)S(1)}, bf16[1,2,8,4096]{3,2,1,0:T(8,128)(2,1)S(1)}, u32[]{:S(2)}, u32[]{:S(2)}) collective-permute-start(bf16[1,2,8,4096]{3,2,1,0:T(8,128)(2,1)S(1)} %get-tuple-element.28), channel_id=1, source_target_pairs={{0,32},{32,64},{64,96},{96,0},{1,33},{33,65},{65,97},{97,1},{2,34}... | collective-permute-start | bytes 393224 | tf_op jit(solution)/shard_map/ppermute | solution.py:51
  17.8 18.7 %collective-permute-start.5 = (f32[8,4096]{1,0:T(8,128)S(1)}, f32[8,4096]{1,0:T(8,128)S(1)}, u32[]{:S(2)}, u32[]{:S(2)}) collective-permute-start(f32[8,4096]{1,0:T(8,128)S(1)} %get-tuple-element.38), channel_id=1, source_target_pairs={{0,1},{1,0},{2,3},{3,2},{4,5},{5,4},{6,7},{7,6},{8,9},{9,8},{10,11... | collective-permute-start | bytes 393224 | tf_op jit(solution)/shard_map/ppermute | solution.py:43
  19.2 9.0 %collective-permute-start.10 = (bf16[1,2,8,4096]{3,2,1,0:T(8,128)(2,1)S(1)}, bf16[1,2,8,4096]{3,2,1,0:T(8,128)(2,1)S(1)}, u32[]{:S(2)}, u32[]{:S(2)}) collective-permute-start(bf16[1,2,8,4096]{3,2,1,0:T(8,128)(2,1)S(1)} %get-tuple-element.26), channel_id=1, source_target_pairs={{0,64},{32,96},{64,0},{96,32},{1,65},{33,97},{65,1},{97,33},{2,66}... | collective-permute-start | bytes 393224 | tf_op jit(solution)/shard_map/ppermute | solution.py:51
  22.0 6.1 %collective-permute-start.9 = (bf16[1,2,8,4096]{3,2,1,0:T(8,128)(2,1)S(1)}, bf16[1,2,8,4096]{3,2,1,0:T(8,128)(2,1)S(1)}, u32[]{:S(2)}, u32[]{:S(2)}) collective-permute-start(bf16[1,2,8,4096]{3,2,1,0:T(8,128)(2,1)S(1)} %get-tuple-element.27), channel_id=1, source_target_pairs={{0,96},{32,0},{64,32},{96,64},{1,97},{33,1},{65,33},{97,65},{2,98}... | collective-permute-start | bytes 393224 | tf_op jit(solution)/shard_map/ppermute | solution.py:51
  26.7 55.0 %collective-permute-start.22 = (bf16[1024,4096]{1,0:T(8,128)(2,1)S(1)}, bf16[1024,4096]{1,0:T(8,128)(2,1)S(1)}, u32[]{:S(2)}, u32[]{:S(2)}) collective-permute-start(bf16[1024,4096]{1,0:T(8,128)(2,1)S(1)} %load_columns.3), channel_id=1, source_target_pairs={{0,1},{1,0},{2,3},{3,2},{4,5},{5,4},{6,7},{7,6},{8,9},{9,8},{10,11... | collective-permute-start | bytes 25165832 | tf_op jit(solution)/shard_map/ppermute | solution.py:43
  28.1 18.3 %collective-permute-start.13 = (bf16[64,4096]{1,0:T(8,128)(2,1)S(1)}, bf16[64,4096]{1,0:T(8,128)(2,1)S(1)}, u32[]{:S(2)}, u32[]{:S(2)}) collective-permute-start(bf16[64,4096]{1,0:T(8,128)(2,1)S(1)} %bitcast.61), channel_id=1, source_target_pairs={{0,4},{1,17},{2,6},{3,19},{4,0},{5,21},{6,2},{7,23},{8,12},{9,25},... | collective-permute-start | bytes 1572872 | tf_op jit(solution)/shard_map/ppermute | solution.py:47
  31.1 15.3 %collective-permute-start.12 = (bf16[64,4096]{1,0:T(8,128)(2,1)S(1)}, bf16[64,4096]{1,0:T(8,128)(2,1)S(1)}, u32[]{:S(2)}, u32[]{:S(2)}) collective-permute-start(bf16[64,4096]{1,0:T(8,128)(2,1)S(1)} %bitcast.62), channel_id=1, source_target_pairs={{0,6},{1,25},{2,0},{3,27},{4,2},{5,29},{6,4},{7,31},{8,14},{9,1},{... | collective-permute-start | bytes 1572872 | tf_op jit(solution)/shard_map/ppermute | solution.py:47
  31.9 14.5 %collective-permute-start.11 = (bf16[64,4096]{1,0:T(8,128)(2,1)S(1)}, bf16[64,4096]{1,0:T(8,128)(2,1)S(1)}, u32[]{:S(2)}, u32[]{:S(2)}) collective-permute-start(bf16[64,4096]{1,0:T(8,128)(2,1)S(1)} %bitcast.63), channel_id=1, source_target_pairs={{0,2},{1,9},{2,4},{3,11},{4,6},{5,13},{6,0},{7,15},{8,10},{9,17},{... | collective-permute-start | bytes 1572872 | tf_op jit(solution)/shard_map/ppermute | solution.py:47
  36.7 6.8 %collective-permute-start.6 = (f32[8,8192]{1,0:T(8,128)S(1)}, f32[8,8192]{1,0:T(8,128)S(1)}, u32[]{:S(2)}, u32[]{:S(2)}) collective-permute-start(f32[8,8192]{1,0:T(8,128)S(1)} %get-tuple-element.23), channel_id=1, source_target_pairs={{0,32},{32,0},{64,96},{96,64},{1,33},{33,1},{65,97},{97,65},{2,34}... | collective-permute-start | bytes 786440 | tf_op jit(solution)/shard_map/ppermute | solution.py:319
  43.5 12.6 %collective-permute-start.7 = (f32[16,8192]{1,0:T(8,128)S(1)}, f32[16,8192]{1,0:T(8,128)S(1)}, u32[]{:S(2)}, u32[]{:S(2)}) collective-permute-start(f32[16,8192]{1,0:T(8,128)S(1)} %pad_maximum_fusion), channel_id=1, source_target_pairs={{0,96},{32,64},{64,32},{96,0},{1,97},{33,65},{65,33},{97,1},{2,98}... | collective-permute-start | bytes 1572872 | tf_op jit(solution)/shard_map/ppermute | solution.py:322
  46.7 15.5 %collective-permute-start.17 = (bf16[256,2048]{1,0:T(8,128)(2,1)S(1)}, bf16[256,2048]{1,0:T(8,128)(2,1)S(1)}, u32[]{:S(2)}, u32[]{:S(2)}) collective-permute-start(bf16[256,2048]{1,0:T(8,128)(2,1)S(1)} %get-tuple-element.24.refs_1_), channel_id=1, source_target_pairs={{0,8},{1,3},{2,10},{3,5},{4,12},{5,7},{6,14},{7,1},{8,16},{9,11},{... | collective-permute-start | bytes 3145736 | tf_op jit(solution)/shard_map/ppermute | solution.py:47
  49.0 18.1 %collective-permute-start.15 = (bf16[256,2048]{1,0:T(8,128)(2,1)S(1)}, bf16[256,2048]{1,0:T(8,128)(2,1)S(1)}, u32[]{:S(2)}, u32[]{:S(2)}) collective-permute-start(bf16[256,2048]{1,0:T(8,128)(2,1)S(1)} %get-tuple-element.24.refs_1_), channel_id=1, source_target_pairs={{0,24},{1,7},{2,26},{3,1},{4,28},{5,3},{6,30},{7,5},{8,0},{9,15},{... | collective-permute-start | bytes 3145736 | tf_op jit(solution)/shard_map/ppermute | solution.py:47
  49.8 23.6 %collective-permute-start.16 = (bf16[256,2048]{1,0:T(8,128)(2,1)S(1)}, bf16[256,2048]{1,0:T(8,128)(2,1)S(1)}, u32[]{:S(2)}, u32[]{:S(2)}) collective-permute-start(bf16[256,2048]{1,0:T(8,128)(2,1)S(1)} %get-tuple-element.25.refs_0_), channel_id=1, source_target_pairs={{0,8},{1,3},{2,10},{3,5},{4,12},{5,7},{6,14},{7,1},{8,16},{9,11},{... | collective-permute-start | bytes 3145736 | tf_op jit(solution)/shard_map/ppermute | solution.py:47
  56.1 18.0 %collective-permute-start.14 = (bf16[256,2048]{1,0:T(8,128)(2,1)S(1)}, bf16[256,2048]{1,0:T(8,128)(2,1)S(1)}, u32[]{:S(2)}, u32[]{:S(2)}) collective-permute-start(bf16[256,2048]{1,0:T(8,128)(2,1)S(1)} %get-tuple-element.25.refs_0_), channel_id=1, source_target_pairs={{0,24},{1,7},{2,26},{3,1},{4,28},{5,3},{6,30},{7,5},{8,0},{9,15},{... | collective-permute-start | bytes 3145736 | tf_op jit(solution)/shard_map/ppermute | solution.py:47
  62.2 26.4 %collective-permute-start.20 = (bf16[256,1024]{1,0:T(8,128)(2,1)S(1)}, bf16[256,1024]{1,0:T(8,128)(2,1)S(1)}, u32[]{:S(2)}, u32[]{:S(2)}) collective-permute-start(bf16[256,1024]{1,0:T(8,128)(2,1)S(1)} %slice.40), channel_id=1, source_target_pairs={{0,8},{1,3},{2,10},{3,5},{4,12},{5,7},{6,14},{7,1},{8,16},{9,11},{... | collective-permute-start | bytes 1572872 | tf_op jit(solution)/shard_map/ppermute | solution.py:47
  67.0 7.2 %copy-start = (bf16[32,8192]{1,0:T(8,128)(2,1)S(1)}, bf16[32,8192]{1,0:T(8,128)(2,1)}, u32[]{:S(2)}) copy-start(bf16[32,8192]{1,0:T(8,128)(2,1)} %get-tuple-element.16.refs_3_) | copy-start | bytes 1572868
  67.1 24.5 %collective-permute-start.21 = (bf16[256,1024]{1,0:T(8,128)(2,1)S(1)}, bf16[256,1024]{1,0:T(8,128)(2,1)S(1)}, u32[]{:S(2)}, u32[]{:S(2)}) collective-permute-start(bf16[256,1024]{1,0:T(8,128)(2,1)S(1)} %slice.41), channel_id=1, source_target_pairs={{0,24},{1,7},{2,26},{3,1},{4,28},{5,3},{6,30},{7,5},{8,0},{9,15},{... | collective-permute-start | bytes 1572872 | tf_op jit(solution)/shard_map/ppermute | solution.py:47
  74.2 17.4 %collective-permute-start.18 = (bf16[256,1024]{1,0:T(8,128)(2,1)S(1)}, bf16[256,1024]{1,0:T(8,128)(2,1)S(1)}, u32[]{:S(2)}, u32[]{:S(2)}) collective-permute-start(bf16[256,1024]{1,0:T(8,128)(2,1)S(1)} %get-tuple-element.18), channel_id=1, source_target_pairs={{0,8},{1,3},{2,10},{3,5},{4,12},{5,7},{6,14},{7,1},{8,16},{9,11},{... | collective-permute-start | bytes 1572872 | tf_op jit(solution)/shard_map/ppermute | solution.py:47
  75.6 16.0 %collective-permute-start.19 = (bf16[256,1024]{1,0:T(8,128)(2,1)S(1)}, bf16[256,1024]{1,0:T(8,128)(2,1)S(1)}, u32[]{:S(2)}, u32[]{:S(2)}) collective-permute-start(bf16[256,1024]{1,0:T(8,128)(2,1)S(1)} %get-tuple-element.19), channel_id=1, source_target_pairs={{0,24},{1,7},{2,26},{3,1},{4,28},{5,3},{6,30},{7,5},{8,0},{9,15},{... | collective-permute-start | bytes 1572872 | tf_op jit(solution)/shard_map/ppermute | solution.py:47
  88.6 8.3 %collective-permute-start.24 = (bf16[2,1024,256]{2,1,0:T(8,128)(2,1)S(1)}, bf16[2,1024,256]{2,1,0:T(8,128)(2,1)S(1)}, u32[]{:S(2)}, u32[]{:S(2)}) collective-permute-start(bf16[2,1024,256]{2,1,0:T(8,128)(2,1)S(1)} %get-tuple-element.21), channel_id=1, source_target_pairs={{0,1},{1,0},{2,3},{3,2},{4,5},{5,4},{6,7},{7,6},{8,9},{9,8},{10,11... | collective-permute-start | bytes 3145736 | tf_op jit(solution)/shard_map/ppermute | solution.py:43
  91.5 5.3 %collective-permute-start.23 = (bf16[1,1024,256]{2,1,0:T(8,128)(2,1)S(1)}, bf16[1,1024,256]{2,1,0:T(8,128)(2,1)S(1)}, u32[]{:S(2)}, u32[]{:S(2)}) collective-permute-start(bf16[1,1024,256]{2,1,0:T(8,128)(2,1)S(1)} %get-tuple-element.20), channel_id=1, source_target_pairs={{0,1},{1,0},{2,3},{3,2},{4,5},{5,4},{6,7},{7,6},{8,9},{9,8},{10,11... | collective-permute-start | bytes 1572872 | tf_op jit(solution)/shard_map/ppermute | solution.py:43
  94.0 2.9 %collective-permute-start.25 = (bf16[1,1024,256]{2,1,0:T(8,128)(2,1)S(1)}, bf16[1,1024,256]{2,1,0:T(8,128)(2,1)S(1)}, u32[]{:S(2)}, u32[]{:S(2)}) collective-permute-start(bf16[1,1024,256]{2,1,0:T(8,128)(2,1)S(1)} %partial_sums.11), channel_id=1, source_target_pairs={{0,1},{1,0},{2,3},{3,2},{4,5},{5,4},{6,7},{7,6},{8,9},{9,8},{10,11... | collective-permute-start | bytes 1572872 | tf_op jit(solution)/shard_map/ppermute | solution.py:43

commit v4 on v3

--- a/solution.py
+++ b/solution.py
@@ -187,7 +187,7 @@
     )(in_vmem(tokens), *[in_vmem(piece) for block in weights for piece in block], *more)
 
 
-COMBINE_ROWS = 256
+COMBINE_ROWS = 128
 
 
 def combine_body(place, own_first, own_mid, own_last, got_first, got_mid, got_last, out, held):

time: 100 us -> 102 us (1.020)
  Pallas kernels: 34.5 us -> 35.7 us
    pallas_call x1, Pallas kernels: 3.2 us -> 4.41 us  [combine(): pl.pallas_call(combine_body, grid=(count // COMBINE_ROWS,), in_specs=[pl....]
where the time goes in v4:
time: 102 us; the launch traced here: 101 us
  starting transfers between devices  38.7 us (38%)
  Pallas kernels  35.7 us (35%)
  waiting for transfers between devices  23 us (23%)
  local copies, waits for them, and re-layouts  2.39 us (2%)
  between operations  1.31 us (1%)
    pallas_call x6, Pallas kernels, partial_sums(): pl.pallas_call(functools.partial(partial_body, per_block, 0 if filled is...  18.5 us
    ppermute x11, starting transfers between devices, to_ring(): return lax.ppermute(value, ('chip', 'core'), ring_pairs(step, second))  17.3 us
    ppermute x6, starting transfers between devices, to_replica(): lax.ppermute(value, 'replica', [(i, (i + step) % SIDE) for i in range(SID...  9.69 us
    pallas_call x2, Pallas kernels, load_columns(): pl.pallas_call(functools.partial(load_body, entry), in_specs=[pl.BlockSpe...  7.87 us
    ppermute x11, waiting for transfers between devices, to_ring(): return lax.ppermute(value, ('chip', 'core'), ring_pairs(step, second))  7.7 us
    ppermute x7, starting transfers between devices, to_mate(): return lax.ppermute(value, 'core', [(0, 1), (1, 0)])  7.17 us
    ppermute x6, waiting for transfers between devices, to_replica(): lax.ppermute(value, 'replica', [(i, (i + step) % SIDE) for i in range(SID...  6.09 us
    ppermute x1, waiting for transfers between devices, on_device(): lax.ppermute(outer_part, 'replica', [(i, i ^ 1) for i in range(SIDE)])  4.75 us
  transfers between devices with their start and end apart: 26, of which 10 were waited for; matrix products, arithmetic and copies ran while one was open for 1% of the time, Pallas kernels for 30%

profile of v4, /device:TPU:1, one launch (start us, length us, event | category | flops | bytes accessed | tf_op | source)
XLA Modules:
  0.0 101.3 jit_solution(15104062622345464436)
XLA Ops:
  0.7 1.1 %constant_dynamic-slice_fusion.3 = (f32[8,8192]{1,0:T(8,128)S(1)}, f32[8,8192]{1,0:T(8,128)S(1)}) fusion(f32[32,8192]{1,0:T(8,128)} %momentum.1, s32[]{:T(128)S(6)} %select_n.177, f32[32,8192]{1,0:T(8,128)} %anchor.1), kind=kLoop, calls=%fused_computation.40 | loop fusion | bytes 1048580 | tf_op jit(solution)/shard_map/dynamic_slice | solution.py:274
  1.8 1.5 %collective-permute-start = (f32[16,4096]{1,0:T(8,128)S(1)}, f32[16,4096]{1,0:T(8,128)S(1)}, u32[]{:S(2)}, u32[]{:S(2)}) collective-permute-start(f32[16,4096]{1,0:T(8,128)S(1)} %get-tuple-element.37), channel_id=1, source_target_pairs={{0,1},{1,0},{2,3},{3,2},{4,5},{5,4},{6,7},{7,6},{8,9},{9,8},{10,11... | collective-permute-start | bytes 786440 | tf_op jit(solution)/shard_map/ppermute | solution.py:43
  3.8 0.7 collective-permute-done
  4.6 0.4 collective-permute-done.1
  5.1 3.8 %collective-permute-start.4 = (bf16[1,2,8,4096]{3,2,1,0:T(8,128)(2,1)S(1)}, bf16[1,2,8,4096]{3,2,1,0:T(8,128)(2,1)S(1)}, u32[]{:S(2)}, u32[]{:S(2)}) collective-permute-start(bf16[1,2,8,4096]{3,2,1,0:T(8,128)(2,1)S(1)} %get-tuple-element.29), channel_id=1, source_target_pairs={{0,64},{32,96},{64,0},{96,32},{1,65},{33,97},{65,1},{97,33},{2,66}... | collective-permute-start | bytes 393224 | tf_op jit(solution)/shard_map/ppermute | solution.py:51
  8.8 0.4 collective-permute-start.3
  9.3 1.0 %collective-permute-start.2 = (bf16[1,2,8,4096]{3,2,1,0:T(8,128)(2,1)S(1)}, bf16[1,2,8,4096]{3,2,1,0:T(8,128)(2,1)S(1)}, u32[]{:S(2)}, u32[]{:S(2)}) collective-permute-start(bf16[1,2,8,4096]{3,2,1,0:T(8,128)(2,1)S(1)} %get-tuple-element.31), channel_id=1, source_target_pairs={{0,32},{32,64},{64,96},{96,0},{1,33},{33,65},{65,97},{97,1},{2,34}... | collective-permute-start | bytes 393224 | tf_op jit(solution)/shard_map/ppermute | solution.py:51
  10.4 4.3 %collective-permute-done.2.refs_0_ = bf16[1,2,8,4096]{3,2,1,0:T(8,128)(2,1)S(1)} collective-permute-done((bf16[1,2,8,4096]{3,2,1,0:T(8,128)(2,1)S(1)}, bf16[1,2,8,4096]{3,2,1,0:T(8,128)(2,1)S(1)}, u32[]{:S(2)}, u32[]{:S(2)}) %collective-permute-start.2) | collective-permute-done | bytes 131104 | tf_op jit(solution)/shard_map/ppermute | solution.py:51
  14.7 1.1 %collective-permute-done.3 = bf16[1,2,8,4096]{3,2,1,0:T(8,128)(2,1)S(1)} collective-permute-done((bf16[1,2,8,4096]{3,2,1,0:T(8,128)(2,1)S(1)}, bf16[1,2,8,4096]{3,2,1,0:T(8,128)(2,1)S(1)}, u32[]{:S(2)}, u32[]{:S(2)}) %collective-permute-start.3) | collective-permute-done | bytes 131104 | tf_op jit(solution)/shard_map/ppermute | solution.py:51
  15.9 0.9 merge.1
  16.9 0.9 collective-permute-start.8
  17.8 1.3 %collective-permute-start.5 = (f32[8,4096]{1,0:T(8,128)S(1)}, f32[8,4096]{1,0:T(8,128)S(1)}, u32[]{:S(2)}, u32[]{:S(2)}) collective-permute-start(f32[8,4096]{1,0:T(8,128)S(1)} %get-tuple-element.38), channel_id=1, source_target_pairs={{0,1},{1,0},{2,3},{3,2},{4,5},{5,4},{6,7},{7,6},{8,9},{9,8},{10,11... | collective-permute-start | bytes 393224 | tf_op jit(solution)/shard_map/ppermute | solution.py:43
  19.2 2.8 %collective-permute-start.10 = (bf16[1,2,8,4096]{3,2,1,0:T(8,128)(2,1)S(1)}, bf16[1,2,8,4096]{3,2,1,0:T(8,128)(2,1)S(1)}, u32[]{:S(2)}, u32[]{:S(2)}) collective-permute-start(bf16[1,2,8,4096]{3,2,1,0:T(8,128)(2,1)S(1)} %get-tuple-element.26), channel_id=1, source_target_pairs={{0,64},{32,96},{64,0},{96,32},{1,65},{33,97},{65,1},{97,33},{2,66}... | collective-permute-start | bytes 393224 | tf_op jit(solution)/shard_map/ppermute | solution.py:51
  22.0 0.8 collective-permute-start.9
  22.7 3.9 %load_columns.3 = bf16[1024,4096]{1,0:T(8,128)(2,1)S(1)} custom-call(s32[5]{0:T(128)S(1)} %stack.59.place, bf16[1024,8192]{1,0:T(8,128)(2,1)} %bitcast.71, bf16[1,2,8,4096]{3,2,1,0:T(8,128)(2,1)S(1)} %collective-permute-done.2.refs_0_, f32[16,4096]{1,0:T(8,128)S(1)} %get-tuple-element.35.anchor.refs_1_), custom_call_target="tpu_custom_call" | custom-call | flops 1024 | bytes 1024 | tf_op jit(solution)/shard_map/load_columns/pallas_call | solution.py:140
  26.7 0.7 collective-permute-start.22
  27.4 0.7 collective-permute-done.9
  28.1 3.0 %collective-permute-start.13 = (bf16[64,4096]{1,0:T(8,128)(2,1)S(1)}, bf16[64,4096]{1,0:T(8,128)(2,1)S(1)}, u32[]{:S(2)}, u32[]{:S(2)}) collective-permute-start(bf16[64,4096]{1,0:T(8,128)(2,1)S(1)} %bitcast.61), channel_id=1, source_target_pairs={{0,4},{1,17},{2,6},{3,19},{4,0},{5,21},{6,2},{7,23},{8,12},{9,25},... | collective-permute-start | bytes 1572872 | tf_op jit(solution)/shard_map/ppermute | solution.py:47
  31.1 0.8 collective-permute-start.12
  31.9 0.7 collective-permute-start.11
  32.6 3.9 %load_columns.2.tokens = bf16[1024,4096]{1,0:T(8,128)(2,1)S(1)} custom-call(s32[5]{0:T(128)S(1)} %stack.59.place, bf16[1024,8192]{1,0:T(8,128)(2,1)} %bitcast.72, bf16[64,4096]{1,0:T(8,128)(2,1)S(1)} %bitcast.64), custom_call_target="tpu_custom_call" | custom-call | flops 1024 | bytes 1024 | tf_op jit(solution)/shard_map/load_columns/pallas_call | solution.py:140
  36.7 1.8 %collective-permute-start.6 = (f32[8,8192]{1,0:T(8,128)S(1)}, f32[8,8192]{1,0:T(8,128)S(1)}, u32[]{:S(2)}, u32[]{:S(2)}) collective-permute-start(f32[8,8192]{1,0:T(8,128)S(1)} %get-tuple-element.23), channel_id=1, source_target_pairs={{0,32},{32,0},{64,96},{96,64},{1,33},{33,1},{65,97},{97,65},{2,34}... | collective-permute-start | bytes 786440 | tf_op jit(solution)/shard_map/ppermute | solution.py:319
  38.5 0.2 broadcast_in_dim.31
  38.7 4.7 %collective-permute-done.6 = f32[8,8192]{1,0:T(8,128)S(1)} collective-permute-done((f32[8,8192]{1,0:T(8,128)S(1)}, f32[8,8192]{1,0:T(8,128)S(1)}, u32[]{:S(2)}, u32[]{:S(2)}) %collective-permute-start.6) | collective-permute-done | bytes 262176 | tf_op jit(solution)/shard_map/ppermute | solution.py:319
  43.5 2.8 %collective-permute-start.7 = (f32[16,8192]{1,0:T(8,128)S(1)}, f32[16,8192]{1,0:T(8,128)S(1)}, u32[]{:S(2)}, u32[]{:S(2)}) collective-permute-start(f32[16,8192]{1,0:T(8,128)S(1)} %pad_maximum_fusion), channel_id=1, source_target_pairs={{0,96},{32,64},{64,32},{96,0},{1,97},{33,65},{65,33},{97,1},{2,98}... | collective-permute-start | bytes 1572872 | tf_op jit(solution)/shard_map/ppermute | solution.py:322
  46.5 0.1 fusion.4
  46.7 2.3 %collective-permute-start.17 = (bf16[256,2048]{1,0:T(8,128)(2,1)S(1)}, bf16[256,2048]{1,0:T(8,128)(2,1)S(1)}, u32[]{:S(2)}, u32[]{:S(2)}) collective-permute-start(bf16[256,2048]{1,0:T(8,128)(2,1)S(1)} %get-tuple-element.24.refs_1_), channel_id=1, source_target_pairs={{0,8},{1,3},{2,10},{3,5},{4,12},{5,7},{6,14},{7,1},{8,16},{9,11},{... | collective-permute-start | bytes 3145736 | tf_op jit(solution)/shard_map/ppermute | solution.py:47
  49.0 0.8 collective-permute-start.15
  49.8 0.7 collective-permute-start.16
  50.4 2.4 %partial_sums.6.refs_2_.own_first = bf16[1,1024,256]{2,1,0:T(8,128)(2,1)S(1)} custom-call(bf16[1024,4096]{1,0:T(8,128)(2,1)S(1)} %load_columns.2.tokens, bf16[256,2048]{1,0:T(8,128)(2,1)S(1)} %get-tuple-element.25.refs_0_, bf16[256,2048]{1,0:T(8,128)(2,1)S(1)} %get-tuple-element.24.refs_1_), custom_call_target="tpu_custom_call" | custom-call | flops 1024 | bytes 1024 | tf_op jit(solution)/shard_map/partial_sums/pallas_call | solution.py:178
  52.8 3.3 %collective-permute-done.7 = f32[16,8192]{1,0:T(8,128)S(1)} collective-permute-done((f32[16,8192]{1,0:T(8,128)S(1)}, f32[16,8192]{1,0:T(8,128)S(1)}, u32[]{:S(2)}, u32[]{:S(2)}) %collective-permute-start.7) | collective-permute-done | bytes 524320 | tf_op jit(solution)/shard_map/ppermute | solution.py:322
  56.1 3.3 %collective-permute-start.14 = (bf16[256,2048]{1,0:T(8,128)(2,1)S(1)}, bf16[256,2048]{1,0:T(8,128)(2,1)S(1)}, u32[]{:S(2)}, u32[]{:S(2)}) collective-permute-start(bf16[256,2048]{1,0:T(8,128)(2,1)S(1)} %get-tuple-element.25.refs_0_), channel_id=1, source_target_pairs={{0,24},{1,7},{2,26},{3,1},{4,28},{5,3},{6,30},{7,5},{8,0},{9,15},{... | collective-permute-start | bytes 3145736 | tf_op jit(solution)/shard_map/ppermute | solution.py:47
  59.5 2.7 %collective-permute-done.17.refs_3_ = bf16[256,2048]{1,0:T(8,128)(2,1)S(1)} collective-permute-done((bf16[256,2048]{1,0:T(8,128)(2,1)S(1)}, bf16[256,2048]{1,0:T(8,128)(2,1)S(1)}, u32[]{:S(2)}, u32[]{:S(2)}) %collective-permute-start.17) | collective-permute-done | bytes 1048608 | tf_op jit(solution)/shard_map/ppermute | solution.py:47
  62.2 0.8 collective-permute-start.20
  63.1 4.0 %update.1 = (f32[32,8192]{1,0:T(8,128)}, f32[32,8192]{1,0:T(8,128)}, bf16[32,8192]{1,0:T(8,128)(2,1)}) custom-call(f32[32,8192]{1,0:T(8,128)} %anchor.1, f32[32,8192]{1,0:T(8,128)} %momentum.1, bf16[32,8192]{1,0:T(8,128)(2,1)} %bitcast.75, f32[32,8192]{1,0:T(8,128)S(1)} %slice_dynamic-update-slice_fusion.outer_grad), custom_call_target="tpu_custom_call" | custom-call | flops 1024 | bytes 1024 | tf_op jit(solution)/shard_map/update/pallas_call | solution.py:118
  67.1 2.0 %collective-permute-start.21 = (bf16[256,1024]{1,0:T(8,128)(2,1)S(1)}, bf16[256,1024]{1,0:T(8,128)(2,1)S(1)}, u32[]{:S(2)}, u32[]{:S(2)}) collective-permute-start(bf16[256,1024]{1,0:T(8,128)(2,1)S(1)} %slice.41), channel_id=1, source_target_pairs={{0,24},{1,7},{2,26},{3,1},{4,28},{5,3},{6,30},{7,5},{8,0},{9,15},{... | collective-permute-start | bytes 1572872 | tf_op jit(solution)/shard_map/ppermute | solution.py:47
  69.1 4.3 %collective-permute-done.16.refs_2_ = bf16[256,2048]{1,0:T(8,128)(2,1)S(1)} collective-permute-done((bf16[256,2048]{1,0:T(8,128)(2,1)S(1)}, bf16[256,2048]{1,0:T(8,128)(2,1)S(1)}, u32[]{:S(2)}, u32[]{:S(2)}) %collective-permute-start.16) | collective-permute-done | bytes 1048608 | tf_op jit(solution)/shard_map/ppermute | solution.py:47
  73.4 0.7 collective-permute-done.14.refs_0_
  74.2 1.3 %collective-permute-start.18 = (bf16[256,1024]{1,0:T(8,128)(2,1)S(1)}, bf16[256,1024]{1,0:T(8,128)(2,1)S(1)}, u32[]{:S(2)}, u32[]{:S(2)}) collective-permute-start(bf16[256,1024]{1,0:T(8,128)(2,1)S(1)} %get-tuple-element.18), channel_id=1, source_target_pairs={{0,8},{1,3},{2,10},{3,5},{4,12},{5,7},{6,14},{7,1},{8,16},{9,11},{... | collective-permute-start | bytes 1572872 | tf_op jit(solution)/shard_map/ppermute | solution.py:47
  75.6 1.6 %collective-permute-start.19 = (bf16[256,1024]{1,0:T(8,128)(2,1)S(1)}, bf16[256,1024]{1,0:T(8,128)(2,1)S(1)}, u32[]{:S(2)}, u32[]{:S(2)}) collective-permute-start(bf16[256,1024]{1,0:T(8,128)(2,1)S(1)} %get-tuple-element.19), channel_id=1, source_target_pairs={{0,24},{1,7},{2,26},{3,1},{4,28},{5,3},{6,30},{7,5},{8,0},{9,15},{... | collective-permute-start | bytes 1572872 | tf_op jit(solution)/shard_map/ppermute | solution.py:47
  77.1 4.5 %partial_sums.7.refs_3_.own_mid = bf16[2,1024,256]{2,1,0:T(8,128)(2,1)S(1)} custom-call(bf16[1024,4096]{1,0:T(8,128)(2,1)S(1)} %load_columns.2.tokens, bf16[256,2048]{1,0:T(8,128)(2,1)S(1)} %collective-permute-done.14.refs_0_, bf16[256,2048]{1,0:T(8,128)(2,1)S(1)} %collective-permute-done.15.refs_1_, bf16[256,2048]{1,0:T(8,128)(2,1)S(1)} %collective-permute-done.16.refs_2_, ...), custom_call_target="tpu_custom_call" | custom-call | flops 1024 | bytes 1024 | tf_op jit(solution)/shard_map/partial_sums/pallas_call | solution.py:178
  81.7 4.5 %partial_sums.10.refs_1_ = bf16[2,1024,256]{2,1,0:T(8,128)(2,1)S(1)} custom-call(bf16[1024,4096]{1,0:T(8,128)(2,1)S(1)} %collective-permute-done.22.tokens, bf16[256,2048]{1,0:T(8,128)(2,1)S(1)} %collective-permute-done.14.refs_0_, bf16[256,2048]{1,0:T(8,128)(2,1)S(1)} %collective-permute-done.15.refs_1_, ...), custom_call_target="tpu_custom_call" | custom-call | flops 1024 | bytes 1024 | tf_op jit(solution)/shard_map/partial_sums/pallas_call | solution.py:178
  86.2 2.4 %partial_sums.9.refs_0_ = bf16[1,1024,256]{2,1,0:T(8,128)(2,1)S(1)} custom-call(bf16[1024,4096]{1,0:T(8,128)(2,1)S(1)} %collective-permute-done.22.tokens, bf16[256,2048]{1,0:T(8,128)(2,1)S(1)} %get-tuple-element.25.refs_0_, bf16[256,2048]{1,0:T(8,128)(2,1)S(1)} %get-tuple-element.24.refs_1_), custom_call_target="tpu_custom_call" | custom-call | flops 1024 | bytes 1024 | tf_op jit(solution)/shard_map/partial_sums/pallas_call | solution.py:178
  88.6 2.9 %collective-permute-start.24 = (bf16[2,1024,256]{2,1,0:T(8,128)(2,1)S(1)}, bf16[2,1024,256]{2,1,0:T(8,128)(2,1)S(1)}, u32[]{:S(2)}, u32[]{:S(2)}) collective-permute-start(bf16[2,1024,256]{2,1,0:T(8,128)(2,1)S(1)} %get-tuple-element.21), channel_id=1, source_target_pairs={{0,1},{1,0},{2,3},{3,2},{4,5},{5,4},{6,7},{7,6},{8,9},{9,8},{10,11... | collective-permute-start | bytes 3145736 | tf_op jit(solution)/shard_map/ppermute | solution.py:43
  91.6 2.4 %partial_sums.11 = bf16[1,1024,256]{2,1,0:T(8,128)(2,1)S(1)} custom-call(bf16[1024,4096]{1,0:T(8,128)(2,1)S(1)} %collective-permute-done.22.tokens, bf16[256,1024]{1,0:T(8,128)(2,1)S(1)} %collective-permute-done.18.refs_0_, bf16[256,1024]{1,0:T(8,128)(2,1)S(1)} %collective-permute-done.19.refs_1_, bf16[256,1024]{1,0:T(8,128)(2,1)S(1)} %collective-permute-done.20.refs_2_, ...), custom_call_target="tpu_custom_call" | custom-call | flops 2147483648 | bytes 8388608 | tf_op jit(solution)/shard_map/partial_sums/pallas_call | solution.py:178
  94.0 0.5 collective-permute-start.25
  94.5 2.4 %partial_sums.8.own_last = bf16[1,1024,256]{2,1,0:T(8,128)(2,1)S(1)} custom-call(bf16[1024,4096]{1,0:T(8,128)(2,1)S(1)} %load_columns.2.tokens, bf16[256,1024]{1,0:T(8,128)(2,1)S(1)} %collective-permute-done.18.refs_0_, bf16[256,1024]{1,0:T(8,128)(2,1)S(1)} %collective-permute-done.19.refs_1_, bf16[256,1024]{1,0:T(8,128)(2,1)S(1)} %collective-permute-done.20.refs_2_, ...), custom_call_target="tpu_custom_call" | custom-call | flops 2147483648 | bytes 8388608 | tf_op jit(solution)/shard_map/partial_sums/pallas_call | solution.py:178
  96.9 4.4 %combine.1 = bf16[1024,1024]{1,0:T(8,128)(2,1)} custom-call(s32[5]{0:T(128)S(1)} %stack.59.place, bf16[1,1024,256]{2,1,0:T(8,128)(2,1)S(1)} %partial_sums.6.refs_2_.own_first, bf16[2,1024,256]{2,1,0:T(8,128)(2,1)S(1)} %partial_sums.7.refs_3_.own_mid, bf16[1,1024,256]{2,1,0:T(8,128)(2,1)S(1)} %partial_sums.8.own_last, ...), custom_call_target="tpu_custom_call" | custom-call | flops 1024 | bytes 1024 | tf_op jit(solution)/shard_map/combine/pallas_call | solution.py:216
  (57 shorter events, 1.4 us)
Async XLA Ops:
  0.6 2.7 %copy-start.1 = (bf16[1,32,8192]{2,1,0:T(8,128)(2,1)S(1)}, bf16[1,32,8192]{2,1,0:T(8,128)(2,1)}, u32[]{:S(2)}) copy-start(bf16[1,32,8192]{2,1,0:T(8,128)(2,1)} %param.6) | copy-start | bytes 1572868
  1.8 2.7 %collective-permute-start = (f32[16,4096]{1,0:T(8,128)S(1)}, f32[16,4096]{1,0:T(8,128)S(1)}, u32[]{:S(2)}, u32[]{:S(2)}) collective-permute-start(f32[16,4096]{1,0:T(8,128)S(1)} %get-tuple-element.37), channel_id=1, source_target_pairs={{0,1},{1,0},{2,3},{3,2},{4,5},{5,4},{6,7},{7,6},{8,9},{9,8},{10,11... | collective-permute-start | bytes 786440 | tf_op jit(solution)/shard_map/ppermute | solution.py:43
  3.4 1.6 %collective-permute-start.1 = (bf16[32,4096]{1,0:T(8,128)(2,1)S(1)}, bf16[32,4096]{1,0:T(8,128)(2,1)S(1)}, u32[]{:S(2)}, u32[]{:S(2)}) collective-permute-start(bf16[32,4096]{1,0:T(8,128)(2,1)S(1)} %get-tuple-element.33), channel_id=1, source_target_pairs={{0,1},{1,0},{2,3},{3,2},{4,5},{5,4},{6,7},{7,6},{8,9},{9,8},{10,11... | collective-permute-start | bytes 786440 | tf_op jit(solution)/shard_map/ppermute | solution.py:43
  5.1 10.7 %collective-permute-start.4 = (bf16[1,2,8,4096]{3,2,1,0:T(8,128)(2,1)S(1)}, bf16[1,2,8,4096]{3,2,1,0:T(8,128)(2,1)S(1)}, u32[]{:S(2)}, u32[]{:S(2)}) collective-permute-start(bf16[1,2,8,4096]{3,2,1,0:T(8,128)(2,1)S(1)} %get-tuple-element.29), channel_id=1, source_target_pairs={{0,64},{32,96},{64,0},{96,32},{1,65},{33,97},{65,1},{97,33},{2,66}... | collective-permute-start | bytes 393224 | tf_op jit(solution)/shard_map/ppermute | solution.py:51
  8.8 7.0 %collective-permute-start.3 = (bf16[1,2,8,4096]{3,2,1,0:T(8,128)(2,1)S(1)}, bf16[1,2,8,4096]{3,2,1,0:T(8,128)(2,1)S(1)}, u32[]{:S(2)}, u32[]{:S(2)}) collective-permute-start(bf16[1,2,8,4096]{3,2,1,0:T(8,128)(2,1)S(1)} %get-tuple-element.30), channel_id=1, source_target_pairs={{0,96},{32,0},{64,32},{96,64},{1,97},{33,1},{65,33},{97,65},{2,98}... | collective-permute-start | bytes 393224 | tf_op jit(solution)/shard_map/ppermute | solution.py:51
  9.3 5.4 %collective-permute-start.2 = (bf16[1,2,8,4096]{3,2,1,0:T(8,128)(2,1)S(1)}, bf16[1,2,8,4096]{3,2,1,0:T(8,128)(2,1)S(1)}, u32[]{:S(2)}, u32[]{:S(2)}) collective-permute-start(bf16[1,2,8,4096]{3,2,1,0:T(8,128)(2,1)S(1)} %get-tuple-element.31), channel_id=1, source_target_pairs={{0,32},{32,64},{64,96},{96,0},{1,33},{33,65},{65,97},{97,1},{2,34}... | collective-permute-start | bytes 393224 | tf_op jit(solution)/shard_map/ppermute | solution.py:51
  16.9 10.6 %collective-permute-start.8 = (bf16[1,2,8,4096]{3,2,1,0:T(8,128)(2,1)S(1)}, bf16[1,2,8,4096]{3,2,1,0:T(8,128)(2,1)S(1)}, u32[]{:S(2)}, u32[]{:S(2)}) collective-permute-start(bf16[1,2,8,4096]{3,2,1,0:T(8,128)(2,1)S(1)} %get-tuple-element.28), channel_id=1, source_target_pairs={{0,32},{32,64},{64,96},{96,0},{1,33},{33,65},{65,97},{97,1},{2,34}... | collective-permute-start | bytes 393224 | tf_op jit(solution)/shard_map/ppermute | solution.py:51
  17.8 18.7 %collective-permute-start.5 = (f32[8,4096]{1,0:T(8,128)S(1)}, f32[8,4096]{1,0:T(8,128)S(1)}, u32[]{:S(2)}, u32[]{:S(2)}) collective-permute-start(f32[8,4096]{1,0:T(8,128)S(1)} %get-tuple-element.38), channel_id=1, source_target_pairs={{0,1},{1,0},{2,3},{3,2},{4,5},{5,4},{6,7},{7,6},{8,9},{9,8},{10,11... | collective-permute-start | bytes 393224 | tf_op jit(solution)/shard_map/ppermute | solution.py:43
  19.2 9.0 %collective-permute-start.10 = (bf16[1,2,8,4096]{3,2,1,0:T(8,128)(2,1)S(1)}, bf16[1,2,8,4096]{3,2,1,0:T(8,128)(2,1)S(1)}, u32[]{:S(2)}, u32[]{:S(2)}) collective-permute-start(bf16[1,2,8,4096]{3,2,1,0:T(8,128)(2,1)S(1)} %get-tuple-element.26), channel_id=1, source_target_pairs={{0,64},{32,96},{64,0},{96,32},{1,65},{33,97},{65,1},{97,33},{2,66}... | collective-permute-start | bytes 393224 | tf_op jit(solution)/shard_map/ppermute | solution.py:51
  22.0 6.1 %collective-permute-start.9 = (bf16[1,2,8,4096]{3,2,1,0:T(8,128)(2,1)S(1)}, bf16[1,2,8,4096]{3,2,1,0:T(8,128)(2,1)S(1)}, u32[]{:S(2)}, u32[]{:S(2)}) collective-permute-start(bf16[1,2,8,4096]{3,2,1,0:T(8,128)(2,1)S(1)} %get-tuple-element.27), channel_id=1, source_target_pairs={{0,96},{32,0},{64,32},{96,64},{1,97},{33,1},{65,33},{97,65},{2,98}... | collective-permute-start | bytes 393224 | tf_op jit(solution)/shard_map/ppermute | solution.py:51
  26.7 55.0 %collective-permute-start.22 = (bf16[1024,4096]{1,0:T(8,128)(2,1)S(1)}, bf16[1024,4096]{1,0:T(8,128)(2,1)S(1)}, u32[]{:S(2)}, u32[]{:S(2)}) collective-permute-start(bf16[1024,4096]{1,0:T(8,128)(2,1)S(1)} %load_columns.3), channel_id=1, source_target_pairs={{0,1},{1,0},{2,3},{3,2},{4,5},{5,4},{6,7},{7,6},{8,9},{9,8},{10,11... | collective-permute-start | bytes 25165832 | tf_op jit(solution)/shard_map/ppermute | solution.py:43
  28.1 18.3 %collective-permute-start.13 = (bf16[64,4096]{1,0:T(8,128)(2,1)S(1)}, bf16[64,4096]{1,0:T(8,128)(2,1)S(1)}, u32[]{:S(2)}, u32[]{:S(2)}) collective-permute-start(bf16[64,4096]{1,0:T(8,128)(2,1)S(1)} %bitcast.61), channel_id=1, source_target_pairs={{0,4},{1,17},{2,6},{3,19},{4,0},{5,21},{6,2},{7,23},{8,12},{9,25},... | collective-permute-start | bytes 1572872 | tf_op jit(solution)/shard_map/ppermute | solution.py:47
  31.1 15.3 %collective-permute-start.12 = (bf16[64,4096]{1,0:T(8,128)(2,1)S(1)}, bf16[64,4096]{1,0:T(8,128)(2,1)S(1)}, u32[]{:S(2)}, u32[]{:S(2)}) collective-permute-start(bf16[64,4096]{1,0:T(8,128)(2,1)S(1)} %bitcast.62), channel_id=1, source_target_pairs={{0,6},{1,25},{2,0},{3,27},{4,2},{5,29},{6,4},{7,31},{8,14},{9,1},{... | collective-permute-start | bytes 1572872 | tf_op jit(solution)/shard_map/ppermute | solution.py:47
  31.9 14.5 %collective-permute-start.11 = (bf16[64,4096]{1,0:T(8,128)(2,1)S(1)}, bf16[64,4096]{1,0:T(8,128)(2,1)S(1)}, u32[]{:S(2)}, u32[]{:S(2)}) collective-permute-start(bf16[64,4096]{1,0:T(8,128)(2,1)S(1)} %bitcast.63), channel_id=1, source_target_pairs={{0,2},{1,9},{2,4},{3,11},{4,6},{5,13},{6,0},{7,15},{8,10},{9,17},{... | collective-permute-start | bytes 1572872 | tf_op jit(solution)/shard_map/ppermute | solution.py:47
  36.7 6.8 %collective-permute-start.6 = (f32[8,8192]{1,0:T(8,128)S(1)}, f32[8,8192]{1,0:T(8,128)S(1)}, u32[]{:S(2)}, u32[]{:S(2)}) collective-permute-start(f32[8,8192]{1,0:T(8,128)S(1)} %get-tuple-element.23), channel_id=1, source_target_pairs={{0,32},{32,0},{64,96},{96,64},{1,33},{33,1},{65,97},{97,65},{2,34}... | collective-permute-start | bytes 786440 | tf_op jit(solution)/shard_map/ppermute | solution.py:319
  43.5 12.6 %collective-permute-start.7 = (f32[16,8192]{1,0:T(8,128)S(1)}, f32[16,8192]{1,0:T(8,128)S(1)}, u32[]{:S(2)}, u32[]{:S(2)}) collective-permute-start(f32[16,8192]{1,0:T(8,128)S(1)} %pad_maximum_fusion), channel_id=1, source_target_pairs={{0,96},{32,64},{64,32},{96,0},{1,97},{33,65},{65,33},{97,1},{2,98}... | collective-permute-start | bytes 1572872 | tf_op jit(solution)/shard_map/ppermute | solution.py:322
  46.7 15.5 %collective-permute-start.17 = (bf16[256,2048]{1,0:T(8,128)(2,1)S(1)}, bf16[256,2048]{1,0:T(8,128)(2,1)S(1)}, u32[]{:S(2)}, u32[]{:S(2)}) collective-permute-start(bf16[256,2048]{1,0:T(8,128)(2,1)S(1)} %get-tuple-element.24.refs_1_), channel_id=1, source_target_pairs={{0,8},{1,3},{2,10},{3,5},{4,12},{5,7},{6,14},{7,1},{8,16},{9,11},{... | collective-permute-start | bytes 3145736 | tf_op jit(solution)/shard_map/ppermute | solution.py:47
  49.0 18.1 %collective-permute-start.15 = (bf16[256,2048]{1,0:T(8,128)(2,1)S(1)}, bf16[256,2048]{1,0:T(8,128)(2,1)S(1)}, u32[]{:S(2)}, u32[]{:S(2)}) collective-permute-start(bf16[256,2048]{1,0:T(8,128)(2,1)S(1)} %get-tuple-element.24.refs_1_), channel_id=1, source_target_pairs={{0,24},{1,7},{2,26},{3,1},{4,28},{5,3},{6,30},{7,5},{8,0},{9,15},{... | collective-permute-start | bytes 3145736 | tf_op jit(solution)/shard_map/ppermute | solution.py:47
  49.8 23.6 %collective-permute-start.16 = (bf16[256,2048]{1,0:T(8,128)(2,1)S(1)}, bf16[256,2048]{1,0:T(8,128)(2,1)S(1)}, u32[]{:S(2)}, u32[]{:S(2)}) collective-permute-start(bf16[256,2048]{1,0:T(8,128)(2,1)S(1)} %get-tuple-element.25.refs_0_), channel_id=1, source_target_pairs={{0,8},{1,3},{2,10},{3,5},{4,12},{5,7},{6,14},{7,1},{8,16},{9,11},{... | collective-permute-start | bytes 3145736 | tf_op jit(solution)/shard_map/ppermute | solution.py:47
  56.1 18.0 %collective-permute-start.14 = (bf16[256,2048]{1,0:T(8,128)(2,1)S(1)}, bf16[256,2048]{1,0:T(8,128)(2,1)S(1)}, u32[]{:S(2)}, u32[]{:S(2)}) collective-permute-start(bf16[256,2048]{1,0:T(8,128)(2,1)S(1)} %get-tuple-element.25.refs_0_), channel_id=1, source_target_pairs={{0,24},{1,7},{2,26},{3,1},{4,28},{5,3},{6,30},{7,5},{8,0},{9,15},{... | collective-permute-start | bytes 3145736 | tf_op jit(solution)/shard_map/ppermute | solution.py:47
  62.2 26.4 %collective-permute-start.20 = (bf16[256,1024]{1,0:T(8,128)(2,1)S(1)}, bf16[256,1024]{1,0:T(8,128)(2,1)S(1)}, u32[]{:S(2)}, u32[]{:S(2)}) collective-permute-start(bf16[256,1024]{1,0:T(8,128)(2,1)S(1)} %slice.40), channel_id=1, source_target_pairs={{0,8},{1,3},{2,10},{3,5},{4,12},{5,7},{6,14},{7,1},{8,16},{9,11},{... | collective-permute-start | bytes 1572872 | tf_op jit(solution)/shard_map/ppermute | solution.py:47
  67.0 7.2 %copy-start = (bf16[32,8192]{1,0:T(8,128)(2,1)S(1)}, bf16[32,8192]{1,0:T(8,128)(2,1)}, u32[]{:S(2)}) copy-start(bf16[32,8192]{1,0:T(8,128)(2,1)} %get-tuple-element.16.refs_3_) | copy-start | bytes 1572868
  67.1 24.5 %collective-permute-start.21 = (bf16[256,1024]{1,0:T(8,128)(2,1)S(1)}, bf16[256,1024]{1,0:T(8,128)(2,1)S(1)}, u32[]{:S(2)}, u32[]{:S(2)}) collective-permute-start(bf16[256,1024]{1,0:T(8,128)(2,1)S(1)} %slice.41), channel_id=1, source_target_pairs={{0,24},{1,7},{2,26},{3,1},{4,28},{5,3},{6,30},{7,5},{8,0},{9,15},{... | collective-permute-start | bytes 1572872 | tf_op jit(solution)/shard_map/ppermute | solution.py:47
  74.2 17.4 %collective-permute-start.18 = (bf16[256,1024]{1,0:T(8,128)(2,1)S(1)}, bf16[256,1024]{1,0:T(8,128)(2,1)S(1)}, u32[]{:S(2)}, u32[]{:S(2)}) collective-permute-start(bf16[256,1024]{1,0:T(8,128)(2,1)S(1)} %get-tuple-element.18), channel_id=1, source_target_pairs={{0,8},{1,3},{2,10},{3,5},{4,12},{5,7},{6,14},{7,1},{8,16},{9,11},{... | collective-permute-start | bytes 1572872 | tf_op jit(solution)/shard_map/ppermute | solution.py:47
  75.6 16.0 %collective-permute-start.19 = (bf16[256,1024]{1,0:T(8,128)(2,1)S(1)}, bf16[256,1024]{1,0:T(8,128)(2,1)S(1)}, u32[]{:S(2)}, u32[]{:S(2)}) collective-permute-start(bf16[256,1024]{1,0:T(8,128)(2,1)S(1)} %get-tuple-element.19), channel_id=1, source_target_pairs={{0,24},{1,7},{2,26},{3,1},{4,28},{5,3},{6,30},{7,5},{8,0},{9,15},{... | collective-permute-start | bytes 1572872 | tf_op jit(solution)/shard_map/ppermute | solution.py:47
  88.6 8.3 %collective-permute-start.24 = (bf16[2,1024,256]{2,1,0:T(8,128)(2,1)S(1)}, bf16[2,1024,256]{2,1,0:T(8,128)(2,1)S(1)}, u32[]{:S(2)}, u32[]{:S(2)}) collective-permute-start(bf16[2,1024,256]{2,1,0:T(8,128)(2,1)S(1)} %get-tuple-element.21), channel_id=1, source_target_pairs={{0,1},{1,0},{2,3},{3,2},{4,5},{5,4},{6,7},{7,6},{8,9},{9,8},{10,11... | collective-permute-start | bytes 3145736 | tf_op jit(solution)/shard_map/ppermute | solution.py:43
  91.5 5.3 %collective-permute-start.23 = (bf16[1,1024,256]{2,1,0:T(8,128)(2,1)S(1)}, bf16[1,1024,256]{2,1,0:T(8,128)(2,1)S(1)}, u32[]{:S(2)}, u32[]{:S(2)}) collective-permute-start(bf16[1,1024,256]{2,1,0:T(8,128)(2,1)S(1)} %get-tuple-element.20), channel_id=1, source_target_pairs={{0,1},{1,0},{2,3},{3,2},{4,5},{5,4},{6,7},{7,6},{8,9},{9,8},{10,11... | collective-permute-start | bytes 1572872 | tf_op jit(solution)/shard_map/ppermute | solution.py:43
  94.0 2.9 %collective-permute-start.25 = (bf16[1,1024,256]{2,1,0:T(8,128)(2,1)S(1)}, bf16[1,1024,256]{2,1,0:T(8,128)(2,1)S(1)}, u32[]{:S(2)}, u32[]{:S(2)}) collective-permute-start(bf16[1,1024,256]{2,1,0:T(8,128)(2,1)S(1)} %partial_sums.11), channel_id=1, source_target_pairs={{0,1},{1,0},{2,3},{3,2},{4,5},{5,4},{6,7},{7,6},{8,9},{9,8},{10,11... | collective-permute-start | bytes 1572872 | tf_op jit(solution)/shard_map/ppermute | solution.py:43
